TPU v7x, 32 devices: a whole 2x2x4 slice. The times are simulated.
32 devices in a mesh: section: 2 (over x), rep: 4 (over y, core), shard: 4 (over z).
Axes of the slice: x: 2, y: 2, z: 4, core: 2. Of those that a mesh axis runs over, the one named last changes fastest.
Arguments:
- tokens: bfloat16 [8, 1024, 2048], P('rep', 'shard'), may hold values from -6 to 6
- cotangent: bfloat16 [8, 1024, 2048], P('rep', 'shard'), may hold values from -6 to 6
- live_counts: int32 [4], P('rep'), may hold values from 1 to 2, as said below
- w_query: bfloat16 [2, 2048, 2048], P('section', 'shard'), may hold values from -0.125 to 0.125
- w_key: bfloat16 [2, 2048, 256], P('section', 'shard'), may hold values from -0.125 to 0.125
- w_value: bfloat16 [2, 2048, 256], P('section', 'shard'), may hold values from -0.125 to 0.125
- w_out: bfloat16 [2, 2048, 2048], P('section', 'shard'), may hold values from -1.5 to 1.5
- w_gate: bfloat16 [2, 2048, 5632], P('section', 'shard'), may hold values from -0.125 to 0.125
- w_up: bfloat16 [2, 2048, 5632], P('section', 'shard'), may hold values from -0.125 to 0.125
- w_down: bfloat16 [2, 5632, 2048], P('section', 'shard'), may hold values from -0.078125 to 0.078125
- norm_gains: bfloat16 [2, 2, 2048], P('section', None, 'shard'), may hold values from 0.5 to 1.5
Outputs:
- acts: bfloat16 [2, 8, 1024, 2048], P('section', 'rep', 'shard')
- grad_in: float32 [2, 8, 1024, 2048], P('section', 'rep', 'shard')
- grad_query: float32 [2, 2048, 2048], P('section', 'shard')
- grad_key: float32 [2, 2048, 256], P('section', 'shard')
- grad_value: float32 [2, 2048, 256], P('section', 'shard')
- grad_w_out: float32 [2, 2048, 2048], P('section', 'shard')
- grad_gate: float32 [2, 2048, 5632], P('section', 'shard')
- grad_up: float32 [2, 2048, 5632], P('section', 'shard')
- grad_down: float32 [2, 5632, 2048], P('section', 'shard')
- grad_gains: float32 [2, 2, 2048], P('section', None, 'shard')
Inputs may be any that keep to these rules, and one draw needn't show every extreme that they name: `live_counts`: each replica group's live sequences fill its first slots; some group holds 2 live sequences and some other group only 1.
All inputs are finite; a program needn't handle non-finite values.
Results may differ from a plain program's by a relative error of at most 0.025.
Values may be sent and summed in bfloat16 or wider, within the bound.
A program may use at most 512 MiB of HBM per device.

v0:
```python
import jax
import jax.numpy as jnp
from jax import lax
from jax.sharding import PartitionSpec as P

HEADS = 32
KV_HEADS = 4
HEAD = 64


EPSILON = 1e-05
ROPE_BASE = 10000.0
NEG_FILL = -1e30


def passed_along(shard, axis, by):
    length = lax.axis_size(axis)
    pairs = [(i, i + by) for i in range(length) if 0 <= i + by < length]
    return lax.ppermute(shard, axis, pairs)


def angles_for(positions):
    half_dim = HEAD // 2
    inverse = ROPE_BASE ** (-(jnp.arange(half_dim, dtype=jnp.float32) * 2.0 / HEAD))
    angle_grid = positions.astype(jnp.float32)[:, None] * inverse[None, :]
    return (jnp.cos(angle_grid), jnp.sin(angle_grid))


def rotate(matrix, cos_table, sin_table):
    row_count = matrix.shape[0]
    half_dim = HEAD // 2
    pieces = matrix.reshape(row_count, -1, 2, half_dim)
    first_half = pieces[:, :, 0, :]
    second_half = pieces[:, :, 1, :]
    cos_wide = cos_table[:, None, :]
    sin_wide = sin_table[:, None, :]
    rotated = jnp.stack(
        [
            first_half * cos_wide - second_half * sin_wide,
            second_half * cos_wide + first_half * sin_wide,
        ],
        axis=2,
    )
    return rotated.reshape(row_count, -1)


def times_t(left_rows, right_rows):
    return lax.dot_general(
        left_rows, right_rows, (((1,), (1,)), ((), ())), preferred_element_type=jnp.float32
    )


def inner_rows(left_rows, right_rows):
    return lax.dot_general(
        left_rows, right_rows, (((0,), (0,)), ((), ())), preferred_element_type=jnp.float32
    )


def norm_back(grad_normed, stream, inv_root, gain_row):
    scaled = grad_normed * gain_row
    cubed = inv_root * inv_root * inv_root
    return inv_root * scaled - stream * cubed * jnp.mean(scaled * stream, axis=-1, keepdims=True)


def score_block(queries, key_all, query_pos, key_pos):
    row_count = queries.shape[0]
    group_size = HEADS // KV_HEADS
    query4 = queries.reshape(row_count, KV_HEADS, group_size, HEAD)
    key_heads = key_all.reshape(-1, KV_HEADS, HEAD)
    scores = jnp.einsum(
        "qhgd,khd->hgqk", query4, key_heads, preferred_element_type=jnp.float32
    ) * HEAD ** (-0.5)
    causal = key_pos[None, :] <= query_pos[:, None]
    return (jnp.where(causal, scores, NEG_FILL), query4, key_heads)


def flatten(matrix):
    return matrix.reshape(-1, matrix.shape[-1])


def body(
    tokens, cotangent, live_counts, w_query, w_key, w_value, w_out, w_gate, w_up, w_down, norm_gains
):
    section_idx = lax.axis_index("section")
    shard_pos = lax.axis_index("shard")
    slot_count, span_len, model_width = tokens.shape
    seq_len = span_len * lax.axis_size("shard")
    group_size = HEADS // KV_HEADS
    query_pos = shard_pos * span_len + jnp.arange(span_len, dtype=jnp.int32)
    key_pos = jnp.arange(seq_len, dtype=jnp.int32)
    cos_table, sin_table = angles_for(query_pos)
    live_mask = (jnp.arange(slot_count) < live_counts[0]).astype(jnp.float32)
    full_fwd = (
        lax.all_gather(w_query[0], "shard", axis=0, tiled=True),
        lax.all_gather(w_key[0], "shard", axis=0, tiled=True),
        lax.all_gather(w_value[0], "shard", axis=0, tiled=True),
        lax.all_gather(w_out[0], "shard", axis=0, tiled=True),
        lax.all_gather(w_gate[0], "shard", axis=0, tiled=True),
        lax.all_gather(w_up[0], "shard", axis=0, tiled=True),
        lax.all_gather(w_down[0], "shard", axis=0, tiled=True),
        lax.all_gather(norm_gains[0], "shard", axis=1, tiled=True),
    )

    def layer_forward(stream_in, full_set):
        w_q, w_k, w_v, w_o, w_g, w_u, w_d, gain_vals = full_set
        gains_wide = gain_vals.astype(jnp.float32)
        stream = stream_in.astype(jnp.float32)
        inv_one = lax.rsqrt(jnp.mean(stream * stream, axis=-1, keepdims=True) + EPSILON)
        normed = (stream * inv_one * gains_wide[0]).astype(jnp.bfloat16)
        queries = rotate(
            jnp.dot(normed, w_q, preferred_element_type=jnp.float32), cos_table, sin_table
        ).astype(jnp.bfloat16)
        key_rows = rotate(
            jnp.dot(normed, w_k, preferred_element_type=jnp.float32), cos_table, sin_table
        ).astype(jnp.bfloat16)
        values = jnp.dot(normed, w_v, preferred_element_type=jnp.float32).astype(jnp.bfloat16)
        key_all, value_all = (
            lax.all_gather(key_rows, "shard", axis=0, tiled=True),
            lax.all_gather(values, "shard", axis=0, tiled=True),
        )
        scores, query4, key_heads = score_block(queries, key_all, query_pos, key_pos)
        row_max = jnp.max(scores, axis=-1, keepdims=True)
        log_total = row_max + jnp.log(jnp.sum(jnp.exp(scores - row_max), axis=-1, keepdims=True))
        prob_vals = jnp.exp(scores - log_total).astype(jnp.bfloat16)
        value3 = value_all.reshape(-1, KV_HEADS, HEAD)
        attended = jnp.einsum(
            "hgqk,khd->qhgd", prob_vals, value3, preferred_element_type=jnp.float32
        )
        attended = attended.reshape(span_len, model_width).astype(jnp.bfloat16)
        middle = stream + jnp.dot(attended, w_o, preferred_element_type=jnp.float32)
        inv_two = lax.rsqrt(jnp.mean(middle * middle, axis=-1, keepdims=True) + EPSILON)
        normed_two = (middle * inv_two * gains_wide[1]).astype(jnp.bfloat16)
        gate_proj = jnp.dot(normed_two, w_g, preferred_element_type=jnp.float32)
        upward = jnp.dot(normed_two, w_u, preferred_element_type=jnp.float32)
        hidden = (jax.nn.silu(gate_proj) * upward).astype(jnp.bfloat16)
        result = middle + jnp.dot(hidden, w_d, preferred_element_type=jnp.float32)
        kept_vals = (
            stream,
            inv_one,
            normed,
            queries,
            key_all,
            value_all,
            log_total,
            attended,
            middle,
            inv_two,
            normed_two,
            gate_proj,
            upward,
            hidden,
        )
        return (result.astype(jnp.bfloat16), kept_vals)

    def layer_backward(grad_out, kept_vals, full_set):
        w_q, w_k, w_v, w_o, w_g, w_u, w_d, gain_vals = full_set
        gains_wide = gain_vals.astype(jnp.float32)
        (
            stream,
            inv_one,
            normed,
            queries,
            key_all,
            value_all,
            log_total,
            attended,
            middle,
            inv_two,
            normed_two,
            gate_proj,
            upward,
            hidden,
        ) = kept_vals
        grad_down = grad_out.astype(jnp.bfloat16)
        grad_hidden = times_t(grad_down, w_d)
        sigmoid_gate = jax.nn.sigmoid(gate_proj)
        grad_gate = (
            grad_hidden * upward * sigmoid_gate * (1.0 + gate_proj * (1.0 - sigmoid_gate))
        ).astype(jnp.bfloat16)
        grad_up = (grad_hidden * gate_proj * sigmoid_gate).astype(jnp.bfloat16)
        grad_normed_two = times_t(grad_gate, w_g) + times_t(grad_up, w_u)
        grad_middle = grad_out + norm_back(grad_normed_two, middle, inv_two, gains_wide[1])
        gain_two = jnp.sum(grad_normed_two * middle * inv_two, axis=0)
        grad_branch = grad_middle.astype(jnp.bfloat16)
        grad_attended = times_t(grad_branch, w_o).astype(jnp.bfloat16)
        scores, query4, key_heads = score_block(queries, key_all, query_pos, key_pos)
        prob_vals = jnp.exp(scores - log_total)
        value3 = value_all.reshape(-1, KV_HEADS, HEAD)
        grad_heads = grad_attended.reshape(span_len, KV_HEADS, group_size, HEAD)
        grad_probs = jnp.einsum(
            "qhgd,khd->hgqk", grad_heads, value3, preferred_element_type=jnp.float32
        )
        grad_scores = prob_vals * (
            grad_probs - jnp.sum(prob_vals * grad_probs, axis=-1, keepdims=True)
        )
        grad_scores = grad_scores.astype(jnp.bfloat16)
        scale_factor = HEAD ** (-0.5)
        grad_q_rot = jnp.einsum(
            "hgqk,khd->qhgd", grad_scores, key_heads, preferred_element_type=jnp.float32
        )
        grad_q_rot = grad_q_rot.reshape(span_len, model_width) * scale_factor
        grad_k_part = jnp.einsum(
            "hgqk,qhgd->khd", grad_scores, query4, preferred_element_type=jnp.float32
        )
        grad_k_part = grad_k_part.reshape(seq_len, -1) * scale_factor
        grad_v_part = jnp.einsum(
            "hgqk,qhgd->khd",
            prob_vals.astype(jnp.bfloat16),
            grad_heads,
            preferred_element_type=jnp.float32,
        ).reshape(seq_len, -1)
        grad_k_rot, grad_v_sum = (
            lax.psum_scatter(
                grad_k_part.astype(jnp.bfloat16), "shard", scatter_dimension=0, tiled=True
            ).astype(jnp.float32),
            lax.psum_scatter(
                grad_v_part.astype(jnp.bfloat16), "shard", scatter_dimension=0, tiled=True
            ).astype(jnp.float32),
        )
        grad_query = rotate(grad_q_rot, cos_table, -sin_table).astype(jnp.bfloat16)
        grad_key = rotate(grad_k_rot, cos_table, -sin_table).astype(jnp.bfloat16)
        grad_value = grad_v_sum.astype(jnp.bfloat16)
        grad_normed = times_t(grad_query, w_q) + times_t(grad_key, w_k) + times_t(grad_value, w_v)
        grad_stream = grad_middle + norm_back(grad_normed, stream, inv_one, gains_wide[0])
        gain_one = jnp.sum(grad_normed * stream * inv_one, axis=0)
        grad_list = (grad_query, grad_key, grad_value, grad_branch, grad_gate, grad_up, grad_down)
        return (grad_stream, grad_list, jnp.stack([gain_one, gain_two]))

    zero_slot = jnp.zeros((1, span_len, model_width), jnp.bfloat16)
    masked_in = (tokens.astype(jnp.float32) * live_mask[:, None, None]).astype(jnp.bfloat16)
    padded_in = jnp.concatenate([masked_in, zero_slot], axis=0)

    def forward_tick(received, slot_in):
        own_in = jnp.where(section_idx == 0, slot_in, received)
        result, kept_vals = layer_forward(own_in, full_fwd)
        passed = passed_along(result, "section", 1)
        return (passed, (result, kept_vals))

    _, (results, kept_all) = lax.scan(forward_tick, zero_slot[0], padded_in)
    acts = lax.dynamic_slice_in_dim(results, section_idx, slot_count, 0)

    def by_slot(matrix):
        return lax.dynamic_slice_in_dim(matrix, section_idx, slot_count, 0)

    kept_slots = jax.tree.map(by_slot, kept_all)
    full_bwd = (
        lax.all_gather(w_query[0], "shard", axis=0, tiled=True),
        lax.all_gather(w_key[0], "shard", axis=0, tiled=True),
        lax.all_gather(w_value[0], "shard", axis=0, tiled=True),
        lax.all_gather(w_out[0], "shard", axis=0, tiled=True),
        lax.all_gather(w_gate[0], "shard", axis=0, tiled=True),
        lax.all_gather(w_up[0], "shard", axis=0, tiled=True),
        lax.all_gather(w_down[0], "shard", axis=0, tiled=True),
        lax.all_gather(norm_gains[0], "shard", axis=1, tiled=True),
    )
    masked_cot = (cotangent.astype(jnp.float32) * live_mask[:, None, None]).astype(jnp.bfloat16)
    padded_cot = jnp.concatenate([jnp.flip(masked_cot, 0), zero_slot], axis=0)
    tick_list = jnp.arange(slot_count + 1, dtype=jnp.int32)

    def backward_tick(carry_vals, tick_item):
        received, gain_total = carry_vals
        tick_idx, slot_cot = tick_item
        which_slot = jnp.clip(slot_count - 1 - tick_idx + (1 - section_idx), 0, slot_count - 1)

        def pick(matrix):
            return lax.dynamic_index_in_dim(matrix, which_slot, 0, keepdims=False)

        kept_vals = jax.tree.map(pick, kept_slots)
        grad_out = jnp.where(section_idx == 1, slot_cot, received).astype(jnp.float32)
        grad_stream, grad_list, gain_grad = layer_backward(grad_out, kept_vals, full_bwd)
        passed = passed_along(grad_stream.astype(jnp.bfloat16), "section", -1)
        return ((passed, gain_total + gain_grad), (grad_stream, grad_list))

    start_carry = (zero_slot[0], jnp.zeros((2, model_width), jnp.float32))
    (_, gain_total), (grad_streams, grad_lists) = lax.scan(
        backward_tick, start_carry, (tick_list, padded_cot)
    )

    def to_slots(matrix):
        return jnp.flip(lax.dynamic_slice_in_dim(matrix, 1 - section_idx, slot_count, 0), 0)

    grad_in = to_slots(grad_streams)
    grad_q_rows, grad_k_rows, grad_v_rows, grad_b_rows, grad_g_rows, grad_u_rows, grad_d_rows = (
        flatten(to_slots(matrix)) for matrix in grad_lists
    )
    normed_rows = flatten(kept_slots[2])
    attended_rows = flatten(kept_slots[7])
    normed_two_rows = flatten(kept_slots[10])
    hidden_rows = flatten(kept_slots[13])
    kv_width = w_key.shape[2]
    ff_width = w_gate.shape[2]
    attn_sum = lax.psum_scatter(
        jnp.concatenate(
            [
                inner_rows(normed_rows, grad_q_rows),
                inner_rows(normed_rows, grad_k_rows),
                inner_rows(normed_rows, grad_v_rows),
                inner_rows(attended_rows, grad_b_rows),
            ],
            axis=1,
        ).astype(jnp.bfloat16),
        "shard",
        scatter_dimension=0,
        tiled=True,
    ).astype(jnp.float32)
    ff_sum = lax.psum_scatter(
        jnp.concatenate(
            [inner_rows(normed_two_rows, grad_g_rows), inner_rows(normed_two_rows, grad_u_rows)],
            axis=1,
        ).astype(jnp.bfloat16),
        "shard",
        scatter_dimension=0,
        tiled=True,
    ).astype(jnp.float32)
    edge_two = model_width + kv_width
    edge_three = edge_two + kv_width
    query_part = attn_sum[:, :model_width]
    key_part = attn_sum[:, model_width:edge_two]
    value_part = attn_sum[:, edge_two:edge_three]
    out_part = attn_sum[:, edge_three:]
    gate_part = ff_sum[:, :ff_width]
    up_part = ff_sum[:, ff_width:]
    down_term = inner_rows(hidden_rows, grad_d_rows)
    down_part, gain_part = (
        lax.psum_scatter(
            down_term.astype(jnp.bfloat16), "shard", scatter_dimension=0, tiled=True
        ).astype(jnp.float32),
        lax.psum_scatter(
            gain_total.astype(jnp.bfloat16), "shard", scatter_dimension=1, tiled=True
        ).astype(jnp.float32),
    )
    totals = (
        lax.psum(query_part.astype(jnp.bfloat16), "rep").astype(jnp.float32),
        lax.psum(key_part.astype(jnp.bfloat16), "rep").astype(jnp.float32),
        lax.psum(value_part.astype(jnp.bfloat16), "rep").astype(jnp.float32),
        lax.psum(out_part.astype(jnp.bfloat16), "rep").astype(jnp.float32),
        lax.psum(gate_part.astype(jnp.bfloat16), "rep").astype(jnp.float32),
        lax.psum(up_part.astype(jnp.bfloat16), "rep").astype(jnp.float32),
        lax.psum(down_part.astype(jnp.bfloat16), "rep").astype(jnp.float32),
        lax.psum(gain_part.astype(jnp.bfloat16), "rep").astype(jnp.float32),
    )
    return (
        acts[None],
        grad_in[None],
        totals[0][None],
        totals[1][None],
        totals[2][None],
        totals[3][None],
        totals[4][None],
        totals[5][None],
        totals[6][None],
        totals[7][None],
    )


def solution(mesh):
    return jax.shard_map(
        body,
        mesh=mesh,
        in_specs=(
            P("rep", "shard", None),
            P("rep", "shard", None),
            P("rep"),
            P("section", "shard", None),
            P("section", "shard", None),
            P("section", "shard", None),
            P("section", "shard", None),
            P("section", "shard", None),
            P("section", "shard", None),
            P("section", "shard", None),
            P("section", None, "shard"),
        ),
        out_specs=(
            P("section", "rep", "shard", None),
            P("section", "rep", "shard", None),
            P("section", "shard", None),
            P("section", "shard", None),
            P("section", "shard", None),
            P("section", "shard", None),
            P("section", "shard", None),
            P("section", "shard", None),
            P("section", "shard", None),
            P("section", None, "shard"),
        ),
        check_vma=False,
    )
```

profile of v0, /device:TPU:0, one launch (start us, length us, event | category | flops | bytes accessed | tf_op | source)
XLA Modules:
  0.0 4757.4 jit_solution(10635017079440590155)
XLA Ops:
  40.6 28.8 all-gather.18.cloned.1.call-done
  69.4 150.7 %all-gather.20.cloned.1.call-done = bf16[1,2048,2048]{2,1,0:T(8,128)(2,1)} async-done(((bf16[1,512,2048]{2,1,0:T(8,128)(2,1)}), bf16[1,2048,2048]{2,1,0:T(8,128)(2,1)}) %all-gather.20.cloned.1.call-update) | async-done | bytes 8388624 | tf_op jit(solution)/shard_map/all_gather | solution.py:94
  220.1 149.3 %all-gather.22.cloned.1.call-done = bf16[1,2048,2048]{2,1,0:T(8,128)(2,1)} async-done(((bf16[1,512,2048]{2,1,0:T(8,128)(2,1)}), bf16[1,2048,2048]{2,1,0:T(8,128)(2,1)}) %all-gather.22.cloned.1.call-update) | async-done | bytes 8388624 | tf_op jit(solution)/shard_map/all_gather | solution.py:97
  369.5 390.8 %all-gather.24.cloned.1.call-done = bf16[1,2048,5632]{2,1,0:T(8,128)(2,1)} async-done(((bf16[1,512,5632]{2,1,0:T(8,128)(2,1)}), bf16[1,2048,5632]{2,1,0:T(8,128)(2,1)}) %all-gather.24.cloned.1.call-update) | async-done | bytes 23068688 | tf_op jit(solution)/shard_map/all_gather | solution.py:98
  760.2 390.9 %all-gather.26.cloned.1.call-done = bf16[1,2048,5632]{2,1,0:T(8,128)(2,1)} async-done(((bf16[1,512,5632]{2,1,0:T(8,128)(2,1)}), bf16[1,2048,5632]{2,1,0:T(8,128)(2,1)}) %all-gather.26.cloned.1.call-update) | async-done | bytes 23068688 | tf_op jit(solution)/shard_map/all_gather | solution.py:99
  1151.1 391.0 %all-gather.28.cloned.1.call-done = bf16[1,5632,2048]{2,1,0:T(8,128)(2,1)} async-done(((bf16[1,1408,2048]{2,1,0:T(8,128)(2,1)}), bf16[1,5632,2048]{2,1,0:T(8,128)(2,1)}) %all-gather.28.cloned.1.call-update) | async-done | bytes 23068688 | tf_op jit(solution)/shard_map/all_gather | solution.py:100
  1560.0 519.6 %while.77 = (s32[]{:T(128)}, bf16[256,2048]{1,0:T(8,128)(2,1)}, bf16[3,256,2048]{2,1,0:T(8,128)(2,1)}, f32[3,256,2048]{2,1,0:T(8,128)}, f32[3,256,1]{1,2,0:T(1,1...) while((s32[]{:T(128)}, bf16[256,2048]{1,0:T(8,128)(2,1)}, ...), condition=%wide.region_5.6_spmd.clone.clone, body=%wide.region_0.5_spmd.clone.clone.sunk | while | flops 24819662848 | bytes 342144192 | solution.py:239
  1847.5 18.0 multiply_convert_fusion.7
  2019.1 18.0 multiply_convert_fusion.7
  2116.8 681.3 %while.78 = (s32[]{:T(128)}, bf16[256,2048]{1,0:T(8,128)(2,1)}, f32[2,2048]{1,0:T(2,128)}, f32[3,256,2048]{2,1,0:T(8,128)}, bf16[3,256,2048]{1,2,0:T(8,128)(2,1)...) while((s32[]{:T(128)}, bf16[256,2048]{1,0:T(8,128)(2,1)}, ...), condition=%wide.region_14.15_spmd.clone.clone.clone, body=%wide.region_6.14_spmd.clone.clone.clone.sunk | while | flops 28083773440 | bytes 481046336 | solution.py:275
  2122.6 25.9 bitcast_dynamic-update-slice_fusion.33
  2203.9 23.3 fusion.254
  2227.3 28.0 fusion.255
  2320.5 21.4 collective-permute-done.1
  2347.5 26.0 bitcast_dynamic-update-slice_fusion.33
  2429.0 23.3 fusion.254
  2452.3 28.0 fusion.255
  2544.1 21.6 collective-permute-done.1
  2571.4 26.0 bitcast_dynamic-update-slice_fusion.33
  2652.8 23.3 fusion.254
  2676.1 28.0 fusion.255
  2768.0 21.4 collective-permute-done.1
  2826.6 34.0 pad_maximum_fusion.2
  2862.4 18.7 bitcast_convert_fusion.1
  2881.2 18.4 bitcast_convert_fusion.2
  2899.5 31.5 pad_maximum_fusion.1
  2931.1 20.0 bitcast_convert_fusion
  2953.0 219.9 %reduce-scatter.9.cloned.1.call-done = bf16[512,4608]{0,1:T(8,128)(2,1)} async-done(((bf16[2048,4608]{0,1:T(8,128)(2,1)}), bf16[512,4608]{0,1:T(8,128)(2,1)}) %reduce-scatter.9.cloned.1.call-update) | async-done | bytes 4718608 | tf_op jit(solution)/shard_map/reduce_scatter | solution.py:292
  3179.2 750.5 %reduce-scatter.11.cloned.1.call-done = bf16[512,11264]{1,0:T(8,128)(2,1)} async-done(((bf16[2048,11264]{1,0:T(8,128)(2,1)}), bf16[512,11264]{1,0:T(8,128)(2,1)}) %reduce-scatter.11.cloned.1.call-update) | async-done | bytes 11534352 | tf_op jit(solution)/shard_map/reduce_scatter | solution.py:306
  3939.3 375.2 %reduce-scatter.13.cloned.1.call-done = bf16[1408,2048]{1,0:T(8,128)(2,1)} async-done(((bf16[5632,2048]{1,0:T(8,128)(2,1)}), bf16[1408,2048]{1,0:T(8,128)(2,1)}) %reduce-scatter.13.cloned.1.call-update) | async-done | bytes 5767184 | tf_op jit(solution)/shard_map/reduce_scatter | solution.py:325
  4322.5 18.2 reduce-scatter.15.cloned.1.call-done
  4347.9 371.4 %all-reduce.5.cloned.1.call-done = (bf16[1,512,2048]{1,2,0:T(8,128)(2,1)}, bf16[1,512,256]{1,2,0:T(8,128)(2,1)}, bf16[1,512,256]{1,2,0:T(8,128)(2,1)}, bf16[1,51...) async-done(((bf16[1,512,2048]{1,2,0:T(8,128)(2,1)}, bf16[1,512,256]{1,2,0:T(8,128)(2,1)}, ...) | async-done | bytes 22020112 | tf_op jit(solution)/shard_map/psum | solution.py:333
  (532 shorter events, 1037.8 us)
Async XLA Ops:
  7.2 33.4 all-gather.16.cloned.1.call-start
  7.9 61.5 %all-gather.18.cloned.1.call-start = ((), (), s32[]{:S(2)}) async-start(), calls=%async_computation.10 | async-start | bytes 1310720 | tf_op jit(solution)/shard_map/all_gather | solution.py:95
  8.7 211.5 %all-gather.20.cloned.1.call-start = ((), (), s32[]{:S(2)}) async-start(), calls=%async_computation.11 | async-start | bytes 10485760 | tf_op jit(solution)/shard_map/all_gather | solution.py:94
  9.4 360.1 %all-gather.22.cloned.1.call-start = ((), (), s32[]{:S(2)}) async-start(), calls=%async_computation.12 | async-start | bytes 10485760 | tf_op jit(solution)/shard_map/all_gather | solution.py:97
  10.0 750.3 %all-gather.24.cloned.1.call-start = ((), (), s32[]{:S(2)}) async-start(), calls=%async_computation.13 | async-start | bytes 28835840 | tf_op jit(solution)/shard_map/all_gather | solution.py:98
  10.6 1140.5 %all-gather.26.cloned.1.call-start = ((), (), s32[]{:S(2)}) async-start(), calls=%async_computation.14 | async-start | bytes 28835840 | tf_op jit(solution)/shard_map/all_gather | solution.py:99
  11.2 1531.0 %all-gather.28.cloned.1.call-start = ((), (), s32[]{:S(2)}) async-start(), calls=%async_computation.15 | async-start | bytes 28835840 | tf_op jit(solution)/shard_map/all_gather | solution.py:100
  1704.7 30.9 collective-permute-start
  1879.1 28.5 collective-permute-start
  2050.7 28.5 collective-permute-start
  2117.0 31.5 copy-start.29
  2117.0 184.6 %reduce-scatter.17.cloned.1.call-start = ((), (), s32[]{:S(2)}) async-start(), calls=%async_computation.18 | async-start | bytes 655360 | tf_op jit(solution)/shard_map/while/body/eval_jaxpr/reduce_scatter | solution.py:213
  2267.0 43.6 reduce-scatter.19.cloned.1.call-start
  2314.4 27.5 copy-start.30
  2316.7 25.2 collective-permute-start.1
  2341.9 31.6 copy-start.29
  2341.9 184.6 %reduce-scatter.17.cloned.1.call-start = ((), (), s32[]{:S(2)}) async-start(), calls=%async_computation.18 | async-start | bytes 655360 | tf_op jit(solution)/shard_map/while/body/eval_jaxpr/reduce_scatter | solution.py:213
  2492.0 42.3 reduce-scatter.19.cloned.1.call-start
  2538.1 27.7 copy-start.30
  2538.1 27.7 copy-start.33
  2540.4 25.4 collective-permute-start.1
  2565.8 31.6 copy-start.29
  2565.8 184.6 %reduce-scatter.17.cloned.1.call-start = ((), (), s32[]{:S(2)}) async-start(), calls=%async_computation.18 | async-start | bytes 655360 | tf_op jit(solution)/shard_map/while/body/eval_jaxpr/reduce_scatter | solution.py:213
  2715.8 42.3 reduce-scatter.19.cloned.1.call-start
  2761.9 27.5 copy-start.30
  2761.9 27.5 copy-start.33
  2764.3 25.1 collective-permute-start.1
  2798.1 374.7 %reduce-scatter.9.cloned.1.call-start = ((), (), s32[]{:S(2)}) async-start(), calls=%async_computation.6 | async-start | bytes 23592960 | tf_op jit(solution)/shard_map/reduce_scatter | solution.py:292
  2860.6 1069.2 %reduce-scatter.11.cloned.1.call-start = ((), (), s32[]{:S(2)}) async-start(), calls=%async_computation.7 | async-start | bytes 57671680 | tf_op jit(solution)/shard_map/reduce_scatter | solution.py:306
  2931.1 1383.4 %reduce-scatter.13.cloned.1.call-start = ((), (), s32[]{:S(2)}) async-start(), calls=%async_computation.8 | async-start | bytes 28835840 | tf_op jit(solution)/shard_map/reduce_scatter | solution.py:325
  2951.2 1389.5 %reduce-scatter.15.cloned.1.call-start = ((), (), s32[]{:S(2)}) async-start(), calls=%async_computation.16 | async-start | bytes 655360
  2953.0 1766.4 %all-reduce.5.cloned.1.call-start = ((), (), s32[]{:S(2)}) async-start(), calls=%async_computation.17 | async-start | bytes 44040192 | tf_op jit(solution)/shard_map/psum | solution.py:333
  (78 other events, 794.9 us)
Sparse Core Ops, SparseCore 0:
  9.6 30.7 all-gather.15
  41.9 27.4 all-gather.17
  71.0 149.1 all-gather.19
  221.6 147.8 all-gather.21
  370.9 389.3 all-gather.23
  761.7 389.3 all-gather.25
  1152.7 389.3 all-gather.27
  2267.1 21.1 reduce-scatter.16
  2290.6 19.9 reduce-scatter.18
  2492.1 19.9 reduce-scatter.16
  2514.3 19.9 reduce-scatter.18
  2716.0 19.7 reduce-scatter.16
  2738.1 19.9 reduce-scatter.18
  2860.7 312.1 reduce-scatter.8
  3175.2 754.5 reduce-scatter.10
  3932.0 382.3 reduce-scatter.12
  4317.2 23.4 reduce-scatter.14
  4345.3 374.0 all-reduce.4
where the time goes:
time: 4770 us; the launch traced here: 4760 us
  waiting for transfers between devices  3320 us (70%)
  matrix products  794 us (17%)
  other arithmetic  280 us (6%)
  local copies, waits for them, and re-layouts  214 us (4%)
  blocking collectives  111 us (2%)
    reduce_scatter x1, waiting for transfers between devices, body(): lax.psum_scatter(jnp.concatenate([inner_rows(normed_two_rows, grad_g_rows...  751 us
    all_gather x1, waiting for transfers between devices, body(): lax.all_gather(w_down[0], 'shard', axis=0, tiled=True)  391 us
    all_gather x1, waiting for transfers between devices, body(): lax.all_gather(w_up[0], 'shard', axis=0, tiled=True)  391 us
    all_gather x1, waiting for transfers between devices, body(): lax.all_gather(w_gate[0], 'shard', axis=0, tiled=True)  391 us
    reduce_scatter x1, waiting for transfers between devices, body(): lax.psum_scatter(down_term.astype(jnp.bfloat16), 'shard', scatter_dimensi...  375 us
    psum x1, waiting for transfers between devices, body(): lax.psum(query_part.astype(jnp.bfloat16), 'rep').astype(jnp.float32)  371 us
    dot_general x21, matrix products, times_t(): lax.dot_general(left_rows, right_rows, (((1,), (1,)), ((), ())), preferre...  220 us
    reduce_scatter x1, waiting for transfers between devices, body(): lax.psum_scatter(jnp.concatenate([inner_rows(normed_rows, grad_q_rows), i...  220 us
  transfers between devices with their start and end apart: 24, of which 17 were waited for; matrix products, arithmetic and copies ran while one was open for 7% of the time, Pallas kernels for 0%

commit v1 on v0

v1 whole, which is shorter than its diff:
```python
import functools, math
import jax
import jax.numpy as jnp
from jax import lax
from jax.sharding import PartitionSpec as P
from jax.experimental import pallas as pl
from jax.experimental.pallas import tpu as pltpu

HEADS = 32
KV_HEADS = 4
HEAD = 64
LOG2E = math.log2(math.e)
NEG_FILL = -1e30
F32, BF16 = jnp.float32, jnp.bfloat16


def mm(a, b):
    return jnp.dot(a, b, preferred_element_type=F32)


def attn_fwd_kernel(axis, pairs, q_ref, k_ref, v_ref, o_ref, lse_ref, bias_ref):
    keys, queries = bias_ref.shape
    offset = lax.axis_index(axis) * queries

    @pl.when(pl.program_id(0) == 0)
    def _():
        key_pos = lax.broadcasted_iota(jnp.int32, (keys, queries), 0)
        query_pos = lax.broadcasted_iota(jnp.int32, (keys, queries), 1) + offset
        bias_ref[...] = jnp.where(key_pos <= query_pos, 0.0, NEG_FILL)

    for half in range(2):
        key = k_ref[:, half * HEAD:(half + 1) * HEAD]
        value_t = v_ref[...].T[half * HEAD:(half + 1) * HEAD, :]
        for pair in range(pairs):
            col = (half * pairs + pair) * 2 * HEAD
            q_t = q_ref[:, col:col + 2 * HEAD].T
            outs = []
            for sub in range(2):
                head = (half * pairs + pair) * 2 + sub
                scores = mm(key, q_t[sub * HEAD:(sub + 1) * HEAD, :]) * (LOG2E * HEAD ** -0.5) + bias_ref[...]
                top = jnp.max(scores, axis=0, keepdims=True)
                prob = jnp.exp2(scores - top)
                total = jnp.sum(prob, axis=0, keepdims=True)
                outs.append(mm(value_t, prob.astype(BF16)) / total)
                lse_ref[0, head:head + 1, :] = top + jnp.log2(total)
            o_ref[:, col:col + 2 * HEAD] = jnp.concatenate(outs, axis=0).T.astype(BF16)


def attn_fwd(q, k, v, axis):
    queries, width = q.shape
    keys = k.shape[0]
    pairs = HEADS // KV_HEADS // 2
    steps = KV_HEADS // 2
    heads = HEADS // steps
    return pl.pallas_call(
        functools.partial(attn_fwd_kernel, axis, pairs),
        grid=(steps,),
        in_specs=[
            pl.BlockSpec((queries, width // steps), lambda i: (0, i)),
            pl.BlockSpec((keys, 2 * HEAD), lambda i: (0, i)),
            pl.BlockSpec((keys, 2 * HEAD), lambda i: (0, i)),
        ],
        out_specs=[
            pl.BlockSpec((queries, width // steps), lambda i: (0, i)),
            pl.BlockSpec((1, heads, queries), lambda i: (i, 0, 0)),
        ],
        out_shape=[
            jax.ShapeDtypeStruct((queries, width), BF16),
            jax.ShapeDtypeStruct((steps, heads, queries), F32),
        ],
        scratch_shapes=[pltpu.VMEM((keys, queries), F32)],
        compiler_params=pltpu.CompilerParams(vmem_limit_bytes=50 * 1024 * 1024),
        cost_estimate=pl.CostEstimate(
            flops=4 * queries * keys * width, bytes_accessed=4 * queries * width * 2,
            transcendentals=queries * keys * HEADS),
        name="attn_fwd",
    )(q, k, v)


def attn_bwd_kernel(axis, pairs, q_ref, k_ref, v_ref, o_ref, do_ref, lse_ref, dq_ref, dk_ref, dv_ref, bias_ref, dk_acc, dv_acc):
    keys, queries = bias_ref.shape
    offset = lax.axis_index(axis) * queries

    @pl.when(pl.program_id(0) == 0)
    def _():
        key_pos = lax.broadcasted_iota(jnp.int32, (keys, queries), 0)
        query_pos = lax.broadcasted_iota(jnp.int32, (keys, queries), 1) + offset
        bias_ref[...] = jnp.where(key_pos <= query_pos, 0.0, NEG_FILL)

    low_lane = lax.broadcasted_iota(jnp.int32, (queries, 2 * HEAD), 1) < HEAD
    for half in range(2):
        key = k_ref[:, half * HEAD:(half + 1) * HEAD]
        value = v_ref[:, half * HEAD:(half + 1) * HEAD]
        key_t = k_ref[...].T[half * HEAD:(half + 1) * HEAD, :]
        for pair in range(pairs):
            col = (half * pairs + pair) * 2 * HEAD
            q_rows = q_ref[:, col:col + 2 * HEAD]
            do_rows = do_ref[:, col:col + 2 * HEAD]
            q_t = q_rows.T
            do_t = do_rows.T
            delta_t = (o_ref[:, col:col + 2 * HEAD].astype(F32) * do_rows.astype(F32)).T
            dqs = []
            for sub in range(2):
                head = (half * pairs + pair) * 2 + sub
                rows = slice(sub * HEAD, (sub + 1) * HEAD)
                lane = low_lane if sub == 0 else jnp.logical_not(low_lane)
                scores = mm(key, q_t[rows, :]) * (LOG2E * HEAD ** -0.5) + bias_ref[...]
                prob = jnp.exp2(scores - lse_ref[0, head:head + 1, :])
                grad_prob = mm(value, do_t[rows, :])
                delta = jnp.sum(delta_t[rows, :], axis=0, keepdims=True)
                grad_score = (prob * (grad_prob - delta)).astype(BF16)
                prob = prob.astype(BF16)
                dqs.append(mm(key_t, grad_score))
                dk_term = mm(grad_score, jnp.where(lane, q_rows, jnp.zeros_like(q_rows)))
                dv_term = mm(prob, jnp.where(lane, do_rows, jnp.zeros_like(do_rows)))
                if pair == 0 and sub == 0:
                    dk_acc[...] = dk_term
                    dv_acc[...] = dv_term
                else:
                    dk_acc[...] += dk_term
                    dv_acc[...] += dv_term
            dq_ref[:, col:col + 2 * HEAD] = jnp.concatenate(dqs, axis=0).T * HEAD ** -0.5
        dk_sum = (dk_acc[:, :HEAD] + dk_acc[:, HEAD:]) * HEAD ** -0.5
        dv_sum = dv_acc[:, :HEAD] + dv_acc[:, HEAD:]
        dk_ref[:, half * HEAD:(half + 1) * HEAD] = dk_sum.astype(dk_ref.dtype)
        dv_ref[:, half * HEAD:(half + 1) * HEAD] = dv_sum.astype(dv_ref.dtype)


def attn_bwd(q, k, v, o, do, lse, axis):
    queries, width = q.shape
    keys = k.shape[0]
    pairs = HEADS // KV_HEADS // 2
    steps = KV_HEADS // 2
    heads = HEADS // steps
    wide = pl.BlockSpec((queries, width // steps), lambda i: (0, i))
    narrow = pl.BlockSpec((keys, 2 * HEAD), lambda i: (0, i))
    return pl.pallas_call(
        functools.partial(attn_bwd_kernel, axis, pairs),
        grid=(steps,),
        in_specs=[wide, narrow, narrow, wide, wide, pl.BlockSpec((1, heads, queries), lambda i: (i, 0, 0))],
        out_specs=[wide, narrow, narrow],
        out_shape=[
            jax.ShapeDtypeStruct((queries, width), F32),
            jax.ShapeDtypeStruct((keys, k.shape[1]), BF16),
            jax.ShapeDtypeStruct((keys, k.shape[1]), BF16),
        ],
        scratch_shapes=[pltpu.VMEM((keys, queries), F32), pltpu.VMEM((keys, 2 * HEAD), F32), pltpu.VMEM((keys, 2 * HEAD), F32)],
        compiler_params=pltpu.CompilerParams(vmem_limit_bytes=50 * 1024 * 1024),
        cost_estimate=pl.CostEstimate(
            flops=10 * queries * keys * width, bytes_accessed=12 * queries * width,
            transcendentals=queries * keys * HEADS),
        name="attn_bwd",
    )(q, k, v, o, do, lse)


EPSILON = 1e-05
ROPE_BASE = 10000.0


def angles_for(positions):
    half_dim = HEAD // 2
    inverse = ROPE_BASE ** (-(jnp.arange(half_dim, dtype=F32) * 2.0 / HEAD))
    angle_grid = positions.astype(F32)[:, None] * inverse[None, :]
    return (jnp.cos(angle_grid), jnp.sin(angle_grid))


def rotate(matrix, cos_table, sin_table):
    row_count = matrix.shape[0]
    half_dim = HEAD // 2
    pieces = matrix.reshape(row_count, -1, 2, half_dim)
    first_half = pieces[:, :, 0, :]
    second_half = pieces[:, :, 1, :]
    cos_wide = cos_table[:, None, :]
    sin_wide = sin_table[:, None, :]
    rotated = jnp.stack(
        [
            first_half * cos_wide - second_half * sin_wide,
            second_half * cos_wide + first_half * sin_wide,
        ],
        axis=2,
    )
    return rotated.reshape(row_count, -1)


def times_t(left_rows, right_rows):
    return lax.dot_general(left_rows, right_rows, (((1,), (1,)), ((), ())), preferred_element_type=F32)


def inner_rows(left_rows, right_rows):
    return lax.dot_general(left_rows, right_rows, (((0,), (0,)), ((), ())), preferred_element_type=F32)


def norm_back(grad_normed, stream, inv_root, gain_row):
    scaled = grad_normed * gain_row
    cubed = inv_root * inv_root * inv_root
    return inv_root * scaled - stream * cubed * jnp.mean(scaled * stream, axis=-1, keepdims=True)


def passed_along(block, axis, by):
    length = lax.axis_size(axis)
    pairs = [(i, i + by) for i in range(length) if 0 <= i + by < length]
    return lax.ppermute(block, axis, pairs)


def gather_rows(weight):
    parts = lax.axis_size("rep")
    rows = weight.shape[0] // parts
    own = lax.dynamic_slice_in_dim(weight, lax.axis_index("rep") * rows, rows, 0)
    return lax.all_gather(own, ("shard", "rep"), axis=0, tiled=True)


def scatter_rows(term):
    part = lax.psum_scatter(term, ("shard", "rep"), scatter_dimension=0, tiled=True)
    return lax.all_gather(part, "rep", axis=0, tiled=True)


def layer_forward(stream_in, weights, cos_table, sin_table):
    w_q, w_k, w_v, w_o, w_g, w_u, w_d, gains_wide = weights
    span_len, model_width = stream_in.shape
    stream = stream_in.astype(F32)
    inv_one = lax.rsqrt(jnp.mean(stream * stream, axis=-1, keepdims=True) + EPSILON)
    normed = (stream * inv_one * gains_wide[0]).astype(BF16)
    key_rows = rotate(mm(normed, w_k), cos_table, sin_table).astype(BF16)
    values = mm(normed, w_v).astype(BF16)
    kv_width = values.shape[1]
    kv_all = lax.all_gather(jnp.concatenate([key_rows, values], axis=1), "shard", axis=0, tiled=True)
    key_all, value_all = kv_all[:, :kv_width], kv_all[:, kv_width:]
    queries = rotate(mm(normed, w_q), cos_table, sin_table).astype(BF16)
    attended, log_total = attn_fwd(queries, key_all, value_all, "shard")
    middle = stream + mm(attended, w_o)
    inv_two = lax.rsqrt(jnp.mean(middle * middle, axis=-1, keepdims=True) + EPSILON)
    normed_two = (middle * inv_two * gains_wide[1]).astype(BF16)
    gate_proj = mm(normed_two, w_g)
    upward = mm(normed_two, w_u)
    hidden = (jax.nn.silu(gate_proj) * upward).astype(BF16)
    result = (middle + mm(hidden, w_d)).astype(BF16)
    kept = (stream, inv_one, normed, queries, key_all, value_all, log_total, attended, middle, inv_two,
            normed_two, gate_proj, upward, hidden)
    return result, kept


def layer_backward(grad_bf, kept, weights, cos_table, sin_table):
    w_q, w_k, w_v, w_o, w_g, w_u, w_d, gains_wide = weights
    (stream, inv_one, normed, queries, key_all, value_all, log_total, attended, middle, inv_two,
     normed_two, gate_proj, upward, hidden) = kept
    grad_out = grad_bf.astype(F32)
    grad_hidden = times_t(grad_bf, w_d)
    sigmoid_gate = jax.nn.sigmoid(gate_proj)
    grad_gate = (grad_hidden * upward * sigmoid_gate * (1.0 + gate_proj * (1.0 - sigmoid_gate))).astype(BF16)
    grad_up = (grad_hidden * gate_proj * sigmoid_gate).astype(BF16)
    grad_normed_two = times_t(grad_gate, w_g) + times_t(grad_up, w_u)
    grad_middle = grad_out + norm_back(grad_normed_two, middle, inv_two, gains_wide[1])
    gain_two = jnp.sum(grad_normed_two * middle * inv_two, axis=0)
    grad_branch = grad_middle.astype(BF16)
    grad_attended = times_t(grad_branch, w_o).astype(BF16)
    grad_q_rot, grad_k_part, grad_v_part = attn_bwd(
        queries, key_all, value_all, attended, grad_attended, log_total, "shard")
    kv_width = grad_k_part.shape[1]
    kv_sum = lax.psum_scatter(
        jnp.concatenate([grad_k_part, grad_v_part], axis=1), "shard", scatter_dimension=0, tiled=True).astype(F32)
    grad_query = rotate(grad_q_rot, cos_table, -sin_table).astype(BF16)
    grad_key = rotate(kv_sum[:, :kv_width], cos_table, -sin_table).astype(BF16)
    grad_value = kv_sum[:, kv_width:].astype(BF16)
    grad_normed = times_t(grad_query, w_q) + times_t(grad_key, w_k) + times_t(grad_value, w_v)
    grad_stream = grad_middle + norm_back(grad_normed, stream, inv_one, gains_wide[0])
    gain_one = jnp.sum(grad_normed * stream * inv_one, axis=0)
    terms = (grad_query, grad_key, grad_value, grad_branch, grad_gate, grad_up, grad_bf)
    return grad_stream, terms, jnp.stack([gain_one, gain_two])


def body(tokens, cotangent, live_counts, w_query, w_key, w_value, w_out, w_gate, w_up, w_down, norm_gains):
    section = lax.axis_index("section")
    slot_count, span_len, model_width = tokens.shape
    query_pos = lax.axis_index("shard") * span_len + jnp.arange(span_len, dtype=jnp.int32)
    cos_table, sin_table = angles_for(query_pos)
    live_mask = (jnp.arange(slot_count) < live_counts[0]).astype(F32)
    gains_wide = lax.all_gather(norm_gains[0], "shard", axis=1, tiled=True).astype(F32)
    weights = tuple(gather_rows(w[0]) for w in (w_query, w_key, w_value, w_out, w_gate, w_up, w_down))
    weights = weights + (gains_wide,)
    masked_in = (tokens.astype(F32) * live_mask[:, None, None]).astype(BF16)
    masked_cot = (cotangent.astype(F32) * live_mask[:, None, None]).astype(BF16)
    zero_slot = jnp.zeros((span_len, model_width), BF16)
    ticks = slot_count + 1
    results, kept_all = [], []
    received = zero_slot
    for tick in range(ticks):
        slot_in = masked_in[tick] if tick < slot_count else zero_slot
        own_in = jnp.where(section == 0, slot_in, received)
        result, kept = layer_forward(own_in, weights, cos_table, sin_table)
        received = passed_along(result, "section", 1)
        results.append(result)
        kept_all.append(kept)
    first = section == 0
    acts = jnp.stack([jnp.where(first, results[j], results[j + 1]) for j in range(slot_count)])
    received = zero_slot
    streams, term_list, gain_total = [], [], 0.0
    for tick in range(ticks):
        slot_cot = masked_cot[slot_count - 1 - tick] if tick < slot_count else zero_slot
        grad_bf = jnp.where(first, received, slot_cot)
        grad_stream, terms, gain_grad = layer_backward(grad_bf, kept_all[ticks - 1 - tick], weights, cos_table, sin_table)
        received = passed_along(grad_stream.astype(BF16), "section", -1)
        streams.append(grad_stream)
        term_list.append(terms)
        gain_total = gain_total + gain_grad
    grad_in = jnp.stack([
        jnp.where(first, streams[slot_count - j], streams[slot_count - 1 - j]) for j in range(slot_count)])

    def rows_of(pick_kept, pick_term):
        lefts, rights = [], []
        for j in range(slot_count):
            f0, f1 = pick_kept(kept_all[j]), pick_kept(kept_all[j + 1])
            lefts.append(jnp.where(first, f0, f1))
            b0, b1 = pick_term(term_list[ticks - 1 - j]), pick_term(term_list[ticks - 2 - j])
            rights.append(jnp.where(first, b0, b1))
        return jnp.concatenate(lefts, axis=0), jnp.concatenate(rights, axis=0)

    def weight_term(index, pick_term):
        left, right = rows_of(lambda k: k[index], pick_term)
        return inner_rows(left, right).astype(BF16)

    down_sum = scatter_rows(weight_term(13, lambda t: t[6]))
    ff_sum = scatter_rows(weight_term(10, lambda t: jnp.concatenate([t[4], t[5]], axis=1)))
    out_sum = scatter_rows(weight_term(7, lambda t: t[3]))
    qkv_sum = scatter_rows(weight_term(2, lambda t: jnp.concatenate([t[0], t[1], t[2]], axis=1)))
    kv_width = w_key.shape[2]
    ff_width = w_gate.shape[2]
    gain_part = lax.psum_scatter(gain_total, "shard", scatter_dimension=1, tiled=True)
    gain_sum = lax.psum(gain_part, "rep")
    outs = (
        qkv_sum[:, :model_width],
        qkv_sum[:, model_width:model_width + kv_width],
        qkv_sum[:, model_width + kv_width:],
        out_sum,
        ff_sum[:, :ff_width],
        ff_sum[:, ff_width:],
        down_sum,
        gain_sum,
    )
    return (acts[None], grad_in[None]) + tuple(out.astype(F32)[None] for out in outs)


def solution(mesh):
    tall = P("section", "shard", None)
    per_slot = P("section", "rep", "shard", None)
    return jax.shard_map(
        body,
        mesh=mesh,
        in_specs=(P("rep", "shard", None), P("rep", "shard", None), P("rep")) + (tall,) * 7 + (P("section", None, "shard"),),
        out_specs=(per_slot, per_slot) + (tall,) * 7 + (P("section", None, "shard"),),
        check_vma=False,
    )
```

time: 4770 us -> 2450 us (0.51)
  waiting for transfers between devices: 3320 us -> 1620 us
  matrix products: 794 us -> 444 us
  other arithmetic: 280 us -> 105 us
  Pallas kernels: 0 us -> 153 us
  local copies, waits for them, and re-layouts: 214 us -> 61.5 us
  blocking collectives: 111 us -> 20.6 us
    all_gather x7 -> x14, waiting for transfers between devices: 1500 us -> 679 us  [the longest x7 479 us: gather_rows(): return lax.all_gather(own, ('shard', 'rep'), axis=0, tiled=True)]
    reduce_scatter x9 -> x7, waiting for transfers between devices: 1360 us -> 842 us  [the longest x4 807 us: scatter_rows(): lax.psum_scatter(term, ('shard', 'rep'), scatter_dimension=0, tiled=True)]
    psum x1 -> x0, waiting for transfers between devices: 371 us -> none  [body(): lax.psum(query_part.astype(jnp.bfloat16), 'rep').astype(jnp.float32)]
    dot_general x42 -> x21, matrix products: 497 us -> 183 us  [mm(): return jnp.dot(a, b, preferred_element_type=F32)]
    pallas_call x0 -> x6, Pallas kernels: none -> 153 us  [the longest x3 79.9 us: attn_bwd(): pl.pallas_call(functools.partial(attn_bwd_kernel, axis, pairs), grid=(ste...]
    all_gather x7 -> x1, blocking collectives: 105 us -> 13.7 us  [body(): lax.all_gather(norm_gains[0], 'shard', axis=1, tiled=True).astype(F32)]
    convert_element_type x16 -> x5, other arithmetic: 90.1 us -> 9.82 us  [the longest x1 5.82 us: body(): masked_cot = (cotangent.astype(F32) * live_mask[:, None, None]).astype(BF16)]
    dynamic_update_slice x51 -> x0, local copies, waits for them, and re-layouts: 78.2 us -> none  [the longest x45 74.2 us: body(): _, (results, kept_all) = lax.scan(forward_tick, zero_slot[0], padded_in)]
  transfers between devices with their start and end apart: 24 -> 26, of which waited for: 17 -> 26; matrix products, arithmetic and copies ran while one was open for 7% -> 11% of each run, Pallas kernels for 0% -> 1%
where the time goes in v1:
time: 2450 us; the launch traced here: 2440 us
  waiting for transfers between devices  1620 us (66%)
  matrix products  444 us (18%)
  Pallas kernels  153 us (6%)
  other arithmetic  105 us (4%)
  local copies, waits for them, and re-layouts  61.5 us (3%)
    reduce_scatter x4, waiting for transfers between devices, scatter_rows(): lax.psum_scatter(term, ('shard', 'rep'), scatter_dimension=0, tiled=True)  807 us
    all_gather x7, waiting for transfers between devices, gather_rows(): return lax.all_gather(own, ('shard', 'rep'), axis=0, tiled=True)  479 us
    dot_general x21, matrix products, times_t(): lax.dot_general(left_rows, right_rows, (((1,), (1,)), ((), ())), preferre...  193 us
    dot_general x21, matrix products, mm(): return jnp.dot(a, b, preferred_element_type=F32)  183 us
    all_gather x4, waiting for transfers between devices, scatter_rows(): return lax.all_gather(part, 'rep', axis=0, tiled=True)  145 us
    ppermute x4, waiting for transfers between devices, passed_along(): return lax.ppermute(block, axis, pairs)  95.2 us
    pallas_call x3, Pallas kernels, attn_bwd(): pl.pallas_call(functools.partial(attn_bwd_kernel, axis, pairs), grid=(ste...  79.9 us
    pallas_call x3, Pallas kernels, attn_fwd(): pl.pallas_call(functools.partial(attn_fwd_kernel, axis, pairs), grid=(ste...  73.1 us
  transfers between devices with their start and end apart: 26, of which 26 were waited for; matrix products, arithmetic and copies ran while one was open for 11% of the time, Pallas kernels for 1%

profile of v1, /device:TPU:0, one launch (start us, length us, event | category | flops | bytes accessed | tf_op | source)
XLA Modules:
  0.0 2437.4 jit_solution(13253074515266689880)
XLA Ops:
  33.7 17.8 all-gather.39.cloned.1.call-done
  54.9 36.1 %all-gather.41.cloned.1.call-done = bf16[1,2048,256]{2,1,0:T(8,128)(2,1)} async-done(((bf16[1,128,256]{2,1,0:T(8,128)(2,1)}), bf16[1,2048,256]{2,1,0:T(8,128)(2,1)}) %all-gather.41.cloned.1.call-update) | async-done | bytes 1048592 | tf_op jit(solution)/shard_map/all_gather | solution.py:209
  122.2 75.7 %all-gather.37.cloned.1.call-done = bf16[1,2048,2048]{2,1,0:T(8,128)(2,1)} async-done(((bf16[1,128,2048]{2,1,0:T(8,128)(2,1)}), bf16[1,2048,2048]{2,1,0:T(8,128)(2,1)}) %all-gather.37.cloned.1.call-update) | async-done | bytes 8388624 | tf_op jit(solution)/shard_map/all_gather | solution.py:209
  217.5 24.5 %attn_fwd.3 = (bf16[256,2048]{1,0:T(8,128)(2,1)S(1)}, f32[2,16,256]{2,1,0:T(8,128)S(1)}) custom-call(bf16[256,2048]{1,0:T(8,128)(2,1)S(1)} %copy.78.q_ref, bf16[1024,256]{1,0:T(8,128)(2,1)S(1)} %get-tuple-element.110.k_ref, bf16[1024,256]{1,0:T(8,128)(2,1)S(1)} %get-tuple-element.109.v_ref), custom_call_target="tpu_custom_call" | custom-call | flops 2147483648 | bytes 4194304 | tf_op jit(solution)/shard_map/attn_fwd/pallas_call | solution.py:55
  242.0 31.6 %all-gather.43.cloned.1.call-done = bf16[1,2048,2048]{2,1,0:T(8,128)(2,1)} async-done(((bf16[1,128,2048]{2,1,0:T(8,128)(2,1)}), bf16[1,2048,2048]{2,1,0:T(8,128)(2,1)}) %all-gather.43.cloned.1.call-update) | async-done | bytes 8388624 | tf_op jit(solution)/shard_map/all_gather | solution.py:209
  281.6 111.1 %all-gather.45.cloned.1.call-done = bf16[1,2048,5632]{2,1,0:T(8,128)(2,1)} async-done(((bf16[1,128,5632]{2,1,0:T(8,128)(2,1)}), bf16[1,2048,5632]{2,1,0:T(8,128)(2,1)}) %all-gather.45.cloned.1.call-update) | async-done | bytes 23068688 | tf_op jit(solution)/shard_map/all_gather | solution.py:209
  408.9 104.7 %all-gather.47.cloned.1.call-done = bf16[1,2048,5632]{2,1,0:T(8,128)(2,1)} async-done(((bf16[1,128,5632]{2,1,0:T(8,128)(2,1)}), bf16[1,2048,5632]{2,1,0:T(8,128)(2,1)}) %all-gather.47.cloned.1.call-update) | async-done | bytes 23068688 | tf_op jit(solution)/shard_map/all_gather | solution.py:209
  513.6 18.5 multiply_convert_fusion.8
  532.0 102.4 %all-gather.49.cloned.1.call-done = bf16[1,5632,2048]{2,1,0:T(8,128)(2,1)} async-done(((bf16[1,352,2048]{2,1,0:T(8,128)(2,1)}), bf16[1,5632,2048]{2,1,0:T(8,128)(2,1)}) %all-gather.49.cloned.1.call-update) | async-done | bytes 23068688 | tf_op jit(solution)/shard_map/all_gather | solution.py:209
  649.6 22.8 collective-permute-done
  688.3 18.8 all-gather.25.cloned.1.call-done
  708.4 24.3 attn_fwd.4
  754.9 18.8 broadcast_select_fusion.1
  789.3 21.8 collective-permute-done.1
  825.2 19.1 all-gather.27.cloned.1.call-done
  845.6 24.3 attn_fwd.5
  891.2 19.0 broadcast_select_fusion
  965.2 26.6 %attn_bwd.3 = (f32[256,2048]{1,0:T(8,128)}, bf16[1024,256]{1,0:T(8,128)(2,1)S(1)}, bf16[1024,256]{1,0:T(8,128)(2,1)S(1)}) custom-call(bf16[256,2048]{1,0:T(8,128)(2,1)S(1)} %copy.86.q_ref, bf16[1024,256]{1,0:T(8,128)(2,1)S(1)} %copy-done.19, bf16[1024,256]{1,0:T(8,128)(2,1)S(1)} %copy-done.17, bf16[256,2048]{1,0:T(8,128)(2,1)} %copy-done.6, ...), custom_call_target="tpu_custom_call" | custom-call | flops 5368709120 | bytes 6291456 | tf_op jit(solution)/shard_map/attn_bwd/pallas_call | solution.py:137
  1029.9 25.3 %collective-permute-done.2 = bf16[256,2048]{1,0:T(8,128)(2,1)S(1)} collective-permute-done((bf16[256,2048]{1,0:T(8,128)(2,1)S(1)}, bf16[256,2048]{1,0:T(8,128)(2,1)S(1)}, u32[]{:S(2)}, u32[]{:S(2)}) %collective-permute-start.2) | collective-permute-done | bytes 1048608 | tf_op jit(solution)/shard_map/ppermute | solution.py:202
  1056.4 24.1 multiply_convert_fusion.3
  1119.8 26.6 %attn_bwd.4 = (f32[256,2048]{1,0:T(8,128)}, bf16[1024,256]{1,0:T(8,128)(2,1)S(1)}, bf16[1024,256]{1,0:T(8,128)(2,1)S(1)}) custom-call(bf16[256,2048]{1,0:T(8,128)(2,1)S(1)} %copy.82.q_ref, bf16[1024,256]{1,0:T(8,128)(2,1)S(1)} %copy-done.15, bf16[1024,256]{1,0:T(8,128)(2,1)S(1)} %copy-done.13, bf16[256,2048]{1,0:T(8,128)(2,1)} %copy-done.4, ...), custom_call_target="tpu_custom_call" | custom-call | flops 5368709120 | bytes 6291456 | tf_op jit(solution)/shard_map/attn_bwd/pallas_call | solution.py:137
  1181.7 25.3 %collective-permute-done.3 = bf16[256,2048]{1,0:T(8,128)(2,1)S(1)} collective-permute-done((bf16[256,2048]{1,0:T(8,128)(2,1)S(1)}, bf16[256,2048]{1,0:T(8,128)(2,1)S(1)}, u32[]{:S(2)}, u32[]{:S(2)}) %collective-permute-start.3) | collective-permute-done | bytes 1048608 | tf_op jit(solution)/shard_map/ppermute | solution.py:202
  1207.0 17.4 multiply_convert_fusion.1
  1263.7 26.6 %attn_bwd.5 = (f32[256,2048]{1,0:T(8,128)}, bf16[1024,256]{1,0:T(8,128)(2,1)S(1)}, bf16[1024,256]{1,0:T(8,128)(2,1)S(1)}) custom-call(bf16[256,2048]{1,0:T(8,128)(2,1)S(1)} %copy.78.q_ref, bf16[1024,256]{1,0:T(8,128)(2,1)S(1)} %copy-done.11, bf16[1024,256]{1,0:T(8,128)(2,1)S(1)} %copy-done.9, bf16[256,2048]{1,0:T(8,128)(2,1)} %copy-done.2, ...), custom_call_target="tpu_custom_call" | custom-call | flops 5368709120 | bytes 6291456 | tf_op jit(solution)/shard_map/attn_bwd/pallas_call | solution.py:137
  1334.6 18.7 convolution_convert_fusion.1
  1364.6 34.1 %convolution_convert_fusion = bf16[2048,11264]{1,0:T(8,128)(2,1)} fusion(bf16[256,11264]{1,0:T(8,128)(2,1)} %get-tuple-element.81, bf16[256,11264]{1,0:T(8,128)(2,1)} %get-tuple-element.80, bf16[256,2048]{1,0:T(8,128)(2,1)S(1)} %copy-done.67, bf16[256,2048]{1,0:T(8,128)(2,1)S(1)} %copy-done.66), kind=kOutput, calls=%fused_computation | convolution fusion | flops 23672651776 | bytes 59768832 | tf_op jit(solution)/shard_map/dot_general | solution.py:190
  1425.1 123.8 %reduce-scatter.17.cloned.1.call-done = bf16[128,2560]{1,0:T(8,128)(2,1)} async-done(((bf16[2048,2560]{1,0:T(8,128)(2,1)}), bf16[128,2560]{1,0:T(8,128)(2,1)}) %reduce-scatter.17.cloned.1.call-update) | async-done | bytes 655376 | tf_op jit(solution)/shard_map/reduce_scatter | solution.py:213
  1549.0 231.1 %reduce-scatter.23.cloned.1.call-done = bf16[352,2048]{1,0:T(8,128)(2,1)} async-done(((bf16[5632,2048]{1,0:T(8,128)(2,1)}), bf16[352,2048]{1,0:T(8,128)(2,1)}) %reduce-scatter.23.cloned.1.call-update) | async-done | bytes 1441808 | tf_op jit(solution)/shard_map/reduce_scatter | solution.py:213
  1780.2 436.9 %reduce-scatter.21.cloned.1.call-done = bf16[128,11264]{1,0:T(8,128)(2,1)} async-done(((bf16[2048,11264]{1,0:T(8,128)(2,1)}), bf16[128,11264]{1,0:T(8,128)(2,1)}) %reduce-scatter.21.cloned.1.call-update) | async-done | bytes 2883600 | tf_op jit(solution)/shard_map/reduce_scatter | solution.py:213
  2273.2 22.9 all-gather.29.cloned.1.call-done
  2302.3 38.8 %all-gather.35.cloned.1.call-done = bf16[1408,2048]{1,0:T(8,128)(2,1)} async-done(((bf16[352,2048]{1,0:T(8,128)(2,1)}), bf16[1408,2048]{1,0:T(8,128)(2,1)}) %all-gather.35.cloned.1.call-update) | async-done | bytes 5767184 | tf_op jit(solution)/shard_map/all_gather | solution.py:214
  2350.0 68.9 %all-gather.33.cloned.1.call-done = bf16[512,11264]{1,0:T(8,128)(2,1)} async-done(((bf16[128,11264]{1,0:T(8,128)(2,1)}), bf16[512,11264]{1,0:T(8,128)(2,1)}) %all-gather.33.cloned.1.call-update) | async-done | bytes 11534352 | tf_op jit(solution)/shard_map/all_gather | solution.py:214
  (408 shorter events, 582.4 us)
Async XLA Ops:
  7.2 44.2 %all-gather.39.cloned.1.call-start = ((), (), s32[]{:S(2)}) async-start(), calls=%async_computation.23 | async-start | bytes 1114112 | tf_op jit(solution)/shard_map/all_gather | solution.py:209
  8.9 82.2 %all-gather.41.cloned.1.call-start = ((), (), s32[]{:S(2)}) async-start(), calls=%async_computation.24 | async-start | bytes 1114112 | tf_op jit(solution)/shard_map/all_gather | solution.py:209
  10.4 110.4 %all-gather.23.cloned.1.call-start = ((), (), s32[]{:S(2)}) async-start(), calls=%async_computation.8 | async-start | bytes 1310720 | tf_op jit(solution)/shard_map/all_gather | solution.py:226
  32.9 177.3 %copy-start.84 = (f32[256]{0:T(256)}, f32[256]{0:T(256)S(1)}, u32[]{:S(2)}) copy-start(f32[256]{0:T(256)S(1)} %get-tuple-element.135) | copy-start | bytes 3076
  93.9 104.0 %all-gather.37.cloned.1.call-start = ((), (), s32[]{:S(2)}) async-start(), calls=%async_computation.22 | async-start | bytes 8912896 | tf_op jit(solution)/shard_map/all_gather | solution.py:209
  94.8 178.9 %all-gather.43.cloned.1.call-start = ((), (), s32[]{:S(2)}) async-start(), calls=%async_computation.25 | async-start | bytes 8912896 | tf_op jit(solution)/shard_map/all_gather | solution.py:209
  96.7 295.9 %all-gather.45.cloned.1.call-start = ((), (), s32[]{:S(2)}) async-start(), calls=%async_computation.26 | async-start | bytes 24510464 | tf_op jit(solution)/shard_map/all_gather | solution.py:209
  99.4 414.2 %all-gather.47.cloned.1.call-start = ((), (), s32[]{:S(2)}) async-start(), calls=%async_computation.27 | async-start | bytes 24510464 | tf_op jit(solution)/shard_map/all_gather | solution.py:209
  102.1 532.4 %all-gather.49.cloned.1.call-start = ((), (), s32[]{:S(2)}) async-start(), calls=%async_computation.28 | async-start | bytes 24510464 | tf_op jit(solution)/shard_map/all_gather | solution.py:209
  104.8 602.3 %all-gather.25.cloned.1.call-start = ((), (), s32[]{:S(2)}) async-start(), calls=%async_computation.9 | async-start | bytes 1310720 | tf_op jit(solution)/shard_map/all_gather | solution.py:226
  122.1 95.3 %copy-start.8 = (bf16[1024,256]{1,0:T(8,128)(2,1)}, bf16[1024,256]{1,0:T(8,128)(2,1)S(1)}, u32[]{:S(2)}) copy-start(bf16[1024,256]{1,0:T(8,128)(2,1)S(1)} %get-tuple-element.109.v_ref) | copy-start | bytes 1572868
  122.1 95.3 %copy-start.10 = (bf16[1024,256]{1,0:T(8,128)(2,1)}, bf16[1024,256]{1,0:T(8,128)(2,1)S(1)}, u32[]{:S(2)}) copy-start(bf16[1024,256]{1,0:T(8,128)(2,1)S(1)} %get-tuple-element.110.k_ref) | copy-start | bytes 1572868
  281.6 232.0 %copy-start.86 = (f32[256]{0:T(256)}, f32[256]{0:T(256)S(1)}, u32[]{:S(2)}) copy-start(f32[256]{0:T(256)S(1)} %get-tuple-element.137) | copy-start | bytes 3076
  392.7 120.9 %copy-start.38 = (f32[256,2048]{1,0:T(8,128)S(1)}, f32[256,2048]{1,0:T(8,128)}, u32[]{:S(2)}) copy-start(f32[256,2048]{1,0:T(8,128)} %get-tuple-element.149) | copy-start | bytes 6291460
  646.0 26.3 %collective-permute-start = (bf16[256,2048]{1,0:T(8,128)(2,1)S(1)}, bf16[256,2048]{1,0:T(8,128)(2,1)S(1)}, u32[]{:S(2)}, u32[]{:S(2)}) collective-permute-start(bf16[256,2048]{1,0:T(8,128)(2,1)S(1)} %fusion.105), channel_id=1, source_target_pairs={{0,16},{1,17},{2,18},{3,19},{4,20},{5,21},{6,22},{7,23},{8,24},{9,... | collective-permute-start | bytes 3145736 | tf_op jit(solution)/shard_map/ppermute | solution.py:202
  678.0 166.3 %all-gather.27.cloned.1.call-start = ((), (), s32[]{:S(2)}) async-start(), calls=%async_computation.10 | async-start | bytes 1310720 | tf_op jit(solution)/shard_map/all_gather | solution.py:226
  785.4 25.6 %collective-permute-start.1 = (bf16[256,2048]{1,0:T(8,128)(2,1)S(1)}, bf16[256,2048]{1,0:T(8,128)(2,1)S(1)}, u32[]{:S(2)}, u32[]{:S(2)}) collective-permute-start(bf16[256,2048]{1,0:T(8,128)(2,1)S(1)} %fusion.102), channel_id=1, source_target_pairs={{0,16},{1,17},{2,18},{3,19},{4,20},{5,21},{6,22},{7,23},{8,24},{9,... | collective-permute-start | bytes 3145736 | tf_op jit(solution)/shard_map/ppermute | solution.py:202
  815.4 204.3 %reduce-scatter.11.cloned.1.call-start = ((), (), s32[]{:S(2)}) async-start(), calls=%async_computation.11 | async-start | bytes 1310720 | tf_op jit(solution)/shard_map/reduce_scatter | solution.py:259
  992.9 179.8 %reduce-scatter.13.cloned.1.call-start = ((), (), s32[]{:S(2)}) async-start(), calls=%async_computation.12 | async-start | bytes 1310720 | tf_op jit(solution)/shard_map/reduce_scatter | solution.py:259
  1028.5 26.8 %collective-permute-start.2 = (bf16[256,2048]{1,0:T(8,128)(2,1)S(1)}, bf16[256,2048]{1,0:T(8,128)(2,1)S(1)}, u32[]{:S(2)}, u32[]{:S(2)}) collective-permute-start(bf16[256,2048]{1,0:T(8,128)(2,1)S(1)} %get-tuple-element.68), channel_id=1, source_target_pairs={{16,0},{17,1},{18,2},{19,3},{20,4},{21,5},{22,6},{23,7},{24,8},{25... | collective-permute-start | bytes 3145736 | tf_op jit(solution)/shard_map/ppermute | solution.py:202
  1147.4 169.2 %reduce-scatter.15.cloned.1.call-start = ((), (), s32[]{:S(2)}) async-start(), calls=%async_computation.13 | async-start | bytes 1310720 | tf_op jit(solution)/shard_map/reduce_scatter | solution.py:259
  1180.4 26.6 %collective-permute-start.3 = (bf16[256,2048]{1,0:T(8,128)(2,1)S(1)}, bf16[256,2048]{1,0:T(8,128)(2,1)S(1)}, u32[]{:S(2)}, u32[]{:S(2)}) collective-permute-start(bf16[256,2048]{1,0:T(8,128)(2,1)S(1)} %get-tuple-element.66), channel_id=1, source_target_pairs={{16,0},{17,1},{18,2},{19,3},{20,4},{21,5},{22,6},{23,7},{24,8},{25... | collective-permute-start | bytes 3145736 | tf_op jit(solution)/shard_map/ppermute | solution.py:202
  1291.4 133.6 %reduce-scatter.19.cloned.1.call-start = ((), (), s32[]{:S(2)}) async-start(), calls=%async_computation.16 | async-start | bytes 8912896 | tf_op jit(solution)/shard_map/reduce_scatter | solution.py:213
  1301.1 247.8 %reduce-scatter.17.cloned.1.call-start = ((), (), s32[]{:S(2)}) async-start(), calls=%async_computation.14 | async-start | bytes 11141120 | tf_op jit(solution)/shard_map/reduce_scatter | solution.py:213
  1333.0 447.2 %reduce-scatter.23.cloned.1.call-start = ((), (), s32[]{:S(2)}) async-start(), calls=%async_computation.20 | async-start | bytes 24510464 | tf_op jit(solution)/shard_map/reduce_scatter | solution.py:213
  1353.4 863.6 %reduce-scatter.21.cloned.1.call-start = ((), (), s32[]{:S(2)}) async-start(), calls=%async_computation.18 | async-start | bytes 49020928 | tf_op jit(solution)/shard_map/reduce_scatter | solution.py:213
  1398.7 847.6 %reduce-scatter.25.cloned.1.call-start = ((), (), s32[]{:S(2)}) async-start(), calls=%async_computation.29 | async-start | bytes 1310720
  1409.6 859.4 %all-gather.31.cloned.1.call-start = ((), (), s32[]{:S(2)}) async-start(), calls=%async_computation.17 | async-start | bytes 2621440 | tf_op jit(solution)/shard_map/all_gather | solution.py:214
  1425.1 871.0 %all-gather.29.cloned.1.call-start = ((), (), s32[]{:S(2)}) async-start(), calls=%async_computation.15 | async-start | bytes 3276800 | tf_op jit(solution)/shard_map/all_gather | solution.py:214
  1548.9 792.1 %all-gather.35.cloned.1.call-start = ((), (), s32[]{:S(2)}) async-start(), calls=%async_computation.21 | async-start | bytes 7208960 | tf_op jit(solution)/shard_map/all_gather | solution.py:214
  1780.1 437.0 %copy-start.63 = (bf16[256,2048]{1,0:T(8,128)(2,1)S(1)}, bf16[256,2048]{1,0:T(8,128)(2,1)}, u32[]{:S(2)}) copy-start(bf16[256,2048]{1,0:T(8,128)(2,1)} %copy-done.62) | copy-start | bytes 3145732
  1780.2 638.7 %all-gather.33.cloned.1.call-start = ((), (), s32[]{:S(2)}) async-start(), calls=%async_computation.19 | async-start | bytes 14417920 | tf_op jit(solution)/shard_map/all_gather | solution.py:214
  (97 other events, 1053.5 us)
Sparse Core Ops, SparseCore 0:
  10.8 40.6 all-gather.38
  54.2 36.8 all-gather.40
  94.0 26.8 all-gather.22
  123.4 74.3 all-gather.36
  200.5 73.1 all-gather.42
  275.7 116.9 all-gather.44
  394.8 118.6 all-gather.46
  515.7 118.6 all-gather.48
  678.1 28.9 all-gather.24
  815.5 28.7 all-gather.26
  993.1 26.6 reduce-scatter.10
  1147.6 25.0 reduce-scatter.12
  1291.5 25.0 reduce-scatter.14
  1321.7 103.3 reduce-scatter.18
  1430.1 118.8 reduce-scatter.16
  1553.4 226.6 reduce-scatter.22
  1784.8 432.2 reduce-scatter.20
  2219.9 26.2 reduce-scatter.24
  2247.8 21.2 all-gather.30
  2270.5 25.5 all-gather.28
  2297.6 43.3 all-gather.34
  2342.6 76.1 all-gather.32

commit v2 on v1

--- a/solution.py
+++ b/solution.py
@@ -153,6 +153,348 @@
     )(q, k, v, o, do, lse)
 
 
+MESH_IDS = pl.DeviceIdType.MESH
+DELAY = 3
+LANES = 128
+BUFS = 26
+
+
+def remote(src, dst, send_sem, recv_sem, peer):
+    return pltpu.make_async_remote_copy(src, dst, send_sem, recv_sem, device_id=peer, device_id_type=MESH_IDS)
+
+
+def reduce_stages(z_first, blocks, segments, place, a_ref, b_ref, bufs):
+    n, me, rep, right, core_peer, y_peer = place
+    own_core, own_y = lax.rem(rep, 2), rep // 2
+    (send_c, own, land_c, keep, send_y, land_y, send_z, land_z, send_f,
+     sc_sem, rc_sem, cr_c, sy_sem, ry_sem, cr_y, sz_sem, rz_sem, ly_sem, sfy_sem, sfc_sem,
+     rfy_sem, rfc_sem, sfw_sem, rfw_sem) = bufs
+    rows = own.shape[2]
+    depth = land_z.shape[1]
+    items = b_ref.shape[2] // LANES * blocks
+    starts = [first for _, _, first in segments]
+    ends = starts[1:] + [items // blocks]
+
+    def spot_of(out, first, r, p):
+        width = out.shape[1] // 4
+        column = pl.multiple_of(r * width + (p // blocks - first) * LANES, LANES)
+        row = pl.multiple_of(lax.rem(p, blocks) * rows, 16)
+        return out.at[pl.ds(row, rows), pl.ds(column, LANES)]
+
+    def each_segment(p, fn):
+        for (out, _, first), last in zip(segments, ends):
+            if len(segments) == 1:
+                fn(lambda r, out=out, first=first: spot_of(out, first, r, p))
+                continue
+            group = p // blocks
+
+            @pl.when(jnp.logical_and(group >= first, group < last))
+            def _(out=out, first=first):
+                fn(lambda r: spot_of(out, first, r, p))
+
+    def c_copy(a, s):
+        return remote(send_c.at[a], land_c.at[s], sc_sem.at[a], rc_sem.at[s], core_peer)
+
+    def y_copy(a, s):
+        return remote(send_y.at[a], land_y.at[s], sy_sem.at[a], ry_sem.at[s], y_peer)
+
+    def z_copy(a, s, p):
+        b = lax.rem(p, depth)
+        return remote(send_z.at[a], land_z.at[s, b], sz_sem.at[a], rz_sem.at[s, b], right)
+
+    def f_local(a, spot):
+        return pltpu.make_async_copy(send_f.at[a], spot(rep), ly_sem.at[a])
+
+    def f_y(a, p, spot):
+        return remote(send_f.at[a], spot(rep), sfy_sem.at[a], rfy_sem.at[p], y_peer)
+
+    def f_core(a, p, spot):
+        return remote(send_f.at[a], spot(rep), sfc_sem.at[a], rfc_sem.at[p], core_peer)
+
+    def f_turn(a, p, spot):
+        there = spot(rep + 2 - 4 * own_y)
+        return remote(there, there, sfw_sem.at[a], rfw_sem.at[p], core_peer)
+
+    def stage_zero(a, s, p):
+        dest = lax.rem(me + 2 * n - 1 - s, n)
+        row = pl.multiple_of((dest * blocks + lax.rem(p, blocks)) * rows, 16)
+        which = 0
+        for (_, index, first) in segments[1:]:
+            which = jnp.where(p // blocks >= first, index, which)
+        block = a_ref[which, pl.ds(row, rows), :]
+        column = pl.ds(pl.multiple_of(p // blocks * LANES, LANES), LANES)
+        for y in range(2):
+            send_c[a, y] = mm(block, b_ref[2 * y + 1 - own_core, :, column]).astype(BF16)
+
+        @pl.when(p >= 1)
+        def _():
+            pl.semaphore_wait(cr_c.at[s], 1)
+        c_copy(a, s).start()
+        for y in range(2):
+            own[a, y] = mm(block, b_ref[2 * y + own_core, :, column])
+
+    def credit(sem, s, p, peer):
+        @pl.when(p + 1 < items)
+        def _():
+            pl.semaphore_signal(sem.at[s], inc=1, device_id=peer, device_id_type=MESH_IDS)
+
+    def start_y(a, s, p):
+        y_copy(a, s).start()
+
+    def finish(a, p, total):
+        send_f[a] = total.astype(BF16)
+
+        def send(spot):
+            f_y(a, p, spot).start()
+            f_core(a, p, spot).start()
+            f_local(a, spot).start()
+        each_segment(p, send)
+
+    def stage_one_y(a, s, p):
+        c_copy(a, s).wait()
+        send_y[a] = (own[a, 1 - own_y] + land_c[s, 1 - own_y].astype(F32)).astype(BF16)
+
+        @pl.when(p >= 1)
+        def _():
+            pl.semaphore_wait(cr_y.at[s], 1)
+        y_copy(a, s).start()
+        keep[a] = own[a, own_y] + land_c[s, own_y].astype(F32)
+        credit(cr_c, s, p, core_peer)
+
+    def stage_two_y(a, s, p):
+        y_copy(a, s).wait()
+        keep[a] = keep[a] + land_y[s].astype(F32)
+        credit(cr_y, s, p, y_peer)
+
+        @pl.when(s > 0)
+        def _():
+            z_copy(a, s - 1, p).wait_recv()
+            keep[a] = keep[a] + land_z[s - 1, lax.rem(p, depth)].astype(F32)
+
+        @pl.when(s < n - 1)
+        def _():
+            send_z[a] = keep[a].astype(BF16)
+            z_copy(a, s, p).start()
+
+        @pl.when(s == n - 1)
+        def _():
+            finish(a, p, keep[a])
+
+    def stage_one_z(a, s, p):
+        c_copy(a, s).wait()
+        for y in range(2):
+            own[a, y] = own[a, y] + land_c[s, y].astype(F32)
+        credit(cr_c, s, p, core_peer)
+
+        @pl.when(s > 0)
+        def _():
+            z_copy(a, s - 1, p).wait_recv()
+            for y in range(2):
+                own[a, y] = own[a, y] + land_z[s - 1, lax.rem(p, depth), y].astype(F32)
+
+        @pl.when(s < n - 1)
+        def _():
+            send_z[a] = own[a].astype(BF16)
+            z_copy(a, s, p).start()
+
+        @pl.when(s == n - 1)
+        def _():
+            send_y[a] = own[a, 1 - own_y].astype(BF16)
+
+            @pl.when(p >= 1)
+            def _():
+                pl.semaphore_wait(cr_y.at[0], 1)
+            y_copy(a, 0).start()
+            keep[a] = own[a, own_y]
+
+    def stage_two_z(a, s, p):
+        @pl.when(s < n - 1)
+        def _():
+            z_copy(a, s, p).wait_send()
+
+        @pl.when(s == n - 1)
+        def _():
+            y_copy(a, 0).wait()
+            finish(a, p, keep[a] + land_y[0].astype(F32))
+            credit(cr_y, 0, p, y_peer)
+
+    def stage_three(a, s, p):
+        if not z_first:
+            @pl.when(s < n - 1)
+            def _():
+                z_copy(a, s, p).wait_send()
+
+        @pl.when(s == n - 1)
+        def _():
+            def turn(spot):
+                f_local(a, spot).wait()
+                f_core(a, p, spot).wait_send()
+                f_y(a, p, spot).wait()
+                f_turn(a, p, spot).start()
+            each_segment(p, turn)
+
+    def stage_four(a, s, p):
+        @pl.when(s == n - 1)
+        def _():
+            def end(spot):
+                f_core(a, p, spot).wait_recv()
+                f_turn(a, p, spot).wait()
+            each_segment(p, end)
+
+    fns = (stage_zero, stage_one_z if z_first else stage_one_y, stage_two_z if z_first else stage_two_y,
+           stage_three, stage_four)
+    return items, fns
+
+
+def reduce_kernel(streams, slots, *refs):
+    n = lax.axis_size("shard")
+    me = lax.axis_index("shard")
+    rep = lax.axis_index("rep")
+    section = lax.axis_index("section")
+    right = {"shard": lax.rem(me + 1, n)}
+    left = {"shard": lax.rem(me + n - 1, n)}
+    core_peer = {"rep": rep + 1 - 2 * lax.rem(rep, 2)}
+    y_peer = {"rep": rep + 2 - 4 * (rep // 2)}
+    place = (n, me, rep, right, core_peer, y_peer)
+
+    refs = list(refs)
+    lefts = [[refs.pop(0) for _ in stream["lefts"]] for stream in streams]
+    rights = [[[[refs.pop(0) for _ in range(slots + 1)] for _ in segment] for segment in stream["rights"]] for stream in streams]
+    outs = [[refs.pop(0) for _ in stream["rights"]] for stream in streams]
+    per = [[refs.pop(0) for _ in range(BUFS)] for _ in streams]
+    load_sem = refs.pop(0)
+
+    barrier = pltpu.get_barrier_semaphore()
+    for peer in (left, right, core_peer, y_peer):
+        pl.semaphore_signal(barrier, inc=1, device_id=peer, device_id_type=MESH_IDS)
+
+    def load_all(at_section):
+        loads = []
+
+        def load(src, dst):
+            loads.append(pltpu.make_async_copy(src, dst, load_sem.at[len(loads)]))
+            loads[-1].start()
+        for left_refs, right_refs, bufs in zip(lefts, rights, per):
+            a_ref, b_ref = bufs[0], bufs[1]
+            for k, src in enumerate(left_refs):
+                load(src, a_ref.at[k])
+            base = 0
+            for segment in right_refs:
+                quarter = sum(ticks[0].shape[1] for ticks in segment) // 4
+                for r in range(4):
+                    at = 0
+                    for ticks in segment:
+                        width = ticks[0].shape[1]
+                        lo, hi = max(r * quarter, at), min((r + 1) * quarter, at + width)
+                        if lo < hi:
+                            for j in range(slots):
+                                tick = ticks[slots - j if at_section == 0 else slots - 1 - j]
+                                span = tick.shape[0]
+                                load(tick.at[:, lo - at:hi - at],
+                                     b_ref.at[r, j * span:(j + 1) * span, base + lo - r * quarter:base + hi - r * quarter])
+                        at += width
+                base += quarter
+        for copy in loads:
+            copy.wait()
+
+    for value in range(2):
+        @pl.when(section == value)
+        def _(value=value):
+            load_all(value)
+    pl.semaphore_wait(barrier, 4)
+
+    work, last = [], 0
+    for stream, segs, bufs in zip(streams, outs, per):
+        items, fns = reduce_stages(
+            stream["z_first"], stream["blocks"],
+            [(out, index, first) for out, index, first in zip(segs, stream["which"], stream["firsts"])],
+            place, bufs[0], bufs[1], bufs[2:])
+        pace = stream["pace"]
+        total = n * (items + n - 1)
+        work.append((pace, items, fns))
+        last = max(last, pace * (total + 4 * DELAY))
+
+    def step(i, carry):
+        for k in (4, 3, 2, 1, 0):
+            for pace, items, fns in work:
+                v = i // pace - DELAY * k
+                s = lax.rem(v + n * DELAY * 4, n)
+                p = (v - s) // n - s
+                fine = jnp.logical_and(jnp.logical_and(v >= 0, lax.rem(i, pace) == 0), jnp.logical_and(p >= 0, p < items))
+
+                @pl.when(fine)
+                def _(s=s, p=p, v=v, fn=fns[k]):
+                    fn(lax.rem(v, DELAY), s, p)
+        return carry
+
+    lax.fori_loop(0, last, step, 0)
+
+
+def reduce_weights(streams, slots, collective_id, name):
+    n = lax.axis_size("shard")
+    operands, out_shapes, scratch, flops, moved, plans, loads = [], [], [], 0, 0, [], 0
+    dma, regular = pltpu.SemaphoreType.DMA, pltpu.SemaphoreType.REGULAR
+    for stream in streams:
+        operands += stream["lefts"]
+    for stream in streams:
+        firsts, at = [], 0
+        tokens = stream["lefts"][0].shape[1]
+        height = stream["lefts"][0].shape[0] // n
+        loads += len(stream["lefts"])
+        for segment in stream["rights"]:
+            width = 0
+            for ticks in segment:
+                operands += ticks
+                width += ticks[0].shape[1]
+                loads += 4 * slots
+            firsts.append(at)
+            at += width // 4 // LANES
+            out_shapes.append(jax.ShapeDtypeStruct((height, width), BF16))
+            flops += 2 * tokens * height * n * width
+            moved += height * width * 4
+        z_first, blocks = stream["z_first"], stream["blocks"]
+        items = at * blocks
+        rows = height // blocks
+        pair = (2,) if z_first else ()
+        depth = min(items, n + 2)
+        tile = (rows, LANES)
+        land_y = 1 if z_first else n
+        scratch += [
+            pltpu.VMEM((len(stream["lefts"]), height * n, tokens), BF16),
+            pltpu.VMEM((4, tokens, at * LANES), BF16),
+            pltpu.VMEM((DELAY, 2) + tile, BF16),
+            pltpu.VMEM((DELAY, 2) + tile, F32),
+            pltpu.VMEM((n, 2) + tile, BF16),
+            pltpu.VMEM((DELAY,) + tile, F32),
+            pltpu.VMEM((DELAY,) + tile, BF16),
+            pltpu.VMEM((land_y,) + tile, BF16),
+            pltpu.VMEM((DELAY,) + pair + tile, BF16),
+            pltpu.VMEM((n - 1, depth) + pair + tile, BF16),
+            pltpu.VMEM((DELAY,) + tile, BF16),
+            dma((DELAY,)), dma((n,)), regular((n,)),
+            dma((DELAY,)), dma((land_y,)), regular((land_y,)),
+            dma((DELAY,)), dma((n - 1, depth)),
+            dma((DELAY,)), dma((DELAY,)), dma((DELAY,)),
+            dma((items,)), dma((items,)), dma((DELAY,)), dma((items,)),
+        ]
+        plans.append({
+            "z_first": z_first, "blocks": blocks, "pace": stream["pace"], "which": tuple(stream["which"]), "firsts": tuple(firsts),
+            "lefts": [None] * len(stream["lefts"]), "rights": [[None] * len(segment) for segment in stream["rights"]]})
+    scratch.append(dma((loads,)))
+    anywhere = pl.BlockSpec(memory_space=pl.ANY)
+    return pl.pallas_call(
+        functools.partial(reduce_kernel, plans, slots),
+        in_specs=[anywhere] * len(operands),
+        out_specs=[anywhere] * len(out_shapes),
+        out_shape=out_shapes,
+        scratch_shapes=scratch,
+        compiler_params=pltpu.CompilerParams(
+            collective_id=collective_id, has_side_effects=True, vmem_limit_bytes=60 * 1024 * 1024),
+        cost_estimate=pl.CostEstimate(flops=flops, bytes_accessed=moved, transcendentals=0),
+        name=name,
+    )(*operands)
+
+
 EPSILON = 1e-05
 ROPE_BASE = 10000.0
 
@@ -207,11 +549,6 @@
     rows = weight.shape[0] // parts
     own = lax.dynamic_slice_in_dim(weight, lax.axis_index("rep") * rows, rows, 0)
     return lax.all_gather(own, ("shard", "rep"), axis=0, tiled=True)
-
-
-def scatter_rows(term):
-    part = lax.psum_scatter(term, ("shard", "rep"), scatter_dimension=0, tiled=True)
-    return lax.all_gather(part, "rep", axis=0, tiled=True)
 
 
 def layer_forward(stream_in, weights, cos_table, sin_table):
@@ -305,25 +642,21 @@
     grad_in = jnp.stack([
         jnp.where(first, streams[slot_count - j], streams[slot_count - 1 - j]) for j in range(slot_count)])
 
-    def rows_of(pick_kept, pick_term):
-        lefts, rights = [], []
-        for j in range(slot_count):
-            f0, f1 = pick_kept(kept_all[j]), pick_kept(kept_all[j + 1])
-            lefts.append(jnp.where(first, f0, f1))
-            b0, b1 = pick_term(term_list[ticks - 1 - j]), pick_term(term_list[ticks - 2 - j])
-            rights.append(jnp.where(first, b0, b1))
-        return jnp.concatenate(lefts, axis=0), jnp.concatenate(rights, axis=0)
-
-    def weight_term(index, pick_term):
-        left, right = rows_of(lambda k: k[index], pick_term)
-        return inner_rows(left, right).astype(BF16)
-
-    down_sum = scatter_rows(weight_term(13, lambda t: t[6]))
-    ff_sum = scatter_rows(weight_term(10, lambda t: jnp.concatenate([t[4], t[5]], axis=1)))
-    out_sum = scatter_rows(weight_term(7, lambda t: t[3]))
-    qkv_sum = scatter_rows(weight_term(2, lambda t: jnp.concatenate([t[0], t[1], t[2]], axis=1)))
+    def turned(index):
+        picks = [jnp.where(first, kept_all[j][index], kept_all[j + 1][index]) for j in range(slot_count)]
+        return jnp.concatenate(picks, axis=0).T
+
+    def by_tick(index):
+        return [terms[index] for terms in term_list]
+
+    gate_sum, up_sum, qkv_sum, out_sum, down_sum = reduce_weights(
+        [
+            {"lefts": [turned(10), turned(2), turned(7)], "which": [0, 0, 1, 2], "z_first": False, "blocks": 1, "pace": 1,
+             "rights": [[by_tick(4)], [by_tick(5)], [by_tick(0), by_tick(1), by_tick(2)], [by_tick(3)]]},
+            {"lefts": [turned(13)], "which": [0], "z_first": True, "blocks": 2, "pace": 3, "rights": [[by_tick(6)]]},
+        ],
+        slot_count, 1, "reduce_weights")
     kv_width = w_key.shape[2]
-    ff_width = w_gate.shape[2]
     gain_part = lax.psum_scatter(gain_total, "shard", scatter_dimension=1, tiled=True)
     gain_sum = lax.psum(gain_part, "rep")
     outs = (
@@ -331,8 +664,8 @@
         qkv_sum[:, model_width:model_width + kv_width],
         qkv_sum[:, model_width + kv_width:],
         out_sum,
-        ff_sum[:, :ff_width],
-        ff_sum[:, ff_width:],
+        gate_sum,
+        up_sum,
         down_sum,
         gain_sum,
     )

time: 2450 us -> 1940 us (0.79)
  waiting for transfers between devices: 1620 us -> 627 us
  Pallas kernels: 153 us -> 681 us
  matrix products: 444 us -> 393 us
    reduce_scatter x4 -> x0, waiting for transfers between devices: 807 us -> none  [scatter_rows(): lax.psum_scatter(term, ('shard', 'rep'), scatter_dimension=0, tiled=True)]
    pallas_call x0 -> x1, Pallas kernels: none -> 528 us  [reduce_weights(): pl.pallas_call(functools.partial(reduce_kernel, plans, slots), in_specs=[...]
    all_gather x4 -> x0, waiting for transfers between devices: 145 us -> none  [scatter_rows(): return lax.all_gather(part, 'rep', axis=0, tiled=True)]
    dot_general x4 -> x0, matrix products: 68.1 us -> none  [inner_rows(): lax.dot_general(left_rows, right_rows, (((0,), (0,)), ((), ())), preferre...]
  transfers between devices with their start and end apart: 26 -> 18, of which waited for: 26 -> 16; matrix products, arithmetic and copies ran while one was open for 11% -> 11% of each run, Pallas kernels for 1% -> 1%
where the time goes in v2:
time: 1940 us; the launch traced here: 1930 us
  Pallas kernels  681 us (35%)
  waiting for transfers between devices  627 us (32%)
  matrix products  393 us (20%)
  other arithmetic  104 us (5%)
  local copies, waits for them, and re-layouts  78.5 us (4%)
  blocking collectives  20.7 us (1%)
    pallas_call x1, Pallas kernels, reduce_weights(): pl.pallas_call(functools.partial(reduce_kernel, plans, slots), in_specs=[...  528 us
    all_gather x7, waiting for transfers between devices, gather_rows(): return lax.all_gather(own, ('shard', 'rep'), axis=0, tiled=True)  484 us
    dot_general x21, matrix products, times_t(): lax.dot_general(left_rows, right_rows, (((1,), (1,)), ((), ())), preferre...  212 us
    dot_general x21, matrix products, mm(): return jnp.dot(a, b, preferred_element_type=F32)  180 us
    pallas_call x3, Pallas kernels, attn_bwd(): pl.pallas_call(functools.partial(attn_bwd_kernel, axis, pairs), grid=(ste...  79.3 us
    ppermute x4, waiting for transfers between devices, passed_along(): return lax.ppermute(block, axis, pairs)  74.4 us
    pallas_call x3, Pallas kernels, attn_fwd(): pl.pallas_call(functools.partial(attn_fwd_kernel, axis, pairs), grid=(ste...  73.7 us
    all_gather x3, waiting for transfers between devices, layer_forward(): lax.all_gather(jnp.concatenate([key_rows, values], axis=1), 'shard', axis...  51.8 us
  transfers between devices with their start and end apart: 18, of which 16 were waited for; matrix products, arithmetic and copies ran while one was open for 11% of the time, Pallas kernels for 1%

profile of v2, /device:TPU:0, one launch (start us, length us, event | category | flops | bytes accessed | tf_op | source)
XLA Modules:
  0.0 1930.8 jit_solution(6820759815664744115)
XLA Ops:
  10.5 13.7 all-gather
  33.7 17.8 all-gather.27.cloned.1.call-done
  54.9 36.1 %all-gather.29.cloned.1.call-done = bf16[1,2048,256]{2,1,0:T(8,128)(2,1)} async-done(((bf16[1,128,256]{2,1,0:T(8,128)(2,1)}), bf16[1,2048,256]{2,1,0:T(8,128)(2,1)}) %all-gather.29.cloned.1.call-update) | async-done | bytes 1048592 | tf_op jit(solution)/shard_map/all_gather | solution.py:551
  104.8 16.0 all-gather.19.cloned.1.call-done
  122.1 75.7 %all-gather.25.cloned.1.call-done = bf16[1,2048,2048]{2,1,0:T(8,128)(2,1)} async-done(((bf16[1,128,2048]{2,1,0:T(8,128)(2,1)}), bf16[1,2048,2048]{2,1,0:T(8,128)(2,1)}) %all-gather.25.cloned.1.call-update) | async-done | bytes 8388624 | tf_op jit(solution)/shard_map/all_gather | solution.py:551
  217.5 24.8 %attn_fwd.3 = (bf16[256,2048]{1,0:T(8,128)(2,1)S(1)}, f32[2,16,256]{2,1,0:T(8,128)S(1)}) custom-call(bf16[256,2048]{1,0:T(8,128)(2,1)S(1)} %copy.92.q_ref, bf16[1024,256]{1,0:T(8,128)(2,1)S(1)} %get-tuple-element.113.k_ref, bf16[1024,256]{1,0:T(8,128)(2,1)S(1)} %get-tuple-element.112.v_ref), custom_call_target="tpu_custom_call" | custom-call | flops 2147483648 | bytes 4194304 | tf_op jit(solution)/shard_map/attn_fwd/pallas_call | solution.py:55
  242.3 31.3 %all-gather.31.cloned.1.call-done = bf16[1,2048,2048]{2,1,0:T(8,128)(2,1)} async-done(((bf16[1,128,2048]{2,1,0:T(8,128)(2,1)}), bf16[1,2048,2048]{2,1,0:T(8,128)(2,1)}) %all-gather.31.cloned.1.call-update) | async-done | bytes 8388624 | tf_op jit(solution)/shard_map/all_gather | solution.py:551
  281.6 111.0 %all-gather.33.cloned.1.call-done = bf16[1,2048,5632]{2,1,0:T(8,128)(2,1)} async-done(((bf16[1,128,5632]{2,1,0:T(8,128)(2,1)}), bf16[1,2048,5632]{2,1,0:T(8,128)(2,1)}) %all-gather.33.cloned.1.call-update) | async-done | bytes 23068688 | tf_op jit(solution)/shard_map/all_gather | solution.py:551
  405.6 107.9 %all-gather.35.cloned.1.call-done = bf16[1,2048,5632]{2,1,0:T(8,128)(2,1)} async-done(((bf16[1,128,5632]{2,1,0:T(8,128)(2,1)}), bf16[1,2048,5632]{2,1,0:T(8,128)(2,1)}) %all-gather.35.cloned.1.call-update) | async-done | bytes 23068688 | tf_op jit(solution)/shard_map/all_gather | solution.py:551
  513.5 16.6 multiply_convert_fusion.8
  530.1 104.3 %all-gather.37.cloned.1.call-done = bf16[1,5632,2048]{2,1,0:T(8,128)(2,1)} async-done(((bf16[1,352,2048]{2,1,0:T(8,128)(2,1)}), bf16[1,5632,2048]{2,1,0:T(8,128)(2,1)}) %all-gather.37.cloned.1.call-update) | async-done | bytes 23068688 | tf_op jit(solution)/shard_map/all_gather | solution.py:551
  650.1 22.8 %collective-permute-done = bf16[256,2048]{1,0:T(8,128)(2,1)S(1)} collective-permute-done((bf16[256,2048]{1,0:T(8,128)(2,1)S(1)}, bf16[256,2048]{1,0:T(8,128)(2,1)S(1)}, u32[]{:S(2)}, u32[]{:S(2)}) %collective-permute-start) | collective-permute-done | bytes 1048608 | tf_op jit(solution)/shard_map/ppermute | solution.py:544
  688.6 19.0 all-gather.21.cloned.1.call-done
  709.0 24.6 %attn_fwd.4 = (bf16[256,2048]{1,0:T(8,128)(2,1)S(1)}, f32[2,16,256]{2,1,0:T(8,128)S(1)}) custom-call(bf16[256,2048]{1,0:T(8,128)(2,1)S(1)} %copy.96.q_ref, bf16[1024,256]{1,0:T(8,128)(2,1)S(1)} %get-tuple-element.111.k_ref, bf16[1024,256]{1,0:T(8,128)(2,1)S(1)} %get-tuple-element.110.v_ref), custom_call_target="tpu_custom_call" | custom-call | flops 2147483648 | bytes 4194304 | tf_op jit(solution)/shard_map/attn_fwd/pallas_call | solution.py:55
  742.1 13.7 fusion.32
  755.8 18.8 broadcast_select_fusion.1
  789.9 22.0 %collective-permute-done.1 = bf16[256,2048]{1,0:T(8,128)(2,1)S(1)} collective-permute-done((bf16[256,2048]{1,0:T(8,128)(2,1)S(1)}, bf16[256,2048]{1,0:T(8,128)(2,1)S(1)}, u32[]{:S(2)}, u32[]{:S(2)}) %collective-permute-start.1) | collective-permute-done | bytes 1048608 | tf_op jit(solution)/shard_map/ppermute | solution.py:544
  828.4 16.8 all-gather.23.cloned.1.call-done
  846.5 24.3 %attn_fwd.5 = (bf16[256,2048]{1,0:T(8,128)(2,1)S(1)}, f32[2,16,256]{2,1,0:T(8,128)S(1)}) custom-call(bf16[256,2048]{1,0:T(8,128)(2,1)S(1)} %copy.100.q_ref, bf16[1024,256]{1,0:T(8,128)(2,1)S(1)} %get-tuple-element.109.k_ref, bf16[1024,256]{1,0:T(8,128)(2,1)S(1)} %get-tuple-element.108.v_ref), custom_call_target="tpu_custom_call" | custom-call | flops 2147483648 | bytes 4194304 | tf_op jit(solution)/shard_map/attn_fwd/pallas_call | solution.py:55
  892.2 18.9 broadcast_select_fusion
  911.2 24.8 %multiply_convert_fusion.5 = (bf16[256,5632]{1,0:T(8,128)(2,1)}, bf16[256,5632]{1,0:T(8,128)(2,1)}) fusion(f32[256,5632]{1,0:T(8,128)} %fusion.30, f32[256,5632]{1,0:T(8,128)} %get-tuple-element.160, bf16[256,2048]{1,0:T(8,128)(2,1)S(1)} %copy-done.55, bf16[1,5632,2048]{2,1,0:T(8,128)(2,1)} %all-gather.37.cloned.1.call-done), kind=kOutput, calls=%fused_computation.67 | convolution fusion | flops 5924323328 | bytes 41418752 | tf_op jit(solution)/shard_map/dot_general | solution.py:528
  948.9 14.5 multiply_reduce_fusion.2
  975.1 26.4 %attn_bwd.3 = (f32[256,2048]{1,0:T(8,128)}, bf16[1024,256]{1,0:T(8,128)(2,1)S(1)}, bf16[1024,256]{1,0:T(8,128)(2,1)S(1)}) custom-call(bf16[256,2048]{1,0:T(8,128)(2,1)S(1)} %copy.100.q_ref, bf16[1024,256]{1,0:T(8,128)(2,1)S(1)} %copy-done.18, bf16[1024,256]{1,0:T(8,128)(2,1)S(1)} %copy-done.16, bf16[256,2048]{1,0:T(8,128)(2,1)} %copy-done.6, ...), custom_call_target="tpu_custom_call" | custom-call | flops 5368709120 | bytes 6291456 | tf_op jit(solution)/shard_map/attn_bwd/pallas_call | solution.py:137
  1049.8 16.5 collective-permute-done.2
  1068.0 25.2 %multiply_convert_fusion.3 = (bf16[256,5632]{1,0:T(8,128)(2,1)}, bf16[256,5632]{1,0:T(8,128)(2,1)}) fusion(f32[256,5632]{1,0:T(8,128)} %fusion.32, f32[256,5632]{1,0:T(8,128)} %get-tuple-element.157, bf16[256,2048]{1,0:T(8,128)(2,1)S(1)} %fusion.144.refs_23_, bf16[1,5632,2048]{2,1,0:T(8,128)(2,1)} %all-gather.37.cloned.1.call-done), kind=kOutput, calls=%fused_computation.65 | convolution fusion | flops 5924323328 | bytes 41418752 | tf_op jit(solution)/shard_map/dot_general | solution.py:528
  1105.7 14.5 multiply_reduce_fusion.1
  1131.8 26.4 %attn_bwd.4 = (f32[256,2048]{1,0:T(8,128)}, bf16[1024,256]{1,0:T(8,128)(2,1)S(1)}, bf16[1024,256]{1,0:T(8,128)(2,1)S(1)}) custom-call(bf16[256,2048]{1,0:T(8,128)(2,1)S(1)} %copy.96.q_ref, bf16[1024,256]{1,0:T(8,128)(2,1)S(1)} %copy-done.14, bf16[1024,256]{1,0:T(8,128)(2,1)S(1)} %copy-done.12, bf16[256,2048]{1,0:T(8,128)(2,1)} %copy-done.4, ...), custom_call_target="tpu_custom_call" | custom-call | flops 5368709120 | bytes 6291456 | tf_op jit(solution)/shard_map/attn_bwd/pallas_call | solution.py:137
  1159.3 13.7 fusion.109
  1222.2 25.1 %multiply_convert_fusion.1 = (bf16[256,5632]{1,0:T(8,128)(2,1)}, bf16[256,5632]{1,0:T(8,128)(2,1)}) fusion(f32[256,5632]{1,0:T(8,128)} %fusion.34, f32[256,5632]{1,0:T(8,128)} %get-tuple-element.154, bf16[256,2048]{1,0:T(8,128)(2,1)S(1)} %broadcast_select_fusion.8.refs_24_, bf16[1,5632,2048]{2,1,0:T(8,128)(2,1)} %all-gather.37.cloned.1.call-done), kind=kOutput, calls=%fused_computation.63 | convolution fusion | flops 5924323328 | bytes 41418752 | tf_op jit(solution)/shard_map/dot_general | solution.py:528
  1259.9 13.9 multiply_reduce_fusion
  1285.5 26.5 %attn_bwd.5 = (f32[256,2048]{1,0:T(8,128)}, bf16[1024,256]{1,0:T(8,128)(2,1)S(1)}, bf16[1024,256]{1,0:T(8,128)(2,1)S(1)}) custom-call(bf16[256,2048]{1,0:T(8,128)(2,1)S(1)} %copy.92.q_ref, bf16[1024,256]{1,0:T(8,128)(2,1)S(1)} %copy-done.10, bf16[1024,256]{1,0:T(8,128)(2,1)S(1)} %copy-done.8, bf16[256,2048]{1,0:T(8,128)(2,1)} %copy-done.2, ...), custom_call_target="tpu_custom_call" | custom-call | flops 5368709120 | bytes 6291456 | tf_op jit(solution)/shard_map/attn_bwd/pallas_call | solution.py:137
  1352.4 527.6 %reduce_weights.1 = (bf16[512,5632]{1,0:T(8,128)(2,1)}, bf16[512,5632]{1,0:T(8,128)(2,1)}, bf16[512,2560]{1,0:T(8,128)(2,1)}, bf16[512,2048]{1,0:T(8,128)(2,1)}, bf16[1408,2048]{1,0:T(8,128)(2,1)}) custom-call(bf16[2048,512]{1,0:T(8,128)(2,1)} %copy.110.refs_0_, bf16[2048,512]{1,0:T(8,128)(2,1)} %copy.111.refs_1_, bf16[2048,512]{1,0:T(8,128)(2,1)} %copy.112.refs_2_, ...), custom_call_target="tpu_custom_call" | custom-call | flops 45097156608 | bytes 44040192 | tf_op jit(solution)/shard_map/reduce_weights/pallas_call | solution.py:485
  (374 shorter events, 423.4 us)
Async XLA Ops:
  7.2 86.7 %copy-start = (bf16[1,512,2048]{2,1,0:T(8,128)(2,1)S(1)}, bf16[1,512,2048]{2,1,0:T(8,128)(2,1)}, u32[]{:S(2)}) copy-start(bf16[1,512,2048]{2,1,0:T(8,128)(2,1)} %param.14) | copy-start | bytes 6291460
  7.2 44.2 %all-gather.27.cloned.1.call-start = ((), (), s32[]{:S(2)}) async-start(), calls=%async_computation.11 | async-start | bytes 1114112 | tf_op jit(solution)/shard_map/all_gather | solution.py:551
  8.9 82.2 %all-gather.29.cloned.1.call-start = ((), (), s32[]{:S(2)}) async-start(), calls=%async_computation.12 | async-start | bytes 1114112 | tf_op jit(solution)/shard_map/all_gather | solution.py:551
  10.4 110.4 %all-gather.19.cloned.1.call-start = ((), (), s32[]{:S(2)}) async-start(), calls=%async_computation.4 | async-start | bytes 1310720 | tf_op jit(solution)/shard_map/all_gather | solution.py:563
  32.8 177.3 %copy-start.73 = (f32[256]{0:T(256)}, f32[256]{0:T(256)S(1)}, u32[]{:S(2)}) copy-start(f32[256]{0:T(256)S(1)} %get-tuple-element.138) | copy-start | bytes 3076
  93.9 104.0 %all-gather.25.cloned.1.call-start = ((), (), s32[]{:S(2)}) async-start(), calls=%async_computation.10 | async-start | bytes 8912896 | tf_op jit(solution)/shard_map/all_gather | solution.py:551
  94.8 178.8 %all-gather.31.cloned.1.call-start = ((), (), s32[]{:S(2)}) async-start(), calls=%async_computation.13 | async-start | bytes 8912896 | tf_op jit(solution)/shard_map/all_gather | solution.py:551
  96.8 295.9 %all-gather.33.cloned.1.call-start = ((), (), s32[]{:S(2)}) async-start(), calls=%async_computation.14 | async-start | bytes 24510464 | tf_op jit(solution)/shard_map/all_gather | solution.py:551
  99.4 414.2 %all-gather.35.cloned.1.call-start = ((), (), s32[]{:S(2)}) async-start(), calls=%async_computation.15 | async-start | bytes 24510464 | tf_op jit(solution)/shard_map/all_gather | solution.py:551
  102.1 532.4 %all-gather.37.cloned.1.call-start = ((), (), s32[]{:S(2)}) async-start(), calls=%async_computation.16 | async-start | bytes 24510464 | tf_op jit(solution)/shard_map/all_gather | solution.py:551
  104.8 602.9 %all-gather.21.cloned.1.call-start = ((), (), s32[]{:S(2)}) async-start(), calls=%async_computation.5 | async-start | bytes 1310720 | tf_op jit(solution)/shard_map/all_gather | solution.py:563
  122.1 95.3 %copy-start.7 = (bf16[1024,256]{1,0:T(8,128)(2,1)}, bf16[1024,256]{1,0:T(8,128)(2,1)S(1)}, u32[]{:S(2)}) copy-start(bf16[1024,256]{1,0:T(8,128)(2,1)S(1)} %get-tuple-element.112.v_ref) | copy-start | bytes 1572868
  122.1 95.3 %copy-start.9 = (bf16[1024,256]{1,0:T(8,128)(2,1)}, bf16[1024,256]{1,0:T(8,128)(2,1)S(1)}, u32[]{:S(2)}) copy-start(bf16[1024,256]{1,0:T(8,128)(2,1)S(1)} %get-tuple-element.113.k_ref) | copy-start | bytes 1572868
  242.3 38.7 %copy-start.2 = (bf16[256,2048]{1,0:T(8,128)(2,1)}, bf16[256,2048]{1,0:T(8,128)(2,1)S(1)}, u32[]{:S(2)}) copy-start(bf16[256,2048]{1,0:T(8,128)(2,1)S(1)} %get-tuple-element.30.o_ref) | copy-start | bytes 3145732
  281.6 231.9 %copy-start.76 = (f32[256]{0:T(256)}, f32[256]{0:T(256)S(1)}, u32[]{:S(2)}) copy-start(f32[256]{0:T(256)S(1)} %get-tuple-element.140) | copy-start | bytes 3076
  646.5 29.4 %copy-start.57 = (bf16[256,2048]{1,0:T(8,128)(2,1)}, bf16[256,2048]{1,0:T(8,128)(2,1)S(1)}, u32[]{:S(2)}) copy-start(bf16[256,2048]{1,0:T(8,128)(2,1)S(1)} %fusion.94) | copy-start | bytes 3145732
  646.5 28.7 %copy-start.22 = (bf16[1,2048,256]{2,1,0:T(8,128)(2,1)S(1)}, bf16[1,2048,256]{2,1,0:T(8,128)(2,1)}, u32[]{:S(2)}) copy-start(bf16[1,2048,256]{2,1,0:T(8,128)(2,1)} %all-gather.27.cloned.1.call-done) | copy-start | bytes 3145732
  646.5 26.3 %collective-permute-start = (bf16[256,2048]{1,0:T(8,128)(2,1)S(1)}, bf16[256,2048]{1,0:T(8,128)(2,1)S(1)}, u32[]{:S(2)}, u32[]{:S(2)}) collective-permute-start(bf16[256,2048]{1,0:T(8,128)(2,1)S(1)} %fusion.94), channel_id=1, source_target_pairs={{0,16},{1,17},{2,18},{3,19},{4,20},{5,21},{6,22},{7,23},{8,24},{9,... | collective-permute-start | bytes 3145736 | tf_op jit(solution)/shard_map/ppermute | solution.py:544
  674.6 59.0 %copy-start.26 = (bf16[256,2048]{1,0:T(8,128)(2,1)}, bf16[256,2048]{1,0:T(8,128)(2,1)S(1)}, u32[]{:S(2)}) copy-start(bf16[256,2048]{1,0:T(8,128)(2,1)S(1)} %get-tuple-element.81) | copy-start | bytes 3145732
  678.6 166.6 %all-gather.23.cloned.1.call-start = ((), (), s32[]{:S(2)}) async-start(), calls=%async_computation.6 | async-start | bytes 1310720 | tf_op jit(solution)/shard_map/all_gather | solution.py:563
  739.9 34.7 %copy-start.30 = (f32[256,2048]{1,0:T(8,128)}, f32[256,2048]{1,0:T(8,128)S(1)}, u32[]{:S(2)}) copy-start(f32[256,2048]{1,0:T(8,128)S(1)} %get-tuple-element.156) | copy-start | bytes 6291460
  774.6 38.3 %copy-start.23 = (bf16[1,2048,256]{2,1,0:T(8,128)(2,1)S(1)}, bf16[1,2048,256]{2,1,0:T(8,128)(2,1)}, u32[]{:S(2)}) copy-start(bf16[1,2048,256]{2,1,0:T(8,128)(2,1)} %all-gather.27.cloned.1.call-done) | copy-start | bytes 3145732
  786.3 27.4 %copy-start.59 = (bf16[256,2048]{1,0:T(8,128)(2,1)}, bf16[256,2048]{1,0:T(8,128)(2,1)S(1)}, u32[]{:S(2)}) copy-start(bf16[256,2048]{1,0:T(8,128)(2,1)S(1)} %fusion.91) | copy-start | bytes 3145732
  786.3 25.6 %collective-permute-start.1 = (bf16[256,2048]{1,0:T(8,128)(2,1)S(1)}, bf16[256,2048]{1,0:T(8,128)(2,1)S(1)}, u32[]{:S(2)}, u32[]{:S(2)}) collective-permute-start(bf16[256,2048]{1,0:T(8,128)(2,1)S(1)} %fusion.91), channel_id=1, source_target_pairs={{0,16},{1,17},{2,18},{3,19},{4,20},{5,21},{6,22},{7,23},{8,24},{9,... | collective-permute-start | bytes 3145736 | tf_op jit(solution)/shard_map/ppermute | solution.py:544
  816.3 213.2 %reduce-scatter.7.cloned.1.call-start = ((), (), s32[]{:S(2)}) async-start(), calls=%async_computation.7 | async-start | bytes 1310720 | tf_op jit(solution)/shard_map/reduce_scatter | solution.py:596
  1002.7 184.2 %reduce-scatter.9.cloned.1.call-start = ((), (), s32[]{:S(2)}) async-start(), calls=%async_computation.8 | async-start | bytes 1310720 | tf_op jit(solution)/shard_map/reduce_scatter | solution.py:596
  1039.3 27.1 %collective-permute-start.2 = (bf16[256,2048]{1,0:T(8,128)(2,1)}, bf16[256,2048]{1,0:T(8,128)(2,1)}, u32[]{:S(2)}, u32[]{:S(2)}) collective-permute-start(bf16[256,2048]{1,0:T(8,128)(2,1)} %get-tuple-element.76), channel_id=1, source_target_pairs={{16,0},{17,1},{18,2},{19,3},{20,4},{21,5},{22,6},{23,7},{24,8},{25... | collective-permute-start | bytes 3145736 | tf_op jit(solution)/shard_map/ppermute | solution.py:544
  1068.0 25.2 %copy-start.47 = (bf16[256,2048]{1,0:T(8,128)(2,1)}, bf16[256,2048]{1,0:T(8,128)(2,1)S(1)}, u32[]{:S(2)}) copy-start(bf16[256,2048]{1,0:T(8,128)(2,1)S(1)} %fusion.144.refs_23_) | copy-start | bytes 3145732
  1159.3 184.7 %reduce-scatter.11.cloned.1.call-start = ((), (), s32[]{:S(2)}) async-start(), calls=%async_computation.9 | async-start | bytes 1310720 | tf_op jit(solution)/shard_map/reduce_scatter | solution.py:596
  1194.9 26.0 %collective-permute-start.3 = (bf16[256,2048]{1,0:T(8,128)(2,1)}, bf16[256,2048]{1,0:T(8,128)(2,1)}, u32[]{:S(2)}, u32[]{:S(2)}) collective-permute-start(bf16[256,2048]{1,0:T(8,128)(2,1)} %get-tuple-element.72), channel_id=1, source_target_pairs={{16,0},{17,1},{18,2},{19,3},{20,4},{21,5},{22,6},{23,7},{24,8},{25... | collective-permute-start | bytes 3145736 | tf_op jit(solution)/shard_map/ppermute | solution.py:544
  1222.2 25.1 %copy-start.56 = (bf16[256,2048]{1,0:T(8,128)(2,1)}, bf16[256,2048]{1,0:T(8,128)(2,1)S(1)}, u32[]{:S(2)}) copy-start(bf16[256,2048]{1,0:T(8,128)(2,1)S(1)} %broadcast_select_fusion.8.refs_24_) | copy-start | bytes 3145732
  1313.0 603.0 %reduce-scatter.13.cloned.1.call-start = ((), (), s32[]{:S(2)}) async-start(), calls=%async_computation.17 | async-start | bytes 1310720
  (80 other events, 570.6 us)
Sparse Core Ops, SparseCore 0:
  10.8 40.6 all-gather.26
  54.2 36.8 all-gather.28
  94.0 26.8 all-gather.18
  123.4 74.3 all-gather.24
  200.4 73.1 all-gather.30
  275.6 116.9 all-gather.32
  394.8 118.6 all-gather.34
  515.7 118.6 all-gather.36
  678.7 28.9 all-gather.20
  816.4 28.7 all-gather.22
  1002.8 26.6 reduce-scatter.6
  1159.4 25.0 reduce-scatter.8
  1313.1 25.3 reduce-scatter.10
  1890.3 25.6 reduce-scatter.12

commit v3 on v2

--- a/solution.py
+++ b/solution.py
@@ -495,6 +495,122 @@
     )(*operands)
 
 
+def gather_kernel(splits, *refs):
+    n = lax.axis_size("shard")
+    me = lax.axis_index("shard")
+    rep = lax.axis_index("rep")
+    right = {"shard": lax.rem(me + 1, n)}
+    left = {"shard": lax.rem(me + n - 1, n)}
+    core_peer = {"rep": rep + 1 - 2 * lax.rem(rep, 2)}
+    y_rep = rep + 2 - 4 * (rep // 2)
+    y_peer = {"rep": y_rep}
+    count = len(splits)
+    ins, outs = refs[:count], refs[count:2 * count]
+    holds = refs[2 * count:3 * count]
+    zs, zr, ys, yr, cs, cr, ts, tr, local = refs[3 * count:]
+
+    barrier = pltpu.get_barrier_semaphore()
+    for peer in (left, right, core_peer, y_peer):
+        pl.semaphore_signal(barrier, inc=1, device_id=peer, device_id_type=MESH_IDS)
+
+    pieces = []
+    for k, split in enumerate(splits):
+        at = 0
+        for width in split:
+            pieces.append((k, at, width))
+            at += width
+
+    def own_load(k):
+        return pltpu.make_async_copy(ins[k], holds[k], local.at[0, k])
+
+    def own_store(k):
+        rows = ins[k].shape[0]
+        return pltpu.make_async_copy(holds[k], outs[k].at[pl.ds(pl.multiple_of(me * rows, 16), rows), :], local.at[1, k])
+
+    def spot(piece, back, r):
+        k, at, width = pieces[piece]
+        rows = ins[k].shape[0]
+        block = lax.rem(me + n - back, n)
+        column = pl.multiple_of(r * (ins[k].shape[1] // 4) + at, LANES)
+        return outs[k].at[pl.ds(pl.multiple_of(block * rows, 16), rows), pl.ds(column, width)]
+
+    def z_copy(piece, s):
+        k, at, width = pieces[piece]
+        there = spot(piece, s, rep)
+        column = pl.multiple_of(rep * (ins[k].shape[1] // 4) + at, LANES)
+        here = ins[k].at[:, pl.ds(column, width)] if s == 0 else there
+        return remote(here, there, zs.at[piece, s], zr.at[piece, s], right)
+
+    def y_copy(piece, s):
+        there = spot(piece, s, rep)
+        return remote(there, there, ys.at[piece, s - 1], yr.at[piece, s - 1], y_peer)
+
+    def c_copy(piece, s):
+        there = spot(piece, s, rep)
+        return remote(there, there, cs.at[piece, s - 1], cr.at[piece, s - 1], core_peer)
+
+    def t_copy(piece, s):
+        there = spot(piece, s, y_rep)
+        return remote(there, there, ts.at[piece, s - 1], tr.at[piece, s - 1], core_peer)
+
+    def turn(piece, s):
+        y_copy(piece, s).wait_recv()
+        t_copy(piece, s).start()
+
+    pl.semaphore_wait(barrier, 4)
+    for piece in range(len(pieces)):
+        z_copy(piece, 0).start()
+    for k in range(count):
+        own_load(k).start()
+    for k in range(count):
+        own_load(k).wait()
+        own_store(k).start()
+    before = []
+    for s in range(1, n):
+        for piece in range(len(pieces)):
+            z_copy(piece, s - 1).wait_recv()
+            if s < n - 1:
+                z_copy(piece, s).start()
+            y_copy(piece, s).start()
+            c_copy(piece, s).start()
+            before.append((piece, s))
+            if len(before) > 1:
+                turn(*before[-2])
+    turn(*before[-1])
+    for k in range(count):
+        own_store(k).wait()
+    for piece, s in before:
+        z_copy(piece, s - 1).wait_send()
+        y_copy(piece, s).wait_send()
+        c_copy(piece, s).wait()
+        t_copy(piece, s).wait()
+
+
+def gather_weights(shards, splits, collective_id, name):
+    n = lax.axis_size("shard")
+    dma = pltpu.SemaphoreType.DMA
+    pieces = sum(len(split) for split in splits)
+    pair = dma((pieces, n - 1))
+    anywhere = pl.BlockSpec(memory_space=pl.ANY)
+    moved = 2 * n * sum(shard.shape[0] * shard.shape[1] for shard in shards)
+    return pl.pallas_call(
+        functools.partial(gather_kernel, splits),
+        in_specs=[anywhere] * len(shards),
+        out_specs=[anywhere] * len(shards),
+        out_shape=[jax.ShapeDtypeStruct((n * shard.shape[0], shard.shape[1]), BF16) for shard in shards],
+        scratch_shapes=[pltpu.VMEM(shard.shape, BF16) for shard in shards] + [pair] * 8 + [dma((2, len(shards)))],
+        compiler_params=pltpu.CompilerParams(collective_id=collective_id, has_side_effects=True, vmem_limit_bytes=40 * 1024 * 1024),
+        cost_estimate=pl.CostEstimate(flops=0, bytes_accessed=moved * 4, transcendentals=0),
+        name=name,
+    )(*shards)
+
+
+def halves(width):
+    quarter = width // 4
+    first = (quarter // LANES + 1) // 2 * LANES
+    return (first, quarter - first) if quarter > first else (quarter,)
+
+
 EPSILON = 1e-05
 ROPE_BASE = 10000.0
 
@@ -552,15 +668,16 @@
 
 
 def layer_forward(stream_in, weights, cos_table, sin_table):
-    w_q, w_k, w_v, w_o, w_g, w_u, w_d, gains_wide = weights
+    w_q, w_kv, w_o, w_g, w_u, w_d, gains_wide = weights
     span_len, model_width = stream_in.shape
     stream = stream_in.astype(F32)
     inv_one = lax.rsqrt(jnp.mean(stream * stream, axis=-1, keepdims=True) + EPSILON)
     normed = (stream * inv_one * gains_wide[0]).astype(BF16)
-    key_rows = rotate(mm(normed, w_k), cos_table, sin_table).astype(BF16)
-    values = mm(normed, w_v).astype(BF16)
-    kv_width = values.shape[1]
-    kv_all = lax.all_gather(jnp.concatenate([key_rows, values], axis=1), "shard", axis=0, tiled=True)
+    kv_rows = mm(normed, w_kv)
+    kv_width = kv_rows.shape[1] // 2
+    kv_rows = jnp.concatenate(
+        [rotate(kv_rows[:, :kv_width], cos_table, sin_table).astype(BF16), kv_rows[:, kv_width:].astype(BF16)], axis=1)
+    kv_all = lax.all_gather(kv_rows, "shard", axis=0, tiled=True)
     key_all, value_all = kv_all[:, :kv_width], kv_all[:, kv_width:]
     queries = rotate(mm(normed, w_q), cos_table, sin_table).astype(BF16)
     attended, log_total = attn_fwd(queries, key_all, value_all, "shard")
@@ -577,7 +694,7 @@
 
 
 def layer_backward(grad_bf, kept, weights, cos_table, sin_table):
-    w_q, w_k, w_v, w_o, w_g, w_u, w_d, gains_wide = weights
+    w_q, w_kv, w_o, w_g, w_u, w_d, gains_wide = weights
     (stream, inv_one, normed, queries, key_all, value_all, log_total, attended, middle, inv_two,
      normed_two, gate_proj, upward, hidden) = kept
     grad_out = grad_bf.astype(F32)
@@ -598,10 +715,11 @@
     grad_query = rotate(grad_q_rot, cos_table, -sin_table).astype(BF16)
     grad_key = rotate(kv_sum[:, :kv_width], cos_table, -sin_table).astype(BF16)
     grad_value = kv_sum[:, kv_width:].astype(BF16)
-    grad_normed = times_t(grad_query, w_q) + times_t(grad_key, w_k) + times_t(grad_value, w_v)
+    grad_kv = jnp.concatenate([grad_key, grad_value], axis=1)
+    grad_normed = times_t(grad_query, w_q) + times_t(grad_kv, w_kv)
     grad_stream = grad_middle + norm_back(grad_normed, stream, inv_one, gains_wide[0])
     gain_one = jnp.sum(grad_normed * stream * inv_one, axis=0)
-    terms = (grad_query, grad_key, grad_value, grad_branch, grad_gate, grad_up, grad_bf)
+    terms = (grad_query, grad_kv, grad_kv, grad_branch, grad_gate, grad_up, grad_bf)
     return grad_stream, terms, jnp.stack([gain_one, gain_two])
 
 
@@ -611,9 +729,14 @@
     query_pos = lax.axis_index("shard") * span_len + jnp.arange(span_len, dtype=jnp.int32)
     cos_table, sin_table = angles_for(query_pos)
     live_mask = (jnp.arange(slot_count) < live_counts[0]).astype(F32)
-    gains_wide = lax.all_gather(norm_gains[0], "shard", axis=1, tiled=True).astype(F32)
-    weights = tuple(gather_rows(w[0]) for w in (w_query, w_key, w_value, w_out, w_gate, w_up, w_down))
-    weights = weights + (gains_wide,)
+    gain_rows = jnp.pad(norm_gains[0], ((0, 14), (0, -norm_gains.shape[2] % (4 * LANES))))
+    shards = [w_query[0], jnp.concatenate([w_key[0], w_value[0]], axis=1), w_out[0], gain_rows, w_gate[0], w_up[0]]
+    w_q, w_kv, w_o, gains, w_g, w_u = gather_weights(shards, [halves(shard.shape[1]) for shard in shards], 2, "gather_weights")
+    down_shard, w_q = lax.optimization_barrier((w_down[0], w_q))
+    w_d = gather_rows(down_shard)
+    gain_blocks = gains.reshape(-1, 16, gain_rows.shape[1])[:, :2, :norm_gains.shape[2]]
+    gains_wide = gain_blocks.transpose(1, 0, 2).reshape(2, model_width).astype(F32)
+    weights = (w_q, w_kv, w_o, w_g, w_u, w_d, gains_wide)
     masked_in = (tokens.astype(F32) * live_mask[:, None, None]).astype(BF16)
     masked_cot = (cotangent.astype(F32) * live_mask[:, None, None]).astype(BF16)
     zero_slot = jnp.zeros((span_len, model_width), BF16)
@@ -652,7 +775,7 @@
     gate_sum, up_sum, qkv_sum, out_sum, down_sum = reduce_weights(
         [
             {"lefts": [turned(10), turned(2), turned(7)], "which": [0, 0, 1, 2], "z_first": False, "blocks": 1, "pace": 1,
-             "rights": [[by_tick(4)], [by_tick(5)], [by_tick(0), by_tick(1), by_tick(2)], [by_tick(3)]]},
+             "rights": [[by_tick(4)], [by_tick(5)], [by_tick(0), by_tick(1)], [by_tick(3)]]},
             {"lefts": [turned(13)], "which": [0], "z_first": True, "blocks": 2, "pace": 3, "rights": [[by_tick(6)]]},
         ],
         slot_count, 1, "reduce_weights")

time: 1940 us -> 1800 us (0.928)
  waiting for transfers between devices: 627 us -> 197 us
  Pallas kernels: 681 us -> 972 us
    all_gather x7 -> x1, waiting for transfers between devices: 484 us -> 54.5 us  [gather_rows(): return lax.all_gather(own, ('shard', 'rep'), axis=0, tiled=True)]
    pallas_call x0 -> x1, Pallas kernels: none -> 292 us  [gather_weights(): pl.pallas_call(functools.partial(gather_kernel, splits), in_specs=[anywhe...]
    dot_general x21 -> x18, matrix products: 180 us -> 177 us  [mm(): return jnp.dot(a, b, preferred_element_type=F32)]
    dot_general x21 -> x18, matrix products: 212 us -> 210 us  [times_t(): lax.dot_general(left_rows, right_rows, (((1,), (1,)), ((), ())), preferre...]
  transfers between devices with their start and end apart: 18 -> 12, of which waited for: 16 -> 10; matrix products, arithmetic and copies ran while one was open for 11% -> 11% of each run, Pallas kernels for 1% -> 1%
where the time goes in v3:
time: 1800 us; the launch traced here: 1790 us
  Pallas kernels  972 us (54%)
  matrix products  387 us (22%)
  waiting for transfers between devices  197 us (11%)
  other arithmetic  116 us (6%)
  local copies, waits for them, and re-layouts  82.3 us (5%)
    pallas_call x1, Pallas kernels, reduce_weights(): pl.pallas_call(functools.partial(reduce_kernel, plans, slots), in_specs=[...  527 us
    pallas_call x1, Pallas kernels, gather_weights(): pl.pallas_call(functools.partial(gather_kernel, splits), in_specs=[anywhe...  292 us
    dot_general x18, matrix products, times_t(): lax.dot_general(left_rows, right_rows, (((1,), (1,)), ((), ())), preferre...  210 us
    dot_general x18, matrix products, mm(): return jnp.dot(a, b, preferred_element_type=F32)  177 us
    pallas_call x3, Pallas kernels, attn_bwd(): pl.pallas_call(functools.partial(attn_bwd_kernel, axis, pairs), grid=(ste...  79.9 us
    ppermute x4, waiting for transfers between devices, passed_along(): return lax.ppermute(block, axis, pairs)  77.4 us
    pallas_call x3, Pallas kernels, attn_fwd(): pl.pallas_call(functools.partial(attn_fwd_kernel, axis, pairs), grid=(ste...  73.4 us
    all_gather x1, waiting for transfers between devices, gather_rows(): return lax.all_gather(own, ('shard', 'rep'), axis=0, tiled=True)  54.5 us
  transfers between devices with their start and end apart: 12, of which 10 were waited for; matrix products, arithmetic and copies ran while one was open for 11% of the time, Pallas kernels for 1%

profile of v3, /device:TPU:0, one launch (start us, length us, event | category | flops | bytes accessed | tf_op | source)
XLA Modules:
  0.0 1789.3 jit_solution(3937141619246508886)
XLA Ops:
  14.8 291.7 %gather_weights.1 = (bf16[2048,2048]{1,0:T(8,128)(2,1)}, bf16[2048,512]{1,0:T(8,128)(2,1)S(1)}, bf16[2048,2048]{1,0:T(8,128)(2,1)}, bf16[64,512]{1,0:T(8,128)(2,...) custom-call(bf16[512,2048]{1,0:T(8,128)(2,1)S(1)} %bitcast.213, ...), custom_call_target="tpu_custom_call" | custom-call | bytes 260308992 | tf_op jit(solution)/shard_map/gather_weights/pallas_call | solution.py:596
  343.1 24.8 %attn_fwd.3 = (bf16[256,2048]{1,0:T(8,128)(2,1)S(1)}, f32[2,16,256]{2,1,0:T(8,128)S(1)}) custom-call(bf16[256,2048]{1,0:T(8,128)(2,1)S(1)} %copy.77.q_ref, bf16[1024,256]{1,0:T(8,128)(2,1)S(1)} %get-tuple-element.129.k_ref, bf16[1024,256]{1,0:T(8,128)(2,1)S(1)} %get-tuple-element.128.v_ref), custom_call_target="tpu_custom_call" | custom-call | flops 2147483648 | bytes 4194304 | tf_op jit(solution)/shard_map/attn_fwd/pallas_call | solution.py:55
  374.9 13.9 fusion.74
  388.8 18.9 %multiply_convert_fusion.8 = (bf16[256,5632]{1,0:T(8,128)(2,1)}, f32[256,5632]{1,0:T(8,128)}) fusion(f32[256,5632]{1,0:T(8,128)} %fusion.74, bf16[2048,5632]{1,0:T(8,128)(2,1)} %get-tuple-element.45, f32[256,2048]{1,0:T(8,128)S(1)} %get-tuple-element.168, f32[2048]{0:T(1024)S(1)} %bitcast.252, f32[256]{0:T(256)S(1)} %get-tuple-element.156), kind=kOutput, calls=%fused_computation.14 | convolution fusion | flops 5915803648 | bytes 39592960 | tf_op jit(solution)/shard_map/dot_general | solution.py:18
  407.8 54.5 %all-gather.7.cloned.1.call-done = bf16[5632,2048]{1,0:T(8,128)(2,1)} async-done(((bf16[352,2048]{1,0:T(8,128)(2,1)}), bf16[5632,2048]{1,0:T(8,128)(2,1)}) %all-gather.7.cloned.1.call-update) | async-done | bytes 23068688 | tf_op jit(solution)/shard_map/all_gather | solution.py:667
  477.9 22.8 %collective-permute-done = bf16[256,2048]{1,0:T(8,128)(2,1)S(1)} collective-permute-done((bf16[256,2048]{1,0:T(8,128)(2,1)S(1)}, bf16[256,2048]{1,0:T(8,128)(2,1)S(1)}, u32[]{:S(2)}, u32[]{:S(2)}) %collective-permute-start) | collective-permute-done | bytes 1048608 | tf_op jit(solution)/shard_map/ppermute | solution.py:660
  518.2 17.8 all-gather.9.cloned.1.call-done
  537.5 24.3 %attn_fwd.4 = (bf16[256,2048]{1,0:T(8,128)(2,1)S(1)}, f32[2,16,256]{2,1,0:T(8,128)S(1)}) custom-call(bf16[256,2048]{1,0:T(8,128)(2,1)S(1)} %copy-done.3, bf16[1024,256]{1,0:T(8,128)(2,1)S(1)} %get-tuple-element.127.k_ref, bf16[1024,256]{1,0:T(8,128)(2,1)S(1)} %get-tuple-element.126.v_ref), custom_call_target="tpu_custom_call" | custom-call | flops 2147483648 | bytes 4194304 | tf_op jit(solution)/shard_map/attn_fwd/pallas_call | solution.py:55
  570.3 13.6 fusion.75
  583.9 19.3 %broadcast_select_fusion.1 = (bf16[256,5632]{1,0:T(8,128)(2,1)}, bf16[256,5632]{1,0:T(8,128)(2,1)}, f32[256,5632]{1,0:T(8,128)}) fusion(bf16[256,5632]{1,0:T(8,128)(2,1)} %get-tuple-element.169, pred[]{:T(512)S(6)} %eq.2, f32[256,5632]{1,0:T(8,128)} %fusion.75, bf16[256,2048]{1,0:T(8,128)(2,1)S(1)} %get-tuple-element.83, ...), kind=kOutput, calls=%fused_computation.32 | convolution fusion | flops 5915672576 | bytes 44302336 | tf_op jit(solution)/shard_map/dot_general | solution.py:18
  618.2 21.8 %collective-permute-done.1 = bf16[256,2048]{1,0:T(8,128)(2,1)S(1)} collective-permute-done((bf16[256,2048]{1,0:T(8,128)(2,1)S(1)}, bf16[256,2048]{1,0:T(8,128)(2,1)S(1)}, u32[]{:S(2)}, u32[]{:S(2)}) %collective-permute-start.1) | collective-permute-done | bytes 1048608 | tf_op jit(solution)/shard_map/ppermute | solution.py:660
  659.0 15.9 all-gather.11.cloned.1.call-done
  676.5 24.3 %attn_fwd.5 = (bf16[256,2048]{1,0:T(8,128)(2,1)S(1)}, f32[2,16,256]{2,1,0:T(8,128)S(1)}) custom-call(bf16[256,2048]{1,0:T(8,128)(2,1)S(1)} %copy-done.5, bf16[1024,256]{1,0:T(8,128)(2,1)S(1)} %get-tuple-element.125.k_ref, bf16[1024,256]{1,0:T(8,128)(2,1)S(1)} %get-tuple-element.124.v_ref), custom_call_target="tpu_custom_call" | custom-call | flops 2147483648 | bytes 4194304 | tf_op jit(solution)/shard_map/attn_fwd/pallas_call | solution.py:55
  708.7 13.3 fusion.76
  722.1 19.3 %broadcast_select_fusion = (bf16[256,5632]{1,0:T(8,128)(2,1)}, bf16[256,5632]{1,0:T(8,128)(2,1)}, f32[256,5632]{1,0:T(8,128)}) fusion(bf16[256,5632]{1,0:T(8,128)(2,1)} %get-tuple-element.79, pred[]{:T(512)S(6)} %eq.2, f32[256,5632]{1,0:T(8,128)} %fusion.76, bf16[256,2048]{1,0:T(8,128)(2,1)S(1)} %get-tuple-element.85, bf16[2048,5632]{1,0:T(8,128)(2,1)} %get-tuple-element.45), kind=kOutput, calls=%fused_computation.31 | convolution fusion | flops 5915672576 | bytes 44302336 | tf_op jit(solution)/shard_map/dot_general | solution.py:18
  741.4 24.7 %multiply_convert_fusion.4 = (bf16[256,5632]{1,0:T(8,128)(2,1)}, bf16[256,5632]{1,0:T(8,128)(2,1)}) fusion(f32[256,5632]{1,0:T(8,128)} %fusion.76, f32[256,5632]{1,0:T(8,128)} %get-tuple-element.176, bf16[256,2048]{1,0:T(8,128)(2,1)S(1)} %copy-done.56, bf16[5632,2048]{1,0:T(8,128)(2,1)} %all-gather.7.cloned.1.call-done), kind=kOutput, calls=%fused_computation.8 | convolution fusion | flops 5924323328 | bytes 41418752 | tf_op jit(solution)/shard_map/dot_general | solution.py:644
  766.1 12.8 fusion.77
  778.9 14.7 multiply_reduce_fusion.2
  805.2 26.7 %attn_bwd.3 = (f32[256,2048]{1,0:T(8,128)}, bf16[1024,256]{1,0:T(8,128)(2,1)S(1)}, bf16[1024,256]{1,0:T(8,128)(2,1)S(1)}) custom-call(bf16[256,2048]{1,0:T(8,128)(2,1)S(1)} %copy-done.6, bf16[1024,256]{1,0:T(8,128)(2,1)S(1)} %copy-done.24, bf16[1024,256]{1,0:T(8,128)(2,1)S(1)} %copy-done.22, bf16[256,2048]{1,0:T(8,128)(2,1)} %copy-done.11, ...), custom_call_target="tpu_custom_call" | custom-call | flops 5368709120 | bytes 6291456 | tf_op jit(solution)/shard_map/attn_bwd/pallas_call | solution.py:137
  846.4 13.0 reduce-scatter.7.cloned.1.call-done
  870.4 24.2 %collective-permute-done.2 = bf16[256,2048]{1,0:T(8,128)(2,1)S(1)} collective-permute-done((bf16[256,2048]{1,0:T(8,128)(2,1)S(1)}, bf16[256,2048]{1,0:T(8,128)(2,1)S(1)}, u32[]{:S(2)}, u32[]{:S(2)}) %collective-permute-start.2) | collective-permute-done | bytes 1048608 | tf_op jit(solution)/shard_map/ppermute | solution.py:660
  894.7 25.1 %multiply_convert_fusion.2 = (bf16[256,5632]{1,0:T(8,128)(2,1)}, bf16[256,5632]{1,0:T(8,128)(2,1)}) fusion(f32[256,5632]{1,0:T(8,128)} %fusion.75, f32[256,5632]{1,0:T(8,128)} %get-tuple-element.173, bf16[256,2048]{1,0:T(8,128)(2,1)S(1)} %fusion.45.refs_20_, bf16[5632,2048]{1,0:T(8,128)(2,1)} %all-gather.7.cloned.1.call-done), kind=kOutput, calls=%fused_computation.6 | convolution fusion | flops 5924323328 | bytes 41418752 | tf_op jit(solution)/shard_map/dot_general | solution.py:644
  919.9 12.5 fusion.79
  932.4 14.5 multiply_reduce_fusion.1
  958.5 26.6 %attn_bwd.4 = (f32[256,2048]{1,0:T(8,128)}, bf16[1024,256]{1,0:T(8,128)(2,1)S(1)}, bf16[1024,256]{1,0:T(8,128)(2,1)S(1)}) custom-call(bf16[256,2048]{1,0:T(8,128)(2,1)S(1)} %copy-done.4, bf16[1024,256]{1,0:T(8,128)(2,1)S(1)} %copy-done.20, bf16[1024,256]{1,0:T(8,128)(2,1)S(1)} %copy-done.18, bf16[256,2048]{1,0:T(8,128)(2,1)} %copy-done.9, ...), custom_call_target="tpu_custom_call" | custom-call | flops 5368709120 | bytes 6291456 | tf_op jit(solution)/shard_map/attn_bwd/pallas_call | solution.py:137
  986.3 13.6 fusion.10
  1061.9 25.1 %multiply_convert_fusion = (bf16[256,5632]{1,0:T(8,128)(2,1)}, bf16[256,5632]{1,0:T(8,128)(2,1)}) fusion(f32[256,5632]{1,0:T(8,128)} %fusion.74, f32[256,5632]{1,0:T(8,128)} %get-tuple-element.170, bf16[256,2048]{1,0:T(8,128)(2,1)S(1)} %broadcast_select_fusion.8.refs_21_, bf16[5632,2048]{1,0:T(8,128)(2,1)} %all-gather.7.cloned.1.call-done), kind=kOutput, calls=%fused_computation.4 | convolution fusion | flops 5924323328 | bytes 41418752 | tf_op jit(solution)/shard_map/dot_general | solution.py:644
  1087.0 12.5 fusion.81
  1099.5 14.5 multiply_reduce_fusion
  1125.6 26.6 %attn_bwd.5 = (f32[256,2048]{1,0:T(8,128)}, bf16[1024,256]{1,0:T(8,128)(2,1)S(1)}, bf16[1024,256]{1,0:T(8,128)(2,1)S(1)}) custom-call(bf16[256,2048]{1,0:T(8,128)(2,1)S(1)} %copy.77.q_ref, bf16[1024,256]{1,0:T(8,128)(2,1)S(1)} %copy-done.16, bf16[1024,256]{1,0:T(8,128)(2,1)S(1)} %copy-done.14, bf16[256,2048]{1,0:T(8,128)(2,1)} %copy-done.7, ...), custom_call_target="tpu_custom_call" | custom-call | flops 5368709120 | bytes 6291456 | tf_op jit(solution)/shard_map/attn_bwd/pallas_call | solution.py:137
  1193.2 527.5 %reduce_weights.1 = (bf16[512,5632]{1,0:T(8,128)(2,1)}, bf16[512,5632]{1,0:T(8,128)(2,1)}, bf16[512,2560]{1,0:T(8,128)(2,1)}, bf16[512,2048]{1,0:T(8,128)(2,1)}, bf16[1408,2048]{1,0:T(8,128)(2,1)}) custom-call(bf16[2048,512]{1,0:T(8,128)(2,1)} %copy.98.refs_0_, bf16[2048,512]{1,0:T(8,128)(2,1)} %copy.99.refs_1_, bf16[2048,512]{1,0:T(8,128)(2,1)} %copy.100.refs_2_, ...), custom_call_target="tpu_custom_call" | custom-call | flops 45097156608 | bytes 44040192 | tf_op jit(solution)/shard_map/reduce_weights/pallas_call | solution.py:485
  1757.1 17.1 reduce-scatter.13.cloned.1.call-done
  (357 shorter events, 345.3 us)
Async XLA Ops:
  7.2 334.6 %all-gather.5.cloned.1.call-start = ((), (), s32[]{:S(2)}) async-start(), calls=%async_computation.4 | async-start | bytes 1310720 | tf_op jit(solution)/shard_map/all_gather | solution.py:680
  313.3 17.7 copy-start.69
  316.0 146.2 %all-gather.7.cloned.1.call-start = ((), (), s32[]{:S(2)}) async-start(), calls=%async_computation.5 | async-start | bytes 24510464 | tf_op jit(solution)/shard_map/all_gather | solution.py:667
  318.7 217.3 %all-gather.9.cloned.1.call-start = ((), (), s32[]{:S(2)}) async-start(), calls=%async_computation.6 | async-start | bytes 1310720 | tf_op jit(solution)/shard_map/all_gather | solution.py:680
  343.1 24.9 %copy-start.13 = (bf16[1024,256]{1,0:T(8,128)(2,1)}, bf16[1024,256]{1,0:T(8,128)(2,1)S(1)}, u32[]{:S(2)}) copy-start(bf16[1024,256]{1,0:T(8,128)(2,1)S(1)} %get-tuple-element.128.v_ref) | copy-start | bytes 1572868
  343.1 24.9 %copy-start.15 = (bf16[1024,256]{1,0:T(8,128)(2,1)}, bf16[1024,256]{1,0:T(8,128)(2,1)S(1)}, u32[]{:S(2)}) copy-start(bf16[1024,256]{1,0:T(8,128)(2,1)S(1)} %get-tuple-element.129.k_ref) | copy-start | bytes 1572868
  343.1 24.9 %copy-start.26 = (bf16[2,256,2048]{2,1,0:T(8,128)(2,1)S(1)}, bf16[2,256,2048]{2,1,0:T(8,128)(2,1)}, u32[]{:S(2)}) copy-start(bf16[2,256,2048]{2,1,0:T(8,128)(2,1)} %copy-done.25) | copy-start | bytes 6291460
  374.3 14.5 copy-start.39
  462.2 38.4 %copy-start.27 = (bf16[2,256,2048]{2,1,0:T(8,128)(2,1)S(1)}, bf16[2,256,2048]{2,1,0:T(8,128)(2,1)}, u32[]{:S(2)}) copy-start(bf16[2,256,2048]{2,1,0:T(8,128)(2,1)} %copy-done.25) | copy-start | bytes 6291460
  474.4 28.1 %copy-start.58 = (bf16[256,2048]{1,0:T(8,128)(2,1)}, bf16[256,2048]{1,0:T(8,128)(2,1)S(1)}, u32[]{:S(2)}) copy-start(bf16[256,2048]{1,0:T(8,128)(2,1)S(1)} %fusion.6) | copy-start | bytes 3145732
  474.4 26.2 %collective-permute-start = (bf16[256,2048]{1,0:T(8,128)(2,1)S(1)}, bf16[256,2048]{1,0:T(8,128)(2,1)S(1)}, u32[]{:S(2)}, u32[]{:S(2)}) collective-permute-start(bf16[256,2048]{1,0:T(8,128)(2,1)S(1)} %fusion.6), channel_id=1, source_target_pairs={{0,16},{1,17},{2,18},{3,19},{4,20},{5,21},{6,22},{7,23},{8,24},{9,... | collective-permute-start | bytes 3145736 | tf_op jit(solution)/shard_map/ppermute | solution.py:660
  506.9 168.0 %all-gather.11.cloned.1.call-start = ((), (), s32[]{:S(2)}) async-start(), calls=%async_computation.7 | async-start | bytes 1310720 | tf_op jit(solution)/shard_map/all_gather | solution.py:680
  537.4 24.5 %copy-start.17 = (bf16[1024,256]{1,0:T(8,128)(2,1)}, bf16[1024,256]{1,0:T(8,128)(2,1)S(1)}, u32[]{:S(2)}) copy-start(bf16[1024,256]{1,0:T(8,128)(2,1)S(1)} %get-tuple-element.126.v_ref) | copy-start | bytes 1572868
  537.4 24.5 %copy-start.19 = (bf16[1024,256]{1,0:T(8,128)(2,1)}, bf16[1024,256]{1,0:T(8,128)(2,1)S(1)}, u32[]{:S(2)}) copy-start(bf16[1024,256]{1,0:T(8,128)(2,1)S(1)} %get-tuple-element.127.k_ref) | copy-start | bytes 1572868
  537.5 24.3 %copy-start.31 = (bf16[256,2048]{1,0:T(8,128)(2,1)S(1)}, bf16[256,2048]{1,0:T(8,128)(2,1)}, u32[]{:S(2)}) copy-start(bf16[256,2048]{1,0:T(8,128)(2,1)} %copy-done.30) | copy-start | bytes 3145732
  568.2 35.0 %copy-start.41 = (f32[256,2048]{1,0:T(8,128)}, f32[256,2048]{1,0:T(8,128)S(1)}, u32[]{:S(2)}) copy-start(f32[256,2048]{1,0:T(8,128)S(1)} %get-tuple-element.172) | copy-start | bytes 6291460
  614.7 27.0 %copy-start.60 = (bf16[256,2048]{1,0:T(8,128)(2,1)}, bf16[256,2048]{1,0:T(8,128)(2,1)S(1)}, u32[]{:S(2)}) copy-start(bf16[256,2048]{1,0:T(8,128)(2,1)S(1)} %fusion.7) | copy-start | bytes 3145732
  614.7 25.2 %collective-permute-start.1 = (bf16[256,2048]{1,0:T(8,128)(2,1)S(1)}, bf16[256,2048]{1,0:T(8,128)(2,1)S(1)}, u32[]{:S(2)}, u32[]{:S(2)}) collective-permute-start(bf16[256,2048]{1,0:T(8,128)(2,1)S(1)} %fusion.7), channel_id=1, source_target_pairs={{0,16},{1,17},{2,18},{3,19},{4,20},{5,21},{6,22},{7,23},{8,24},{9,... | collective-permute-start | bytes 3145736 | tf_op jit(solution)/shard_map/ppermute | solution.py:660
  646.0 213.3 %reduce-scatter.7.cloned.1.call-start = ((), (), s32[]{:S(2)}) async-start(), calls=%async_computation.8 | async-start | bytes 1310720 | tf_op jit(solution)/shard_map/reduce_scatter | solution.py:713
  676.3 24.5 %copy-start.21 = (bf16[1024,256]{1,0:T(8,128)(2,1)}, bf16[1024,256]{1,0:T(8,128)(2,1)S(1)}, u32[]{:S(2)}) copy-start(bf16[1024,256]{1,0:T(8,128)(2,1)S(1)} %get-tuple-element.124.v_ref) | copy-start | bytes 1572868
  676.3 24.5 %copy-start.23 = (bf16[1024,256]{1,0:T(8,128)(2,1)}, bf16[1024,256]{1,0:T(8,128)(2,1)S(1)}, u32[]{:S(2)}) copy-start(bf16[1024,256]{1,0:T(8,128)(2,1)S(1)} %get-tuple-element.125.k_ref) | copy-start | bytes 1572868
  676.5 24.3 %copy-start.36 = (bf16[256,2048]{1,0:T(8,128)(2,1)S(1)}, bf16[256,2048]{1,0:T(8,128)(2,1)}, u32[]{:S(2)}) copy-start(bf16[256,2048]{1,0:T(8,128)(2,1)} %copy-done.34) | copy-start | bytes 3145732
  722.1 19.3 %copy-start.56 = (bf16[256,2048]{1,0:T(8,128)(2,1)S(1)}, bf16[256,2048]{1,0:T(8,128)(2,1)}, u32[]{:S(2)}) copy-start(bf16[256,2048]{1,0:T(8,128)(2,1)} %fusion.46.refs_19_) | copy-start | bytes 3145732
  833.0 189.1 %reduce-scatter.9.cloned.1.call-start = ((), (), s32[]{:S(2)}) async-start(), calls=%async_computation.9 | async-start | bytes 1310720 | tf_op jit(solution)/shard_map/reduce_scatter | solution.py:713
  867.8 26.7 %copy-start.33 = (bf16[2,256,2048]{2,1,0:T(8,128)(2,1)S(1)}, bf16[2,256,2048]{2,1,0:T(8,128)(2,1)}, u32[]{:S(2)}) copy-start(bf16[2,256,2048]{2,1,0:T(8,128)(2,1)} %get-tuple-element.165) | copy-start | bytes 6291460
  867.9 26.7 %collective-permute-start.2 = (bf16[256,2048]{1,0:T(8,128)(2,1)S(1)}, bf16[256,2048]{1,0:T(8,128)(2,1)S(1)}, u32[]{:S(2)}, u32[]{:S(2)}) collective-permute-start(bf16[256,2048]{1,0:T(8,128)(2,1)S(1)} %get-tuple-element.92), channel_id=1, source_target_pairs={{16,0},{17,1},{18,2},{19,3},{20,4},{21,5},{22,6},{23,7},{24,8},{25... | collective-permute-start | bytes 3145736 | tf_op jit(solution)/shard_map/ppermute | solution.py:660
  894.7 25.1 %copy-start.51 = (bf16[256,2048]{1,0:T(8,128)(2,1)}, bf16[256,2048]{1,0:T(8,128)(2,1)S(1)}, u32[]{:S(2)}) copy-start(bf16[256,2048]{1,0:T(8,128)(2,1)S(1)} %fusion.45.refs_20_) | copy-start | bytes 3145732
  986.2 200.7 %reduce-scatter.11.cloned.1.call-start = ((), (), s32[]{:S(2)}) async-start(), calls=%async_computation.10 | async-start | bytes 1310720 | tf_op jit(solution)/shard_map/reduce_scatter | solution.py:713
  1034.4 26.2 %collective-permute-start.3 = (bf16[256,2048]{1,0:T(8,128)(2,1)}, bf16[256,2048]{1,0:T(8,128)(2,1)}, u32[]{:S(2)}, u32[]{:S(2)}) collective-permute-start(bf16[256,2048]{1,0:T(8,128)(2,1)} %get-tuple-element.88), channel_id=1, source_target_pairs={{16,0},{17,1},{18,2},{19,3},{20,4},{21,5},{22,6},{23,7},{24,8},{25... | collective-permute-start | bytes 3145736 | tf_op jit(solution)/shard_map/ppermute | solution.py:660
  1061.9 25.1 %copy-start.57 = (bf16[256,2048]{1,0:T(8,128)(2,1)}, bf16[256,2048]{1,0:T(8,128)(2,1)S(1)}, u32[]{:S(2)}) copy-start(bf16[256,2048]{1,0:T(8,128)(2,1)S(1)} %broadcast_select_fusion.8.refs_21_) | copy-start | bytes 3145732
  1099.5 14.5 copy-start.85
  1153.3 620.9 %reduce-scatter.13.cloned.1.call-start = ((), (), s32[]{:S(2)}) async-start(), calls=%async_computation.11 | async-start | bytes 1310720
  (73 other events, 374.8 us)
Sparse Core Ops, SparseCore 0:
  316.1 25.6 all-gather.4
  344.0 118.1 all-gather.6
  507.0 28.9 all-gather.8
  646.2 28.7 all-gather.10
  833.1 26.1 reduce-scatter.6
  986.4 25.0 reduce-scatter.8
  1153.5 25.2 reduce-scatter.10
  1748.6 25.5 reduce-scatter.12

commit v4 on v3

--- a/solution.py
+++ b/solution.py
@@ -16,141 +16,6 @@
 
 def mm(a, b):
     return jnp.dot(a, b, preferred_element_type=F32)
-
-
-def attn_fwd_kernel(axis, pairs, q_ref, k_ref, v_ref, o_ref, lse_ref, bias_ref):
-    keys, queries = bias_ref.shape
-    offset = lax.axis_index(axis) * queries
-
-    @pl.when(pl.program_id(0) == 0)
-    def _():
-        key_pos = lax.broadcasted_iota(jnp.int32, (keys, queries), 0)
-        query_pos = lax.broadcasted_iota(jnp.int32, (keys, queries), 1) + offset
-        bias_ref[...] = jnp.where(key_pos <= query_pos, 0.0, NEG_FILL)
-
-    for half in range(2):
-        key = k_ref[:, half * HEAD:(half + 1) * HEAD]
-        value_t = v_ref[...].T[half * HEAD:(half + 1) * HEAD, :]
-        for pair in range(pairs):
-            col = (half * pairs + pair) * 2 * HEAD
-            q_t = q_ref[:, col:col + 2 * HEAD].T
-            outs = []
-            for sub in range(2):
-                head = (half * pairs + pair) * 2 + sub
-                scores = mm(key, q_t[sub * HEAD:(sub + 1) * HEAD, :]) * (LOG2E * HEAD ** -0.5) + bias_ref[...]
-                top = jnp.max(scores, axis=0, keepdims=True)
-                prob = jnp.exp2(scores - top)
-                total = jnp.sum(prob, axis=0, keepdims=True)
-                outs.append(mm(value_t, prob.astype(BF16)) / total)
-                lse_ref[0, head:head + 1, :] = top + jnp.log2(total)
-            o_ref[:, col:col + 2 * HEAD] = jnp.concatenate(outs, axis=0).T.astype(BF16)
-
-
-def attn_fwd(q, k, v, axis):
-    queries, width = q.shape
-    keys = k.shape[0]
-    pairs = HEADS // KV_HEADS // 2
-    steps = KV_HEADS // 2
-    heads = HEADS // steps
-    return pl.pallas_call(
-        functools.partial(attn_fwd_kernel, axis, pairs),
-        grid=(steps,),
-        in_specs=[
-            pl.BlockSpec((queries, width // steps), lambda i: (0, i)),
-            pl.BlockSpec((keys, 2 * HEAD), lambda i: (0, i)),
-            pl.BlockSpec((keys, 2 * HEAD), lambda i: (0, i)),
-        ],
-        out_specs=[
-            pl.BlockSpec((queries, width // steps), lambda i: (0, i)),
-            pl.BlockSpec((1, heads, queries), lambda i: (i, 0, 0)),
-        ],
-        out_shape=[
-            jax.ShapeDtypeStruct((queries, width), BF16),
-            jax.ShapeDtypeStruct((steps, heads, queries), F32),
-        ],
-        scratch_shapes=[pltpu.VMEM((keys, queries), F32)],
-        compiler_params=pltpu.CompilerParams(vmem_limit_bytes=50 * 1024 * 1024),
-        cost_estimate=pl.CostEstimate(
-            flops=4 * queries * keys * width, bytes_accessed=4 * queries * width * 2,
-            transcendentals=queries * keys * HEADS),
-        name="attn_fwd",
-    )(q, k, v)
-
-
-def attn_bwd_kernel(axis, pairs, q_ref, k_ref, v_ref, o_ref, do_ref, lse_ref, dq_ref, dk_ref, dv_ref, bias_ref, dk_acc, dv_acc):
-    keys, queries = bias_ref.shape
-    offset = lax.axis_index(axis) * queries
-
-    @pl.when(pl.program_id(0) == 0)
-    def _():
-        key_pos = lax.broadcasted_iota(jnp.int32, (keys, queries), 0)
-        query_pos = lax.broadcasted_iota(jnp.int32, (keys, queries), 1) + offset
-        bias_ref[...] = jnp.where(key_pos <= query_pos, 0.0, NEG_FILL)
-
-    low_lane = lax.broadcasted_iota(jnp.int32, (queries, 2 * HEAD), 1) < HEAD
-    for half in range(2):
-        key = k_ref[:, half * HEAD:(half + 1) * HEAD]
-        value = v_ref[:, half * HEAD:(half + 1) * HEAD]
-        key_t = k_ref[...].T[half * HEAD:(half + 1) * HEAD, :]
-        for pair in range(pairs):
-            col = (half * pairs + pair) * 2 * HEAD
-            q_rows = q_ref[:, col:col + 2 * HEAD]
-            do_rows = do_ref[:, col:col + 2 * HEAD]
-            q_t = q_rows.T
-            do_t = do_rows.T
-            delta_t = (o_ref[:, col:col + 2 * HEAD].astype(F32) * do_rows.astype(F32)).T
-            dqs = []
-            for sub in range(2):
-                head = (half * pairs + pair) * 2 + sub
-                rows = slice(sub * HEAD, (sub + 1) * HEAD)
-                lane = low_lane if sub == 0 else jnp.logical_not(low_lane)
-                scores = mm(key, q_t[rows, :]) * (LOG2E * HEAD ** -0.5) + bias_ref[...]
-                prob = jnp.exp2(scores - lse_ref[0, head:head + 1, :])
-                grad_prob = mm(value, do_t[rows, :])
-                delta = jnp.sum(delta_t[rows, :], axis=0, keepdims=True)
-                grad_score = (prob * (grad_prob - delta)).astype(BF16)
-                prob = prob.astype(BF16)
-                dqs.append(mm(key_t, grad_score))
-                dk_term = mm(grad_score, jnp.where(lane, q_rows, jnp.zeros_like(q_rows)))
-                dv_term = mm(prob, jnp.where(lane, do_rows, jnp.zeros_like(do_rows)))
-                if pair == 0 and sub == 0:
-                    dk_acc[...] = dk_term
-                    dv_acc[...] = dv_term
-                else:
-                    dk_acc[...] += dk_term
-                    dv_acc[...] += dv_term
-            dq_ref[:, col:col + 2 * HEAD] = jnp.concatenate(dqs, axis=0).T * HEAD ** -0.5
-        dk_sum = (dk_acc[:, :HEAD] + dk_acc[:, HEAD:]) * HEAD ** -0.5
-        dv_sum = dv_acc[:, :HEAD] + dv_acc[:, HEAD:]
-        dk_ref[:, half * HEAD:(half + 1) * HEAD] = dk_sum.astype(dk_ref.dtype)
-        dv_ref[:, half * HEAD:(half + 1) * HEAD] = dv_sum.astype(dv_ref.dtype)
-
-
-def attn_bwd(q, k, v, o, do, lse, axis):
-    queries, width = q.shape
-    keys = k.shape[0]
-    pairs = HEADS // KV_HEADS // 2
-    steps = KV_HEADS // 2
-    heads = HEADS // steps
-    wide = pl.BlockSpec((queries, width // steps), lambda i: (0, i))
-    narrow = pl.BlockSpec((keys, 2 * HEAD), lambda i: (0, i))
-    return pl.pallas_call(
-        functools.partial(attn_bwd_kernel, axis, pairs),
-        grid=(steps,),
-        in_specs=[wide, narrow, narrow, wide, wide, pl.BlockSpec((1, heads, queries), lambda i: (i, 0, 0))],
-        out_specs=[wide, narrow, narrow],
-        out_shape=[
-            jax.ShapeDtypeStruct((queries, width), F32),
-            jax.ShapeDtypeStruct((keys, k.shape[1]), BF16),
-            jax.ShapeDtypeStruct((keys, k.shape[1]), BF16),
-        ],
-        scratch_shapes=[pltpu.VMEM((keys, queries), F32), pltpu.VMEM((keys, 2 * HEAD), F32), pltpu.VMEM((keys, 2 * HEAD), F32)],
-        compiler_params=pltpu.CompilerParams(vmem_limit_bytes=50 * 1024 * 1024),
-        cost_estimate=pl.CostEstimate(
-            flops=10 * queries * keys * width, bytes_accessed=12 * queries * width,
-            transcendentals=queries * keys * HEADS),
-        name="attn_bwd",
-    )(q, k, v, o, do, lse)
 
 
 MESH_IDS = pl.DeviceIdType.MESH
@@ -612,6 +477,408 @@
 
 
 EPSILON = 1e-05
+FF_TILE = 512
+
+
+def mm_t(a, b):
+    return lax.dot_general(a, b, (((1,), (1,)), ((), ())), preferred_element_type=F32)
+
+
+def inv_root_of(rows):
+    return lax.rsqrt(jnp.mean(rows * rows, axis=-1, keepdims=True) + EPSILON)
+
+
+def ffn_fwd_kernel(mid_ref, gain_ref, w_g, w_u, w_d, out_ref, normed_ref, hidden_ref, gate_fac, up_fac, acc):
+    step = pl.program_id(0)
+
+    @pl.when(step == 0)
+    def _():
+        mid = mid_ref[...]
+        normed_ref[...] = (mid * inv_root_of(mid) * gain_ref[...]).astype(BF16)
+        acc[...] = mid
+
+    gate = mm(normed_ref[...], w_g[...])
+    up = mm(normed_ref[...], w_u[...])
+    sig = jax.nn.sigmoid(gate)
+    act = gate * sig
+    hidden = (act * up).astype(BF16)
+    hidden_ref[...] = hidden
+    up_fac[...] = act.astype(BF16)
+    gate_fac[...] = (up * sig * (1.0 + gate * (1.0 - sig))).astype(BF16)
+    acc[...] += mm(hidden, w_d[...])
+
+    @pl.when(step == pl.num_programs(0) - 1)
+    def _():
+        out_ref[...] = acc[...].astype(BF16)
+
+
+def ffn_fwd(middle, gain, w_g, w_u, w_d):
+    rows, width = middle.shape
+    ff = w_g.shape[1]
+    whole = pl.BlockSpec((rows, width), lambda i: (0, 0))
+    part = pl.BlockSpec((rows, FF_TILE), lambda i: (0, i))
+    tall = pl.BlockSpec((width, FF_TILE), lambda i: (0, i))
+    wide = jax.ShapeDtypeStruct((rows, ff), BF16)
+    return pl.pallas_call(
+        ffn_fwd_kernel,
+        grid=(ff // FF_TILE,),
+        in_specs=[whole, pl.BlockSpec((1, width), lambda i: (0, 0)), tall, tall, pl.BlockSpec((FF_TILE, width), lambda i: (i, 0))],
+        out_specs=[whole, whole, part, part, part],
+        out_shape=[jax.ShapeDtypeStruct((rows, width), BF16)] * 2 + [wide] * 3,
+        scratch_shapes=[pltpu.VMEM((rows, width), F32)],
+        compiler_params=pltpu.CompilerParams(vmem_limit_bytes=58 * 1024 * 1024),
+        cost_estimate=pl.CostEstimate(flops=6 * rows * width * ff, bytes_accessed=6 * width * ff, transcendentals=rows * ff),
+        name="ffn_fwd",
+    )(middle, gain, w_g, w_u, w_d)
+
+
+def ffn_bwd_kernel(grad_ref, mid_ref, gain_ref, gate_fac, up_fac, w_g, w_u, w_d,
+                   dgate_ref, dup_ref, dmid_ref, da_ref, dgain_ref, acc):
+    step = pl.program_id(0)
+    dhidden = mm_t(grad_ref[...], w_d[...])
+    dgate = (dhidden * gate_fac[...].astype(F32)).astype(BF16)
+    dup = (dhidden * up_fac[...].astype(F32)).astype(BF16)
+    dgate_ref[...] = dgate
+    dup_ref[...] = dup
+    term = mm_t(dgate, w_g[...]) + mm_t(dup, w_u[...])
+
+    @pl.when(step == 0)
+    def _():
+        acc[...] = term
+
+    @pl.when(step > 0)
+    def _():
+        acc[...] += term
+
+    @pl.when(step == pl.num_programs(0) - 1)
+    def _():
+        mid = mid_ref[...]
+        root = inv_root_of(mid)
+        dnormed = acc[...]
+        scaled = dnormed * gain_ref[...]
+        dmid = grad_ref[...].astype(F32) + root * scaled - mid * (root * root * root * jnp.mean(scaled * mid, axis=-1, keepdims=True))
+        dmid_ref[...] = dmid
+        da_ref[...] = dmid.astype(BF16)
+        dgain_ref[...] = jnp.sum(dnormed * mid * root, axis=0, keepdims=True)
+
+
+def ffn_bwd(grad, middle, gain, gate_fac, up_fac, w_g, w_u, w_d):
+    rows, width = middle.shape
+    ff = w_g.shape[1]
+    whole = pl.BlockSpec((rows, width), lambda i: (0, 0))
+    flat = pl.BlockSpec((1, width), lambda i: (0, 0))
+    part = pl.BlockSpec((rows, FF_TILE), lambda i: (0, i))
+    tall = pl.BlockSpec((width, FF_TILE), lambda i: (0, i))
+    wide = jax.ShapeDtypeStruct((rows, ff), BF16)
+    return pl.pallas_call(
+        ffn_bwd_kernel,
+        grid=(ff // FF_TILE,),
+        in_specs=[whole, whole, flat, part, part, tall, tall, pl.BlockSpec((FF_TILE, width), lambda i: (i, 0))],
+        out_specs=[part, part, whole, whole, flat],
+        out_shape=[wide, wide, jax.ShapeDtypeStruct((rows, width), F32), jax.ShapeDtypeStruct((rows, width), BF16),
+                   jax.ShapeDtypeStruct((1, width), F32)],
+        scratch_shapes=[pltpu.VMEM((rows, width), F32)],
+        compiler_params=pltpu.CompilerParams(vmem_limit_bytes=58 * 1024 * 1024),
+        cost_estimate=pl.CostEstimate(flops=6 * rows * width * ff, bytes_accessed=6 * width * ff, transcendentals=0),
+        name="ffn_bwd",
+    )(grad, middle, gain, gate_fac, up_fac, w_g, w_u, w_d)
+
+
+def rotated(rows, cos_ref, sin_ref):
+    width = rows.shape[1]
+    low_half = lax.rem(lax.broadcasted_iota(jnp.int32, rows.shape, 1), HEAD) < HEAD // 2
+    swapped = jnp.where(low_half, pltpu.roll(rows, width - HEAD // 2, 1), pltpu.roll(rows, HEAD // 2, 1))
+    reps = width // LANES
+    return rows * jnp.tile(cos_ref[...], (1, reps)) + swapped * jnp.tile(sin_ref[...], (1, reps))
+
+
+def attend_block_kernel(x_ref, gain_ref, cos_ref, sin_ref, w_q, w_kv, w_o,
+                        normed_ref, q_ref, kv_ref, attended_ref, lse_ref, mid_ref,
+                        wq_ref, wkv_ref, wo_ref, q_turn, acc, top_ref, total_ref, land,
+                        load_sem, send_sem, recv_sem):
+    n = lax.axis_size("shard")
+    me = lax.axis_index("shard")
+    rows, width = x_ref.shape
+    kv_width = wkv_ref.shape[1] // 2
+    group = HEADS // KV_HEADS
+    scale = LOG2E * HEAD ** -0.5
+    barrier = pltpu.get_barrier_semaphore()
+    for d in range(1, n):
+        @pl.when(me >= d)
+        def _(d=d):
+            pl.semaphore_signal(barrier, inc=1, device_id={"shard": me - d}, device_id_type=MESH_IDS)
+    loads = [pltpu.make_async_copy(src, dst, load_sem.at[k])
+             for k, (src, dst) in enumerate(((w_kv, wkv_ref), (w_q, wq_ref), (w_o, wo_ref)))]
+    for load in loads:
+        load.start()
+
+    def to_later(d):
+        return remote(land.at[0], land.at[d], send_sem.at[d - 1], recv_sem.at[d - 1], {"shard": me + d})
+
+    def from_earlier(d):
+        return remote(land.at[0], land.at[d], send_sem.at[d - 1], recv_sem.at[d - 1], {"shard": me - d})
+
+    x = x_ref[...].astype(F32)
+    normed_ref[...] = (x * inv_root_of(x) * gain_ref[...]).astype(BF16)
+    loads[0].wait()
+    kv = mm(normed_ref[...], wkv_ref[...])
+    land[0, :, :kv_width] = rotated(kv[:, :kv_width], cos_ref, sin_ref).astype(BF16)
+    land[0, :, kv_width:] = kv[:, kv_width:].astype(BF16)
+    @pl.when(me < n - 1)
+    def _():
+        pl.semaphore_wait(barrier, n - 1 - me)
+
+    for d in range(1, n):
+        @pl.when(me + d < n)
+        def _(d=d):
+            to_later(d).start()
+    loads[1].wait()
+    chunk = 4 * LANES
+    for at in range(0, width, chunk):
+        q_chunk = rotated(mm(normed_ref[...], wq_ref[:, at:at + chunk]), cos_ref, sin_ref).astype(BF16)
+        q_ref[:, at:at + chunk] = q_chunk
+        q_turn[at:at + chunk, :] = q_chunk.T
+
+    def heads_of(d):
+        for h in range(KV_HEADS):
+            key = land[d, :, h * HEAD:(h + 1) * HEAD]
+            pair_t = land[d, :, kv_width + h // 2 * LANES:kv_width + (h // 2 + 1) * LANES].T
+            value_t = pair_t[h % 2 * HEAD:(h % 2 + 1) * HEAD, :]
+            for j in range(h * group, (h + 1) * group):
+                yield j, key, value_t
+
+    key_pos = lax.broadcasted_iota(jnp.int32, (rows, rows), 0)
+    query_pos = lax.broadcasted_iota(jnp.int32, (rows, rows), 1)
+    bias = jnp.where(key_pos <= query_pos, 0.0, NEG_FILL)
+    for j, key, value_t in heads_of(0):
+        span = slice(j * HEAD, (j + 1) * HEAD)
+        scores = mm(key, q_turn[span, :]) * scale + bias
+        top = jnp.max(scores, axis=0, keepdims=True)
+        prob = jnp.exp2(scores - top)
+        top_ref[j:j + 1, :] = top
+        total_ref[j:j + 1, :] = jnp.sum(prob, axis=0, keepdims=True)
+        acc[span, :] = mm(value_t, prob.astype(BF16))
+
+    def earlier(d, carry):
+        from_earlier(d).wait_recv()
+        for j, key, value_t in heads_of(d):
+            span = slice(j * HEAD, (j + 1) * HEAD)
+            scores = mm(key, q_turn[span, :]) * scale
+            old = top_ref[j:j + 1, :]
+            top = jnp.maximum(old, jnp.max(scores, axis=0, keepdims=True))
+            fade = jnp.exp2(old - top)
+            prob = jnp.exp2(scores - top)
+            top_ref[j:j + 1, :] = top
+            total_ref[j:j + 1, :] = total_ref[j:j + 1, :] * fade + jnp.sum(prob, axis=0, keepdims=True)
+            acc[span, :] = acc[span, :] * fade + mm(value_t, prob.astype(BF16))
+        return carry
+
+    lax.fori_loop(1, me + 1, earlier, 0)
+    total = total_ref[...]
+    lse_ref[...] = top_ref[...] + jnp.log2(total)
+    total_ref[...] = 1.0 / total
+    for pair in range(HEADS // 2):
+        col = pair * LANES
+        halves_t = [acc[col + k * HEAD:col + (k + 1) * HEAD, :] * total_ref[2 * pair + k:2 * pair + k + 1, :] for k in range(2)]
+        attended_ref[:, col:col + LANES] = jnp.concatenate(halves_t, axis=0).T.astype(BF16)
+    for d in range(n):
+        @pl.when(me >= d)
+        def _(d=d):
+            kv_ref[d] = land[d]
+    loads[2].wait()
+    for at in range(0, width, chunk):
+        mid_ref[:, at:at + chunk] = x_ref[:, at:at + chunk].astype(F32) + mm(attended_ref[...], wo_ref[:, at:at + chunk])
+    for d in range(1, n):
+        @pl.when(me + d < n)
+        def _(d=d):
+            to_later(d).wait_send()
+
+
+def attend_block(x, gain, cos_table, sin_table, w_q, w_kv, w_o, collective_id):
+    n = lax.axis_size("shard")
+    rows, width = x.shape
+    kv_both = w_kv.shape[1]
+    vmem = pl.BlockSpec(memory_space=pltpu.VMEM)
+    anywhere = pl.BlockSpec(memory_space=pl.ANY)
+    dma = pltpu.SemaphoreType.DMA
+    flops = 2 * rows * width * (2 * width + kv_both) + 4 * rows * rows * n * width
+    return pl.pallas_call(
+        attend_block_kernel,
+        in_specs=[vmem] * 4 + [anywhere] * 3,
+        out_specs=[vmem] * 6,
+        out_shape=[
+            jax.ShapeDtypeStruct((rows, width), BF16),
+            jax.ShapeDtypeStruct((rows, width), BF16),
+            jax.ShapeDtypeStruct((n, rows, kv_both), BF16),
+            jax.ShapeDtypeStruct((rows, width), BF16),
+            jax.ShapeDtypeStruct((HEADS, rows), F32),
+            jax.ShapeDtypeStruct((rows, width), F32),
+        ],
+        scratch_shapes=[
+            pltpu.VMEM(w_q.shape, BF16), pltpu.VMEM(w_kv.shape, BF16), pltpu.VMEM(w_o.shape, BF16),
+            pltpu.VMEM((width, rows), BF16), pltpu.VMEM((width, rows), F32),
+            pltpu.VMEM((HEADS, rows), F32), pltpu.VMEM((HEADS, rows), F32),
+            pltpu.VMEM((n, rows, kv_both), BF16),
+            dma((3,)), dma((n - 1,)), dma((n - 1,)),
+        ],
+        compiler_params=pltpu.CompilerParams(
+            collective_id=collective_id, has_side_effects=True, vmem_limit_bytes=56 * 1024 * 1024),
+        cost_estimate=pl.CostEstimate(flops=flops, bytes_accessed=2 * width * (2 * width + kv_both), transcendentals=rows * rows * n * HEADS),
+        name="attend_block",
+    )(x, gain, cos_table, sin_table, w_q, w_kv, w_o)
+
+
+def attend_back_kernel(da_ref, dmid_ref, x_ref, gain_ref, cos_ref, sin_ref, q_ref, kv_ref, attended_ref, lse_ref, w_q, w_kv, w_o,
+                       dq_ref, dkv_ref, grad_ref, grad_low_ref, dgain_ref,
+                       wq_ref, wkv_ref, wo_ref, do_ref, q_turn, do_turn, delta_ref, dq_acc, dkv_acc, dn_ref, send_kv, land_kv,
+                       load_sem, send_sem, recv_sem):
+    n = lax.axis_size("shard")
+    me = lax.axis_index("shard")
+    rows, width = x_ref.shape
+    kv_width = wkv_ref.shape[1] // 2
+    pairs = HEADS // KV_HEADS // 2
+    scale = LOG2E * HEAD ** -0.5
+    barrier = pltpu.get_barrier_semaphore()
+    for d in range(1, n):
+        @pl.when(me + d < n)
+        def _(d=d):
+            pl.semaphore_signal(barrier, inc=1, device_id={"shard": me + d}, device_id_type=MESH_IDS)
+    loads = [pltpu.make_async_copy(src, dst, load_sem.at[k])
+             for k, (src, dst) in enumerate(((w_o, wo_ref), (w_q, wq_ref), (w_kv, wkv_ref)))]
+    for load in loads:
+        load.start()
+
+    def to_earlier(d):
+        return remote(send_kv.at[d - 1], land_kv.at[d - 1], send_sem.at[d - 1], recv_sem.at[d - 1], {"shard": me - d})
+
+    def from_later(d):
+        return remote(send_kv.at[d - 1], land_kv.at[d - 1], send_sem.at[d - 1], recv_sem.at[d - 1], {"shard": me + d})
+
+    chunk = 4 * LANES
+    for at in range(0, width, LANES):
+        q_turn[at:at + LANES, :] = q_ref[:, at:at + LANES].T
+    loads[0].wait()
+    for at in range(0, width, chunk):
+        do_chunk = mm_t(da_ref[...], wo_ref[at:at + chunk, :]).astype(BF16)
+        do_ref[:, at:at + chunk] = do_chunk
+        do_turn[at:at + chunk, :] = do_chunk.T
+    for pair in range(HEADS // 2):
+        cols = slice(pair * LANES, (pair + 1) * LANES)
+        both = (attended_ref[:, cols].astype(F32) * do_ref[:, cols].astype(F32)).T
+        for k in range(2):
+            delta_ref[2 * pair + k:2 * pair + k + 1, :] = jnp.sum(both[k * HEAD:(k + 1) * HEAD, :], axis=0, keepdims=True)
+    dq_acc[...] = jnp.zeros_like(dq_acc)
+    low_lane = lax.broadcasted_iota(jnp.int32, (rows, LANES), 1) < HEAD
+    zero_rows = jnp.zeros((rows, LANES), BF16)
+
+    def block(d, bias):
+        for h in range(KV_HEADS):
+            own = slice(h * HEAD, (h + 1) * HEAD)
+            key = kv_ref[d, :, own]
+            value = kv_ref[d, :, kv_width + h * HEAD:kv_width + (h + 1) * HEAD]
+            key_t = kv_ref[d, :, h // 2 * LANES:(h // 2 + 1) * LANES].T[h % 2 * HEAD:(h % 2 + 1) * HEAD, :]
+            dk = jnp.zeros((rows, LANES), F32)
+            dv = jnp.zeros((rows, LANES), F32)
+            for pair in range(h * pairs, (h + 1) * pairs):
+                cols = slice(pair * LANES, (pair + 1) * LANES)
+                q_rows = q_ref[:, cols]
+                do_rows = do_ref[:, cols]
+                for k in range(2):
+                    j = 2 * pair + k
+                    span = slice(j * HEAD, (j + 1) * HEAD)
+                    lane = low_lane if k == 0 else jnp.logical_not(low_lane)
+                    scores = mm(key, q_turn[span, :]) * scale
+                    if bias is not None:
+                        scores = scores + bias
+                    prob = jnp.exp2(scores - lse_ref[j:j + 1, :])
+                    dprob = mm(value, do_turn[span, :])
+                    dscore = (prob * (dprob - delta_ref[j:j + 1, :])).astype(BF16)
+                    dq_acc[span, :] += mm(key_t, dscore)
+                    dk = dk + mm(dscore, jnp.where(lane, q_rows, zero_rows))
+                    dv = dv + mm(prob.astype(BF16), jnp.where(lane, do_rows, zero_rows))
+            dkv_acc[:, own] = (dk[:, :HEAD] + dk[:, HEAD:]) * HEAD ** -0.5
+            dkv_acc[:, kv_width + h * HEAD:kv_width + (h + 1) * HEAD] = dv[:, :HEAD] + dv[:, HEAD:]
+
+    @pl.when(me > 0)
+    def _():
+        pl.semaphore_wait(barrier, me)
+
+    def earlier(i, carry):
+        d = me - i
+        block(d, None)
+        send_kv[d - 1] = dkv_acc[...].astype(BF16)
+        to_earlier(d).start()
+        return carry
+
+    lax.fori_loop(0, me, earlier, 0)
+    key_pos = lax.broadcasted_iota(jnp.int32, (rows, rows), 0)
+    query_pos = lax.broadcasted_iota(jnp.int32, (rows, rows), 1)
+    block(0, jnp.where(key_pos <= query_pos, 0.0, NEG_FILL))
+
+    loads[1].wait()
+    loads[2].wait()
+    for at in range(0, width, chunk):
+        for col in range(at, at + chunk, LANES):
+            dq_ref[:, col:col + LANES] = rotated(dq_acc[col:col + LANES, :].T * HEAD ** -0.5, cos_ref, sin_ref).astype(BF16)
+    for at in range(0, width, chunk):
+        dn_ref[:, at:at + chunk] = mm_t(dq_ref[...], wq_ref[at:at + chunk, :])
+    for d in range(1, n):
+        @pl.when(me + d < n)
+        def _(d=d):
+            from_later(d).wait_recv()
+            dkv_acc[...] += land_kv[d - 1].astype(F32)
+    dkv_ref[:, :kv_width] = rotated(dkv_acc[:, :kv_width], cos_ref, sin_ref).astype(BF16)
+    dkv_ref[:, kv_width:] = dkv_acc[:, kv_width:].astype(BF16)
+    for at in range(0, width, chunk):
+        dn_ref[:, at:at + chunk] += mm_t(dkv_ref[...], wkv_ref[at:at + chunk, :])
+    x = x_ref[...].astype(F32)
+    root = inv_root_of(x)
+    dnormed = dn_ref[...]
+    scaled = dnormed * gain_ref[...]
+    grad = dmid_ref[...] + root * scaled - x * (root * root * root * jnp.mean(scaled * x, axis=-1, keepdims=True))
+    grad_ref[...] = grad
+    grad_low_ref[...] = grad.astype(BF16)
+    dgain_ref[...] = jnp.sum(dnormed * x * root, axis=0, keepdims=True)
+    for d in range(1, n):
+        @pl.when(me >= d)
+        def _(d=d):
+            to_earlier(d).wait_send()
+
+
+def attend_back(da, dmid, x, gain, cos_table, back_sin, q, kv, attended, lse, w_q, w_kv, w_o, collective_id):
+    n = lax.axis_size("shard")
+    rows, width = x.shape
+    kv_both = w_kv.shape[1]
+    vmem = pl.BlockSpec(memory_space=pltpu.VMEM)
+    anywhere = pl.BlockSpec(memory_space=pl.ANY)
+    dma = pltpu.SemaphoreType.DMA
+    flops = 2 * rows * width * (2 * width + kv_both) + 10 * rows * rows * n * width
+    return pl.pallas_call(
+        attend_back_kernel,
+        in_specs=[vmem] * 10 + [anywhere] * 3,
+        out_specs=[vmem] * 5,
+        out_shape=[
+            jax.ShapeDtypeStruct((rows, width), BF16),
+            jax.ShapeDtypeStruct((rows, kv_both), BF16),
+            jax.ShapeDtypeStruct((rows, width), F32),
+            jax.ShapeDtypeStruct((rows, width), BF16),
+            jax.ShapeDtypeStruct((1, width), F32),
+        ],
+        scratch_shapes=[
+            pltpu.VMEM(w_q.shape, BF16), pltpu.VMEM(w_kv.shape, BF16), pltpu.VMEM(w_o.shape, BF16),
+            pltpu.VMEM((rows, width), BF16), pltpu.VMEM((width, rows), BF16), pltpu.VMEM((width, rows), BF16),
+            pltpu.VMEM((HEADS, rows), F32), pltpu.VMEM((width, rows), F32), pltpu.VMEM((rows, kv_both), F32),
+            pltpu.VMEM((rows, width), F32),
+            pltpu.VMEM((n - 1, rows, kv_both), BF16), pltpu.VMEM((n - 1, rows, kv_both), BF16),
+            dma((3,)), dma((n - 1,)), dma((n - 1,)),
+        ],
+        compiler_params=pltpu.CompilerParams(
+            collective_id=collective_id, has_side_effects=True, vmem_limit_bytes=58 * 1024 * 1024),
+        cost_estimate=pl.CostEstimate(flops=flops, bytes_accessed=2 * width * (2 * width + kv_both), transcendentals=rows * rows * n * HEADS),
+        name="attend_back",
+    )(da, dmid, x, gain, cos_table, back_sin, q, kv, attended, lse, w_q, w_kv, w_o)
+
+
 ROPE_BASE = 10000.0
 
 
@@ -622,38 +889,6 @@
     return (jnp.cos(angle_grid), jnp.sin(angle_grid))
 
 
-def rotate(matrix, cos_table, sin_table):
-    row_count = matrix.shape[0]
-    half_dim = HEAD // 2
-    pieces = matrix.reshape(row_count, -1, 2, half_dim)
-    first_half = pieces[:, :, 0, :]
-    second_half = pieces[:, :, 1, :]
-    cos_wide = cos_table[:, None, :]
-    sin_wide = sin_table[:, None, :]
-    rotated = jnp.stack(
-        [
-            first_half * cos_wide - second_half * sin_wide,
-            second_half * cos_wide + first_half * sin_wide,
-        ],
-        axis=2,
-    )
-    return rotated.reshape(row_count, -1)
-
-
-def times_t(left_rows, right_rows):
-    return lax.dot_general(left_rows, right_rows, (((1,), (1,)), ((), ())), preferred_element_type=F32)
-
-
-def inner_rows(left_rows, right_rows):
-    return lax.dot_general(left_rows, right_rows, (((0,), (0,)), ((), ())), preferred_element_type=F32)
-
-
-def norm_back(grad_normed, stream, inv_root, gain_row):
-    scaled = grad_normed * gain_row
-    cubed = inv_root * inv_root * inv_root
-    return inv_root * scaled - stream * cubed * jnp.mean(scaled * stream, axis=-1, keepdims=True)
-
-
 def passed_along(block, axis, by):
     length = lax.axis_size(axis)
     pairs = [(i, i + by) for i in range(length) if 0 <= i + by < length]
@@ -667,67 +902,35 @@
     return lax.all_gather(own, ("shard", "rep"), axis=0, tiled=True)
 
 
-def layer_forward(stream_in, weights, cos_table, sin_table):
+def layer_forward(stream_in, weights, tables):
     w_q, w_kv, w_o, w_g, w_u, w_d, gains_wide = weights
-    span_len, model_width = stream_in.shape
-    stream = stream_in.astype(F32)
-    inv_one = lax.rsqrt(jnp.mean(stream * stream, axis=-1, keepdims=True) + EPSILON)
-    normed = (stream * inv_one * gains_wide[0]).astype(BF16)
-    kv_rows = mm(normed, w_kv)
-    kv_width = kv_rows.shape[1] // 2
-    kv_rows = jnp.concatenate(
-        [rotate(kv_rows[:, :kv_width], cos_table, sin_table).astype(BF16), kv_rows[:, kv_width:].astype(BF16)], axis=1)
-    kv_all = lax.all_gather(kv_rows, "shard", axis=0, tiled=True)
-    key_all, value_all = kv_all[:, :kv_width], kv_all[:, kv_width:]
-    queries = rotate(mm(normed, w_q), cos_table, sin_table).astype(BF16)
-    attended, log_total = attn_fwd(queries, key_all, value_all, "shard")
-    middle = stream + mm(attended, w_o)
-    inv_two = lax.rsqrt(jnp.mean(middle * middle, axis=-1, keepdims=True) + EPSILON)
-    normed_two = (middle * inv_two * gains_wide[1]).astype(BF16)
-    gate_proj = mm(normed_two, w_g)
-    upward = mm(normed_two, w_u)
-    hidden = (jax.nn.silu(gate_proj) * upward).astype(BF16)
-    result = (middle + mm(hidden, w_d)).astype(BF16)
-    kept = (stream, inv_one, normed, queries, key_all, value_all, log_total, attended, middle, inv_two,
-            normed_two, gate_proj, upward, hidden)
+    cos_table, sin_table = tables
+    normed, queries, kv, attended, lse, middle = attend_block(
+        stream_in, gains_wide[0:1], cos_table, sin_table, w_q, w_kv, w_o, 3)
+    result, normed_two, hidden, gate_fac, up_fac = ffn_fwd(middle, gains_wide[1:2], w_g, w_u, w_d)
+    kept = {"stream": stream_in, "normed": normed, "queries": queries, "kv": kv, "attended": attended, "lse": lse,
+            "middle": middle, "normed_two": normed_two, "hidden": hidden, "gate_fac": gate_fac, "up_fac": up_fac}
     return result, kept
 
 
-def layer_backward(grad_bf, kept, weights, cos_table, sin_table):
+def layer_backward(grad_bf, kept, weights, tables):
     w_q, w_kv, w_o, w_g, w_u, w_d, gains_wide = weights
-    (stream, inv_one, normed, queries, key_all, value_all, log_total, attended, middle, inv_two,
-     normed_two, gate_proj, upward, hidden) = kept
-    grad_out = grad_bf.astype(F32)
-    grad_hidden = times_t(grad_bf, w_d)
-    sigmoid_gate = jax.nn.sigmoid(gate_proj)
-    grad_gate = (grad_hidden * upward * sigmoid_gate * (1.0 + gate_proj * (1.0 - sigmoid_gate))).astype(BF16)
-    grad_up = (grad_hidden * gate_proj * sigmoid_gate).astype(BF16)
-    grad_normed_two = times_t(grad_gate, w_g) + times_t(grad_up, w_u)
-    grad_middle = grad_out + norm_back(grad_normed_two, middle, inv_two, gains_wide[1])
-    gain_two = jnp.sum(grad_normed_two * middle * inv_two, axis=0)
-    grad_branch = grad_middle.astype(BF16)
-    grad_attended = times_t(grad_branch, w_o).astype(BF16)
-    grad_q_rot, grad_k_part, grad_v_part = attn_bwd(
-        queries, key_all, value_all, attended, grad_attended, log_total, "shard")
-    kv_width = grad_k_part.shape[1]
-    kv_sum = lax.psum_scatter(
-        jnp.concatenate([grad_k_part, grad_v_part], axis=1), "shard", scatter_dimension=0, tiled=True).astype(F32)
-    grad_query = rotate(grad_q_rot, cos_table, -sin_table).astype(BF16)
-    grad_key = rotate(kv_sum[:, :kv_width], cos_table, -sin_table).astype(BF16)
-    grad_value = kv_sum[:, kv_width:].astype(BF16)
-    grad_kv = jnp.concatenate([grad_key, grad_value], axis=1)
-    grad_normed = times_t(grad_query, w_q) + times_t(grad_kv, w_kv)
-    grad_stream = grad_middle + norm_back(grad_normed, stream, inv_one, gains_wide[0])
-    gain_one = jnp.sum(grad_normed * stream * inv_one, axis=0)
-    terms = (grad_query, grad_kv, grad_kv, grad_branch, grad_gate, grad_up, grad_bf)
-    return grad_stream, terms, jnp.stack([gain_one, gain_two])
+    cos_table, sin_table = tables
+    grad_gate, grad_up, grad_middle, grad_branch, gain_two = ffn_bwd(
+        grad_bf, kept["middle"], gains_wide[1:2], kept["gate_fac"], kept["up_fac"], w_g, w_u, w_d)
+    grad_query, grad_kv, grad_stream, grad_low, gain_one = attend_back(
+        grad_branch, grad_middle, kept["stream"], gains_wide[0:1], cos_table, -sin_table, kept["queries"], kept["kv"],
+        kept["attended"], kept["lse"], w_q, w_kv, w_o, 4)
+    terms = (grad_query, grad_kv, grad_branch, grad_gate, grad_up, grad_bf)
+    return grad_stream, grad_low, terms, jnp.concatenate([gain_one, gain_two], axis=0)
 
 
 def body(tokens, cotangent, live_counts, w_query, w_key, w_value, w_out, w_gate, w_up, w_down, norm_gains):
     section = lax.axis_index("section")
     slot_count, span_len, model_width = tokens.shape
     query_pos = lax.axis_index("shard") * span_len + jnp.arange(span_len, dtype=jnp.int32)
-    cos_table, sin_table = angles_for(query_pos)
+    cos_half, sin_half = angles_for(query_pos)
+    tables = (jnp.tile(cos_half, (1, 4)), jnp.tile(jnp.concatenate([-sin_half, sin_half], axis=1), (1, 2)))
     live_mask = (jnp.arange(slot_count) < live_counts[0]).astype(F32)
     gain_rows = jnp.pad(norm_gains[0], ((0, 14), (0, -norm_gains.shape[2] % (4 * LANES))))
     shards = [w_query[0], jnp.concatenate([w_key[0], w_value[0]], axis=1), w_out[0], gain_rows, w_gate[0], w_up[0]]
@@ -746,7 +949,7 @@
     for tick in range(ticks):
         slot_in = masked_in[tick] if tick < slot_count else zero_slot
         own_in = jnp.where(section == 0, slot_in, received)
-        result, kept = layer_forward(own_in, weights, cos_table, sin_table)
+        result, kept = layer_forward(own_in, weights, tables)
         received = passed_along(result, "section", 1)
         results.append(result)
         kept_all.append(kept)
@@ -757,8 +960,8 @@
     for tick in range(ticks):
         slot_cot = masked_cot[slot_count - 1 - tick] if tick < slot_count else zero_slot
         grad_bf = jnp.where(first, received, slot_cot)
-        grad_stream, terms, gain_grad = layer_backward(grad_bf, kept_all[ticks - 1 - tick], weights, cos_table, sin_table)
-        received = passed_along(grad_stream.astype(BF16), "section", -1)
+        grad_stream, grad_low, terms, gain_grad = layer_backward(grad_bf, kept_all[ticks - 1 - tick], weights, tables)
+        received = passed_along(grad_low, "section", -1)
         streams.append(grad_stream)
         term_list.append(terms)
         gain_total = gain_total + gain_grad
@@ -774,9 +977,9 @@
 
     gate_sum, up_sum, qkv_sum, out_sum, down_sum = reduce_weights(
         [
-            {"lefts": [turned(10), turned(2), turned(7)], "which": [0, 0, 1, 2], "z_first": False, "blocks": 1, "pace": 1,
-             "rights": [[by_tick(4)], [by_tick(5)], [by_tick(0), by_tick(1)], [by_tick(3)]]},
-            {"lefts": [turned(13)], "which": [0], "z_first": True, "blocks": 2, "pace": 3, "rights": [[by_tick(6)]]},
+            {"lefts": [turned("normed_two"), turned("normed"), turned("attended")], "which": [0, 0, 1, 2], "z_first": False, "blocks": 1, "pace": 1,
+             "rights": [[by_tick(3)], [by_tick(4)], [by_tick(0), by_tick(1)], [by_tick(2)]]},
+            {"lefts": [turned("hidden")], "which": [0], "z_first": True, "blocks": 2, "pace": 3, "rights": [[by_tick(5)]]},
         ],
         slot_count, 1, "reduce_weights")
     kv_width = w_key.shape[2]

time: 1800 us -> 1630 us (0.906)
  Pallas kernels: 972 us -> 1360 us
  matrix products: 387 us -> 0 us
  waiting for transfers between devices: 197 us -> 137 us
  other arithmetic: 116 us -> 58 us
  local copies, waits for them, and re-layouts: 82.3 us -> 41.6 us
    dot_general x36 -> x0, matrix products: 387 us -> none  [the longest x18 210 us: times_t(): lax.dot_general(left_rows, right_rows, (((1,), (1,)), ((), ())), preferre...]
    pallas_call x6 -> x12, Pallas kernels: 153 us -> 507 us  [the longest x3 168 us: attend_back(): pl.pallas_call(attend_back_kernel, in_specs=[vmem] * 10 + [anywhere] * 3,...]
    all_gather x3 -> x0, waiting for transfers between devices: 35.4 us -> none  [layer_forward(): kv_all = lax.all_gather(kv_rows, 'shard', axis=0, tiled=True)]
    pallas_call x1, Pallas kernels: 527 us -> 557 us  [reduce_weights(): pl.pallas_call(functools.partial(reduce_kernel, plans, slots), in_specs=[...]
    all_gather x1, waiting for transfers between devices: 54.5 us -> 77.3 us  [gather_rows(): return lax.all_gather(own, ('shard', 'rep'), axis=0, tiled=True)]
  transfers between devices with their start and end apart: 12 -> 6, of which waited for: 10 -> 5; matrix products, arithmetic and copies ran while one was open for 11% -> 4% of each run, Pallas kernels for 1% -> 37%
where the time goes in v4:
time: 1630 us
  Pallas kernels  1360 us (83%)
  waiting for transfers between devices  137 us (8%)
  other arithmetic  58 us (4%)
  local copies, waits for them, and re-layouts  41.6 us (3%)
    pallas_call x1, Pallas kernels, reduce_weights(): pl.pallas_call(functools.partial(reduce_kernel, plans, slots), in_specs=[...  557 us
    pallas_call x1, Pallas kernels, gather_weights(): pl.pallas_call(functools.partial(gather_kernel, splits), in_specs=[anywhe...  292 us
    pallas_call x3, Pallas kernels, attend_back(): pl.pallas_call(attend_back_kernel, in_specs=[vmem] * 10 + [anywhere] * 3,...  168 us
    pallas_call x3, Pallas kernels, attend_block(): pl.pallas_call(attend_block_kernel, in_specs=[vmem] * 4 + [anywhere] * 3,...  121 us
    pallas_call x3, Pallas kernels, ffn_bwd(): pl.pallas_call(ffn_bwd_kernel, grid=(ff // FF_TILE,), in_specs=[whole, wh...  113 us
    pallas_call x3, Pallas kernels, ffn_fwd(): pl.pallas_call(ffn_fwd_kernel, grid=(ff // FF_TILE,), in_specs=[whole, pl...  106 us
    all_gather x1, waiting for transfers between devices, gather_rows(): return lax.all_gather(own, ('shard', 'rep'), axis=0, tiled=True)  77.3 us
    ppermute x4, waiting for transfers between devices, passed_along(): return lax.ppermute(block, axis, pairs)  59.6 us
  transfers between devices with their start and end apart: 6, of which 5 were waited for; matrix products, arithmetic and copies ran while one was open for 4% of the time, Pallas kernels for 37%

profile of v4, /device:TPU:0, one launch (start us, length us, event | category | flops | bytes accessed | tf_op | source)
XLA Modules:
  0.0 1626.9 jit_solution(12104197824305940214)
XLA Ops:
  14.8 291.7 %gather_weights.1 = (bf16[2048,2048]{1,0:T(8,128)(2,1)}, bf16[2048,512]{1,0:T(8,128)(2,1)S(1)}, bf16[2048,2048]{1,0:T(8,128)(2,1)}, bf16[64,512]{1,0:T(8,128)(2,...) custom-call(bf16[512,2048]{1,0:T(8,128)(2,1)S(1)} %bitcast.78, ...), custom_call_target="tpu_custom_call" | custom-call | bytes 260308992 | tf_op jit(solution)/shard_map/gather_weights/pallas_call | solution.py:461
  314.2 4.2 multiply_convert_fusion
  321.1 41.4 %attend_block.3 = (bf16[256,2048]{1,0:T(8,128)(2,1)}, bf16[256,2048]{1,0:T(8,128)(2,1)}, bf16[4,256,512]{2,1,0:T(8,128)(2,1)}, bf16[256,2048]{1,0:T(8,128)(2,1)}...) custom-call(bf16[256,2048]{1,0:T(8,128)(2,1)} %get-tuple-element.182.x_ref, f32[1,2048]{1,0:T(1,128)} %bitcast.100, ...), custom_call_target="tpu_custom_call" | custom-call | flops 6979321856 | bytes 18874368 | tf_op jit(solution)/shard_map/attend_block/pallas_call | solution.py:705
  362.5 77.3 %all-gather.2.cloned.1.call-done.w_d = bf16[5632,2048]{1,0:T(8,128)(2,1)} async-done(((bf16[352,2048]{1,0:T(8,128)(2,1)}), bf16[5632,2048]{1,0:T(8,128)(2,1)}) %all-gather.2.cloned.1.call-update) | async-done | bytes 23068688 | tf_op jit(solution)/shard_map/all_gather | solution.py:902
  439.8 35.2 %ffn_fwd.3 = (bf16[256,2048]{1,0:T(8,128)(2,1)}, bf16[256,2048]{1,0:T(8,128)(2,1)}, bf16[256,5632]{1,0:T(8,128)(2,1)}, bf16[256,5632]{1,0:T(8,128)(2,1)}, bf16[256,5632]{1,0:T(8,128)(2,1)}) custom-call(f32[256,2048]{1,0:T(8,128)} %get-tuple-element.90.mid_ref, f32[1,2048]{1,0:T(1,128)} %bitcast.89, bf16[2048,5632]{1,0:T(8,128)(2,1)} %get-tuple-element.91.w_g, ...), custom_call_target="tpu_custom_call" | custom-call | flops 17716740096 | bytes 69206016 | tf_op jit(solution)/shard_map/ffn_fwd/pallas_call | solution.py:522
  475.0 3.6 collective-permute-start
  478.6 22.7 %collective-permute-done = bf16[256,2048]{1,0:T(8,128)(2,1)S(1)} collective-permute-done((bf16[256,2048]{1,0:T(8,128)(2,1)}, bf16[256,2048]{1,0:T(8,128)(2,1)S(1)}, u32[]{:S(2)}, u32[]{:S(2)}) %collective-permute-start) | collective-permute-done | bytes 1048608 | tf_op jit(solution)/shard_map/ppermute | solution.py:895
  502.4 31.9 %attend_block.4 = (bf16[256,2048]{1,0:T(8,128)(2,1)}, bf16[256,2048]{1,0:T(8,128)(2,1)}, bf16[4,256,512]{2,1,0:T(8,128)(2,1)}, bf16[256,2048]{1,0:T(8,128)(2,1)}...) custom-call(bf16[256,2048]{1,0:T(8,128)(2,1)} %fusion.2.x_ref, f32[1,2048]{1,0:T(1,128)} %bitcast.101, f32[256,128]{1,0:T(8,128)} %copy.48.cos_ref, ...), custom_call_target="tpu_custom_call" | custom-call | flops 6979321856 | bytes 18874368 | tf_op jit(solution)/shard_map/attend_block/pallas_call | solution.py:705
  534.3 35.2 %ffn_fwd.4 = (bf16[256,2048]{1,0:T(8,128)(2,1)}, bf16[256,2048]{1,0:T(8,128)(2,1)}, bf16[256,5632]{1,0:T(8,128)(2,1)}, bf16[256,5632]{1,0:T(8,128)(2,1)}, bf16[256,5632]{1,0:T(8,128)(2,1)}) custom-call(f32[256,2048]{1,0:T(8,128)} %get-tuple-element.95.mid_ref, f32[1,2048]{1,0:T(1,128)} %bitcast.90, bf16[2048,5632]{1,0:T(8,128)(2,1)} %get-tuple-element.91.w_g, ...), custom_call_target="tpu_custom_call" | custom-call | flops 17716740096 | bytes 69206016 | tf_op jit(solution)/shard_map/ffn_fwd/pallas_call | solution.py:522
  569.6 5.3 collective-permute-start.1
  575.5 3.1 copy.58
  578.6 4.6 copy.59
  583.2 12.0 collective-permute-done.1
  596.3 47.4 %attend_block.5 = (bf16[256,2048]{1,0:T(8,128)(2,1)}, bf16[256,2048]{1,0:T(8,128)(2,1)}, bf16[4,256,512]{2,1,0:T(8,128)(2,1)}, bf16[256,2048]{1,0:T(8,128)(2,1)}...) custom-call(bf16[256,2048]{1,0:T(8,128)(2,1)} %broadcast_select_fusion.9.x_ref, f32[1,2048]{1,0:T(1,128)} %bitcast.102, ...), custom_call_target="tpu_custom_call" | custom-call | flops 6979321856 | bytes 18874368 | tf_op jit(solution)/shard_map/attend_block/pallas_call | solution.py:705
  645.4 3.9 copy.63.refs_1_
  649.4 35.2 %ffn_fwd.5 = (bf16[256,2048]{1,0:T(8,128)(2,1)}, bf16[256,2048]{1,0:T(8,128)(2,1)}, bf16[256,5632]{1,0:T(8,128)(2,1)}, bf16[256,5632]{1,0:T(8,128)(2,1)}, bf16[256,5632]{1,0:T(8,128)(2,1)}) custom-call(f32[256,2048]{1,0:T(8,128)} %get-tuple-element.97.mid_ref, f32[1,2048]{1,0:T(1,128)} %bitcast.91, bf16[2048,5632]{1,0:T(8,128)(2,1)} %get-tuple-element.91.w_g, ...), custom_call_target="tpu_custom_call" | custom-call | flops 17716740096 | bytes 69206016 | tf_op jit(solution)/shard_map/ffn_fwd/pallas_call | solution.py:522
  684.6 4.6 copy.61
  689.2 37.4 %ffn_bwd.3 = (bf16[256,5632]{1,0:T(8,128)(2,1)}, bf16[256,5632]{1,0:T(8,128)(2,1)}, f32[256,2048]{1,0:T(8,128)}, bf16[256,2048]{1,0:T(8,128)(2,1)}, f32[1,2048]{1,0:T(1,128)}) custom-call(bf16[256,2048]{1,0:T(8,128)(2,1)} %get-tuple-element.181.grad_ref.refs_19_, f32[256,2048]{1,0:T(8,128)} %get-tuple-element.97.mid_ref, f32[1,2048]{1,0:T(1,128)} %bitcast.92, ...), custom_call_target="tpu_custom_call" | custom-call | flops 17716740096 | bytes 69206016 | tf_op jit(solution)/shard_map/ffn_bwd/pallas_call | solution.py:573
  726.6 58.3 %attend_back.3 = (bf16[256,2048]{1,0:T(8,128)(2,1)}, bf16[256,512]{1,0:T(8,128)(2,1)}, f32[256,2048]{1,0:T(8,128)}, bf16[256,2048]{1,0:T(8,128)(2,1)}, f32[1,2048]{1,0:T(1,128)}) custom-call(bf16[256,2048]{1,0:T(8,128)(2,1)} %get-tuple-element.101.da_ref.refs_16_, f32[256,2048]{1,0:T(8,128)} %get-tuple-element.102.dmid_ref, ...), custom_call_target="tpu_custom_call" | custom-call | flops 10200547328 | bytes 18874368 | tf_op jit(solution)/shard_map/attend_back/pallas_call | solution.py:856
  790.0 3.1 broadcast_select_fusion.1
  801.4 7.9 collective-permute-done.2
  811.6 37.5 %ffn_bwd.4 = (bf16[256,5632]{1,0:T(8,128)(2,1)}, bf16[256,5632]{1,0:T(8,128)(2,1)}, f32[256,2048]{1,0:T(8,128)}, bf16[256,2048]{1,0:T(8,128)(2,1)}, f32[1,2048]{1,0:T(1,128)}) custom-call(bf16[256,2048]{1,0:T(8,128)(2,1)} %fusion.grad_ref.refs_20_, f32[256,2048]{1,0:T(8,128)} %get-tuple-element.95.mid_ref, f32[1,2048]{1,0:T(1,128)} %bitcast.93, ...), custom_call_target="tpu_custom_call" | custom-call | flops 17716740096 | bytes 69206016 | tf_op jit(solution)/shard_map/ffn_bwd/pallas_call | solution.py:573
  849.1 54.9 %attend_back.4 = (bf16[256,2048]{1,0:T(8,128)(2,1)}, bf16[256,512]{1,0:T(8,128)(2,1)}, f32[256,2048]{1,0:T(8,128)}, bf16[256,2048]{1,0:T(8,128)(2,1)}, f32[1,2048]{1,0:T(1,128)}) custom-call(bf16[256,2048]{1,0:T(8,128)(2,1)} %get-tuple-element.110.da_ref.refs_17_, f32[256,2048]{1,0:T(8,128)} %get-tuple-element.111.dmid_ref, bf16[256,2048]{1,0:T(8,128)(2,1)} %fusion.2.x_ref, ...), custom_call_target="tpu_custom_call" | custom-call | flops 10200547328 | bytes 18874368 | tf_op jit(solution)/shard_map/attend_back/pallas_call | solution.py:856
  910.1 17.0 %collective-permute-done.3 = bf16[256,2048]{1,0:T(8,128)(2,1)S(1)} collective-permute-done((bf16[256,2048]{1,0:T(8,128)(2,1)}, bf16[256,2048]{1,0:T(8,128)(2,1)S(1)}, u32[]{:S(2)}, u32[]{:S(2)}) %collective-permute-start.3) | collective-permute-done | bytes 1048608 | tf_op jit(solution)/shard_map/ppermute | solution.py:895
  928.2 37.6 %ffn_bwd.5 = (bf16[256,5632]{1,0:T(8,128)(2,1)}, bf16[256,5632]{1,0:T(8,128)(2,1)}, f32[256,2048]{1,0:T(8,128)}, bf16[256,2048]{1,0:T(8,128)(2,1)}, f32[1,2048]{1,0:T(1,128)}) custom-call(bf16[256,2048]{1,0:T(8,128)(2,1)} %broadcast_select_fusion.8.grad_ref.refs_21_, f32[256,2048]{1,0:T(8,128)} %get-tuple-element.90.mid_ref, f32[1,2048]{1,0:T(1,128)} %bitcast.94, ...), custom_call_target="tpu_custom_call" | custom-call | flops 17716740096 | bytes 69206016 | tf_op jit(solution)/shard_map/ffn_bwd/pallas_call | solution.py:573
  965.9 54.6 %attend_back.5 = (bf16[256,2048]{1,0:T(8,128)(2,1)}, bf16[256,512]{1,0:T(8,128)(2,1)}, f32[256,2048]{1,0:T(8,128)}, bf16[256,2048]{1,0:T(8,128)(2,1)}, f32[1,2048]{1,0:T(1,128)}) custom-call(bf16[256,2048]{1,0:T(8,128)(2,1)} %get-tuple-element.119.da_ref.refs_18_, f32[256,2048]{1,0:T(8,128)} %get-tuple-element.120.dmid_ref, ...), custom_call_target="tpu_custom_call" | custom-call | flops 10200547328 | bytes 18874368 | tf_op jit(solution)/shard_map/attend_back/pallas_call | solution.py:856
  1022.8 557.2 %reduce_weights.1 = (bf16[512,5632]{1,0:T(8,128)(2,1)}, bf16[512,5632]{1,0:T(8,128)(2,1)}, bf16[512,2560]{1,0:T(8,128)(2,1)}, bf16[512,2048]{1,0:T(8,128)(2,1)}, bf16[1408,2048]{1,0:T(8,128)(2,1)}) custom-call(bf16[2048,512]{1,0:T(8,128)(2,1)} %copy.62.refs_0_, bf16[2048,512]{1,0:T(8,128)(2,1)} %copy.63.refs_1_, bf16[2048,512]{1,0:T(8,128)(2,1)} %copy.64.refs_2_, ...), custom_call_target="tpu_custom_call" | custom-call | flops 45097156608 | bytes 44040192 | tf_op jit(solution)/shard_map/reduce_weights/pallas_call | solution.py:350
  1580.0 4.3 bitcast_convert_fusion.4
  1588.4 5.9 bitcast_convert_fusion.2
  1594.4 5.9 bitcast_convert_fusion.1
  1600.3 6.0 bitcast_convert_fusion
  1612.5 7.3 psum.7
  (118 shorter events, 57.2 us)
Async XLA Ops:
  7.2 432.6 %all-gather.2.cloned.1.call-start = ((), (), s32[]{:S(2)}) async-start(), calls=%async_computation.1 | async-start | bytes 24510464 | tf_op jit(solution)/shard_map/all_gather | solution.py:902
  9.0 2.6 copy-start
  310.4 1301.0 %reduce-scatter.4.cloned.1.call-start = ((), (), s32[]{:S(2)}) async-start(), calls=%async_computation.2 | async-start | bytes 1310720
  475.0 26.3 %collective-permute-start = (bf16[256,2048]{1,0:T(8,128)(2,1)}, bf16[256,2048]{1,0:T(8,128)(2,1)S(1)}, u32[]{:S(2)}, u32[]{:S(2)}) collective-permute-start(bf16[256,2048]{1,0:T(8,128)(2,1)} %get-tuple-element.94), channel_id=1, source_target_pairs={{0,16},{1,17},{2,18},{3,19},{4,20},{5,21},{6,22},{7,23},{8,24},{9,... | collective-permute-start | bytes 3145736 | tf_op jit(solution)/shard_map/ppermute | solution.py:895
  534.3 40.5 %copy-start.24 = (f32[256,128]{1,0:T(8,128)S(1)}, f32[256,128]{1,0:T(8,128)}, u32[]{:S(2)}) copy-start(f32[256,128]{1,0:T(8,128)} %copy.49.sin_ref) | copy-start | bytes 393220
  569.6 25.7 %collective-permute-start.1 = (bf16[256,2048]{1,0:T(8,128)(2,1)}, bf16[256,2048]{1,0:T(8,128)(2,1)}, u32[]{:S(2)}, u32[]{:S(2)}) collective-permute-start(bf16[256,2048]{1,0:T(8,128)(2,1)} %get-tuple-element.96), channel_id=1, source_target_pairs={{0,16},{1,17},{2,18},{3,19},{4,20},{5,21},{6,22},{7,23},{8,24},{9,... | collective-permute-start | bytes 3145736 | tf_op jit(solution)/shard_map/ppermute | solution.py:895
  596.3 47.4 %copy-start.21 = (bf16[256,2048]{1,0:T(8,128)(2,1)S(1)}, bf16[256,2048]{1,0:T(8,128)(2,1)}, u32[]{:S(2)}) copy-start(bf16[256,2048]{1,0:T(8,128)(2,1)} %get-tuple-element.131) | copy-start | bytes 3145732
  596.3 47.4 %copy-start.23 = (bf16[256,2048]{1,0:T(8,128)(2,1)S(1)}, bf16[256,2048]{1,0:T(8,128)(2,1)}, u32[]{:S(2)}) copy-start(bf16[256,2048]{1,0:T(8,128)(2,1)} %get-tuple-element.132) | copy-start | bytes 3145732
  726.6 59.9 %copy-start.16 = (bf16[256,2048]{1,0:T(8,128)(2,1)S(1)}, bf16[256,2048]{1,0:T(8,128)(2,1)}, u32[]{:S(2)}) copy-start(bf16[256,2048]{1,0:T(8,128)(2,1)} %get-tuple-element.123.attended_ref) | copy-start | bytes 3145732
  726.6 59.9 %copy-start.17 = (bf16[256,2048]{1,0:T(8,128)(2,1)S(1)}, bf16[256,2048]{1,0:T(8,128)(2,1)}, u32[]{:S(2)}) copy-start(bf16[256,2048]{1,0:T(8,128)(2,1)} %get-tuple-element.114.attended_ref) | copy-start | bytes 3145732
  784.9 24.4 %collective-permute-start.2 = (bf16[256,2048]{1,0:T(8,128)(2,1)}, bf16[256,2048]{1,0:T(8,128)(2,1)}, u32[]{:S(2)}, u32[]{:S(2)}) collective-permute-start(bf16[256,2048]{1,0:T(8,128)(2,1)} %get-tuple-element.107), channel_id=1, source_target_pairs={{16,0},{17,1},{18,2},{19,3},{20,4},{21,5},{22,6},{23,7},{24,8},{25... | collective-permute-start | bytes 3145736 | tf_op jit(solution)/shard_map/ppermute | solution.py:895
  786.5 2.6 copy-start.5
  786.7 3.3 copy-start.4
  793.4 2.6 copy-start.11
  799.8 9.4 copy-start.9
  849.1 58.0 %copy-start.7 = (bf16[256,5632]{0,1:T(8,128)(2,1)S(1)}, bf16[256,5632]{0,1:T(8,128)(2,1)}, u32[]{:S(2)}) copy-start(bf16[256,5632]{0,1:T(8,128)(2,1)} %get-tuple-element.161) | copy-start | bytes 8650756
  904.0 3.1 copy-start.6
  904.0 23.1 %collective-permute-start.3 = (bf16[256,2048]{1,0:T(8,128)(2,1)}, bf16[256,2048]{1,0:T(8,128)(2,1)S(1)}, u32[]{:S(2)}, u32[]{:S(2)}) collective-permute-start(bf16[256,2048]{1,0:T(8,128)(2,1)} %get-tuple-element.116), channel_id=1, source_target_pairs={{16,0},{17,1},{18,2},{19,3},{20,4},{21,5},{22,6},{23,7},{24,8},{25... | collective-permute-start | bytes 3145736 | tf_op jit(solution)/shard_map/ppermute | solution.py:895
  965.9 54.6 %copy-start.25 = (f32[1,2048]{1,0:T(1,128)S(1)}, f32[1,2048]{1,0:T(1,128)}, u32[]{:S(2)}) copy-start(f32[1,2048]{1,0:T(1,128)} %get-tuple-element.155) | copy-start | bytes 24580
  965.9 54.6 %copy-start.26 = (f32[1,2048]{1,0:T(1,128)S(1)}, f32[1,2048]{1,0:T(1,128)}, u32[]{:S(2)}) copy-start(f32[1,2048]{1,0:T(1,128)} %get-tuple-element.154) | copy-start | bytes 24580
  965.9 54.6 %copy-start.27 = (f32[1,2048]{1,0:T(1,128)S(1)}, f32[1,2048]{1,0:T(1,128)}, u32[]{:S(2)}) copy-start(f32[1,2048]{1,0:T(1,128)} %get-tuple-element.157) | copy-start | bytes 24580
  965.9 54.6 %copy-start.28 = (f32[1,2048]{1,0:T(1,128)S(1)}, f32[1,2048]{1,0:T(1,128)}, u32[]{:S(2)}) copy-start(f32[1,2048]{1,0:T(1,128)} %get-tuple-element.156) | copy-start | bytes 24580
  965.9 54.6 %copy-start.29 = (f32[1,2048]{1,0:T(1,128)S(1)}, f32[1,2048]{1,0:T(1,128)}, u32[]{:S(2)}) copy-start(f32[1,2048]{1,0:T(1,128)} %get-tuple-element.159) | copy-start | bytes 24580
  1580.0 4.3 copy-start.12
  1584.3 4.1 copy-start.10
  1584.3 10.1 slice-start.2
  1588.4 5.9 slice-start.3
  1588.4 11.9 slice-start
  1594.4 5.9 slice-start.1
  1600.3 6.0 copy-start.13
  1600.3 6.0 copy-start.14
  1600.3 6.0 copy-start.15
  (8 other events, 13.8 us)
Sparse Core Ops, SparseCore 0:
  310.6 129.2 all-gather.1
  1022.9 58.9 reduce-scatter.3

commit v5 on v4

--- a/solution.py
+++ b/solution.py
@@ -19,7 +19,6 @@
 
 
 MESH_IDS = pl.DeviceIdType.MESH
-DELAY = 3
 LANES = 128
 BUFS = 26
 
@@ -28,14 +27,16 @@
     return pltpu.make_async_remote_copy(src, dst, send_sem, recv_sem, device_id=peer, device_id_type=MESH_IDS)
 
 
-def reduce_stages(z_first, blocks, segments, place, a_ref, b_ref, bufs):
+def reduce_stages(kind, blocks, delay, segments, place, a_ref, b_ref, bufs):
     n, me, rep, right, core_peer, y_peer = place
     own_core, own_y = lax.rem(rep, 2), rep // 2
+    paired = kind == "pair"
     (send_c, own, land_c, keep, send_y, land_y, send_z, land_z, send_f,
      sc_sem, rc_sem, cr_c, sy_sem, ry_sem, cr_y, sz_sem, rz_sem, ly_sem, sfy_sem, sfc_sem,
      rfy_sem, rfc_sem, sfw_sem, rfw_sem) = bufs
     rows = own.shape[2]
     depth = land_z.shape[1]
+    span = a_ref.shape[3]
     items = b_ref.shape[2] // LANES * blocks
     starts = [first for _, _, first in segments]
     ends = starts[1:] + [items // blocks]
@@ -82,29 +83,33 @@
 
     def stage_zero(a, s, p):
         dest = lax.rem(me + 2 * n - 1 - s, n)
-        row = pl.multiple_of((dest * blocks + lax.rem(p, blocks)) * rows, 16)
+        row = pl.ds(pl.multiple_of((dest * blocks + lax.rem(p, blocks)) * rows, 16), rows)
         which = 0
         for (_, index, first) in segments[1:]:
             which = jnp.where(p // blocks >= first, index, which)
-        block = a_ref[which, pl.ds(row, rows), :]
         column = pl.ds(pl.multiple_of(p // blocks * LANES, LANES), LANES)
-        for y in range(2):
-            send_c[a, y] = mm(block, b_ref[2 * y + 1 - own_core, :, column]).astype(BF16)
+
+        def product(r):
+            total = None
+            for k in range(a_ref.shape[1]):
+                term = mm(a_ref[which, k, row, :], b_ref[r, k * span:(k + 1) * span, column])
+                total = term if total is None else total + term
+            return total
+        tiles = range(1 if paired else 2)
+        for y in tiles:
+            send_c[a, y] = product(2 * y + 1 - own_core).astype(BF16)
 
         @pl.when(p >= 1)
         def _():
             pl.semaphore_wait(cr_c.at[s], 1)
         c_copy(a, s).start()
-        for y in range(2):
-            own[a, y] = mm(block, b_ref[2 * y + own_core, :, column])
+        for y in tiles:
+            own[a, y] = product(2 * y + own_core)
 
     def credit(sem, s, p, peer):
         @pl.when(p + 1 < items)
         def _():
             pl.semaphore_signal(sem.at[s], inc=1, device_id=peer, device_id_type=MESH_IDS)
-
-    def start_y(a, s, p):
-        y_copy(a, s).start()
 
     def finish(a, p, total):
         send_f[a] = total.astype(BF16)
@@ -114,6 +119,27 @@
             f_core(a, p, spot).start()
             f_local(a, spot).start()
         each_segment(p, send)
+
+    def go_round(a, s, p, ref):
+        @pl.when(s > 0)
+        def _():
+            z_copy(a, s - 1, p).wait_recv()
+            ref[...] = ref[...] + land_z[s - 1, lax.rem(p, depth)].astype(F32)
+
+        @pl.when(s < n - 1)
+        def _():
+            send_z[a] = ref[...].astype(BF16)
+            z_copy(a, s, p).start()
+
+        @pl.when(s == n - 1)
+        def _():
+            finish(a, p, ref[...])
+
+    def stage_one_pair(a, s, p):
+        c_copy(a, s).wait()
+        own[a, 0] = own[a, 0] + land_c[s, 0].astype(F32)
+        credit(cr_c, s, p, core_peer)
+        go_round(a, s, p, own.at[a, 0])
 
     def stage_one_y(a, s, p):
         c_copy(a, s).wait()
@@ -130,64 +156,12 @@
         y_copy(a, s).wait()
         keep[a] = keep[a] + land_y[s].astype(F32)
         credit(cr_y, s, p, y_peer)
-
-        @pl.when(s > 0)
-        def _():
-            z_copy(a, s - 1, p).wait_recv()
-            keep[a] = keep[a] + land_z[s - 1, lax.rem(p, depth)].astype(F32)
-
-        @pl.when(s < n - 1)
-        def _():
-            send_z[a] = keep[a].astype(BF16)
-            z_copy(a, s, p).start()
-
-        @pl.when(s == n - 1)
-        def _():
-            finish(a, p, keep[a])
-
-    def stage_one_z(a, s, p):
-        c_copy(a, s).wait()
-        for y in range(2):
-            own[a, y] = own[a, y] + land_c[s, y].astype(F32)
-        credit(cr_c, s, p, core_peer)
-
-        @pl.when(s > 0)
-        def _():
-            z_copy(a, s - 1, p).wait_recv()
-            for y in range(2):
-                own[a, y] = own[a, y] + land_z[s - 1, lax.rem(p, depth), y].astype(F32)
-
-        @pl.when(s < n - 1)
-        def _():
-            send_z[a] = own[a].astype(BF16)
-            z_copy(a, s, p).start()
-
-        @pl.when(s == n - 1)
-        def _():
-            send_y[a] = own[a, 1 - own_y].astype(BF16)
-
-            @pl.when(p >= 1)
-            def _():
-                pl.semaphore_wait(cr_y.at[0], 1)
-            y_copy(a, 0).start()
-            keep[a] = own[a, own_y]
-
-    def stage_two_z(a, s, p):
+        go_round(a, s, p, keep.at[a])
+
+    def turn_over(a, s, p):
         @pl.when(s < n - 1)
         def _():
             z_copy(a, s, p).wait_send()
-
-        @pl.when(s == n - 1)
-        def _():
-            y_copy(a, 0).wait()
-            finish(a, p, keep[a] + land_y[0].astype(F32))
-            credit(cr_y, 0, p, y_peer)
-
-    def stage_three(a, s, p):
-        if not z_first:
-            @pl.when(s < n - 1)
-            def _():
-                z_copy(a, s, p).wait_send()
 
         @pl.when(s == n - 1)
         def _():
@@ -198,7 +172,7 @@
                 f_turn(a, p, spot).start()
             each_segment(p, turn)
 
-    def stage_four(a, s, p):
+    def end_of(a, s, p):
         @pl.when(s == n - 1)
         def _():
             def end(spot):
@@ -206,9 +180,49 @@
                 f_turn(a, p, spot).wait()
             each_segment(p, end)
 
-    fns = (stage_zero, stage_one_z if z_first else stage_one_y, stage_two_z if z_first else stage_two_y,
-           stage_three, stage_four)
-    return items, fns
+    if paired:
+        return items, (stage_zero, stage_one_pair, turn_over, end_of)
+    return items, (stage_zero, stage_one_y, stage_two_y, turn_over, end_of)
+
+
+def gain_steps(place, gain_ref, out_ref, total, land_c, land_y, land_z, sends, lands):
+    n, me, _, _, core_peer, y_peer = place
+    chunk = out_ref.shape[1]
+
+    def over_core():
+        return remote(total, land_c, sends.at[0], lands.at[0], core_peer)
+
+    def over_y():
+        return remote(total, land_y, sends.at[1], lands.at[1], y_peer)
+
+    def over_z(d):
+        dest = lax.rem(me + d, n)
+        part = total.at[:, pl.ds(pl.multiple_of(dest * chunk, LANES), chunk)]
+        return remote(part, land_z.at[d - 1], sends.at[d + 1], lands.at[d + 1], {"shard": dest})
+
+    def begin():
+        total[...] = gain_ref[...]
+        over_core().start()
+
+    def add_core():
+        over_core().wait()
+        total[...] = total[...] + land_c[...]
+        over_y().start()
+
+    def add_y():
+        over_y().wait()
+        total[...] = total[...] + land_y[...]
+        for d in range(1, n):
+            over_z(d).start()
+
+    def add_z():
+        result = total[:, pl.ds(pl.multiple_of(me * chunk, LANES), chunk)]
+        for d in range(1, n):
+            over_z(d).wait()
+            result = result + land_z[d - 1]
+        out_ref[...] = result
+
+    return ((3, begin), (30, add_core), (60, add_y), (90, add_z))
 
 
 def reduce_kernel(streams, slots, *refs):
@@ -217,20 +231,25 @@
     rep = lax.axis_index("rep")
     section = lax.axis_index("section")
     right = {"shard": lax.rem(me + 1, n)}
-    left = {"shard": lax.rem(me + n - 1, n)}
     core_peer = {"rep": rep + 1 - 2 * lax.rem(rep, 2)}
     y_peer = {"rep": rep + 2 - 4 * (rep // 2)}
     place = (n, me, rep, right, core_peer, y_peer)
 
     refs = list(refs)
-    lefts = [[refs.pop(0) for _ in stream["lefts"]] for stream in streams]
-    rights = [[[[refs.pop(0) for _ in range(slots + 1)] for _ in segment] for segment in stream["rights"]] for stream in streams]
+    gain_ref = refs.pop(0)
+
+    def taken(tree):
+        return [taken(x) for x in tree] if isinstance(tree, list) else refs.pop(0)
+    lefts = [taken(stream["lefts"]) for stream in streams]
+    rights = [taken(stream["rights"]) for stream in streams]
     outs = [[refs.pop(0) for _ in stream["rights"]] for stream in streams]
+    gain_out = refs.pop(0)
     per = [[refs.pop(0) for _ in range(BUFS)] for _ in streams]
     load_sem = refs.pop(0)
+    timed = gain_steps(place, gain_ref, gain_out, *refs)
 
     barrier = pltpu.get_barrier_semaphore()
-    for peer in (left, right, core_peer, y_peer):
+    for peer in [{"shard": lax.rem(me + d, n)} for d in range(1, n)] + [core_peer, y_peer]:
         pl.semaphore_signal(barrier, inc=1, device_id=peer, device_id_type=MESH_IDS)
 
     def load_all(at_section):
@@ -239,12 +258,31 @@
         def load(src, dst):
             loads.append(pltpu.make_async_copy(src, dst, load_sem.at[len(loads)]))
             loads[-1].start()
-        for left_refs, right_refs, bufs in zip(lefts, rights, per):
+
+        def tick_of(ticks, j):
+            return ticks[slots - j if at_section == 0 else slots - 1 - j]
+        for stream, left_refs, right_refs, bufs in zip(streams, lefts, rights, per):
             a_ref, b_ref = bufs[0], bufs[1]
-            for k, src in enumerate(left_refs):
-                load(src, a_ref.at[k])
+            for k, groups in enumerate(left_refs):
+                for g, ticks in enumerate(groups):
+                    for j in range(slots):
+                        load(tick_of(ticks, j), a_ref.at[k, g * slots + j])
             base = 0
             for segment in right_refs:
+                if stream["kind"] == "pair":
+                    mine, other = segment
+                    quarter = mine[0].shape[1] // 4
+                    for c in range(2):
+                        column = pl.ds(pl.multiple_of((rep // 2 * 2 + c) * quarter, LANES), quarter)
+                        for g, ticks in enumerate((mine, other)):
+                            for j in range(slots):
+                                tick = tick_of(ticks, j)
+                                span = tick.shape[0]
+                                at = (g * slots + j) * span
+                                load(tick.at[:, column] if g == 0 else tick.at[:, 2 * base + c * quarter:2 * base + (c + 1) * quarter],
+                                     b_ref.at[c, at:at + span, base:base + quarter])
+                    base += quarter
+                    continue
                 quarter = sum(ticks[0].shape[1] for ticks in segment) // 4
                 for r in range(4):
                     at = 0
@@ -253,7 +291,7 @@
                         lo, hi = max(r * quarter, at), min((r + 1) * quarter, at + width)
                         if lo < hi:
                             for j in range(slots):
-                                tick = ticks[slots - j if at_section == 0 else slots - 1 - j]
+                                tick = tick_of(ticks, j)
                                 span = tick.shape[0]
                                 load(tick.at[:, lo - at:hi - at],
                                      b_ref.at[r, j * span:(j + 1) * span, base + lo - r * quarter:base + hi - r * quarter])
@@ -266,98 +304,110 @@
         @pl.when(section == value)
         def _(value=value):
             load_all(value)
-    pl.semaphore_wait(barrier, 4)
+    pl.semaphore_wait(barrier, n + 1)
 
     work, last = [], 0
     for stream, segs, bufs in zip(streams, outs, per):
+        delay = stream["delay"]
         items, fns = reduce_stages(
-            stream["z_first"], stream["blocks"],
+            stream["kind"], stream["blocks"], delay,
             [(out, index, first) for out, index, first in zip(segs, stream["which"], stream["firsts"])],
             place, bufs[0], bufs[1], bufs[2:])
         pace = stream["pace"]
-        total = n * (items + n - 1)
-        work.append((pace, items, fns))
-        last = max(last, pace * (total + 4 * DELAY))
+        work.append((pace, delay, items, fns))
+        last = max(last, pace * (n * (items + n - 1) + (len(fns) - 1) * delay))
 
     def step(i, carry):
         for k in (4, 3, 2, 1, 0):
-            for pace, items, fns in work:
-                v = i // pace - DELAY * k
-                s = lax.rem(v + n * DELAY * 4, n)
+            for pace, delay, items, fns in work:
+                if k >= len(fns):
+                    continue
+                v = i // pace - delay * k
+                s = lax.rem(v + n * delay * 4, n)
                 p = (v - s) // n - s
                 fine = jnp.logical_and(jnp.logical_and(v >= 0, lax.rem(i, pace) == 0), jnp.logical_and(p >= 0, p < items))
 
                 @pl.when(fine)
-                def _(s=s, p=p, v=v, fn=fns[k]):
-                    fn(lax.rem(v, DELAY), s, p)
+                def _(s=s, p=p, v=v, fn=fns[k], delay=delay):
+                    fn(lax.rem(v, delay), s, p)
+        for at, fn in timed:
+            pl.when(i == at)(fn)
         return carry
 
     lax.fori_loop(0, last, step, 0)
 
 
-def reduce_weights(streams, slots, collective_id, name):
+def reduce_weights(gain, streams, slots, collective_id, name):
     n = lax.axis_size("shard")
     operands, out_shapes, scratch, flops, moved, plans, loads = [], [], [], 0, 0, [], 0
     dma, regular = pltpu.SemaphoreType.DMA, pltpu.SemaphoreType.REGULAR
-    for stream in streams:
-        operands += stream["lefts"]
-    for stream in streams:
+
+    def listed(tree):
+        if isinstance(tree, list):
+            return [listed(x) for x in tree]
+        operands.append(tree)
+        return None
+    left_plans = [listed(stream["lefts"]) for stream in streams]
+    right_plans = [listed(stream["rights"]) for stream in streams]
+    for stream, left_plan, right_plan in zip(streams, left_plans, right_plans):
+        paired = stream["kind"] == "pair"
+        blocks, delay = stream["blocks"], stream["delay"]
+        height, span = stream["lefts"][0][0][0].shape
+        height //= n
+        chunks = len(stream["lefts"][0]) * slots
         firsts, at = [], 0
-        tokens = stream["lefts"][0].shape[1]
-        height = stream["lefts"][0].shape[0] // n
-        loads += len(stream["lefts"])
         for segment in stream["rights"]:
-            width = 0
-            for ticks in segment:
-                operands += ticks
-                width += ticks[0].shape[1]
-                loads += 4 * slots
+            width = segment[0][0].shape[1] if paired else sum(ticks[0].shape[1] for ticks in segment)
             firsts.append(at)
             at += width // 4 // LANES
             out_shapes.append(jax.ShapeDtypeStruct((height, width), BF16))
-            flops += 2 * tokens * height * n * width
+            flops += 2 * span * slots * height * n * width
             moved += height * width * 4
-        z_first, blocks = stream["z_first"], stream["blocks"]
+            loads += 4 * slots * len(segment)
+        loads += len(stream["lefts"]) * chunks
         items = at * blocks
-        rows = height // blocks
-        pair = (2,) if z_first else ()
         depth = min(items, n + 2)
-        tile = (rows, LANES)
-        land_y = 1 if z_first else n
+        tile = (height // blocks, LANES)
+        both = 1 if paired else 2
+        few = (16, LANES)
         scratch += [
-            pltpu.VMEM((len(stream["lefts"]), height * n, tokens), BF16),
-            pltpu.VMEM((4, tokens, at * LANES), BF16),
-            pltpu.VMEM((DELAY, 2) + tile, BF16),
-            pltpu.VMEM((DELAY, 2) + tile, F32),
-            pltpu.VMEM((n, 2) + tile, BF16),
-            pltpu.VMEM((DELAY,) + tile, F32),
-            pltpu.VMEM((DELAY,) + tile, BF16),
-            pltpu.VMEM((land_y,) + tile, BF16),
-            pltpu.VMEM((DELAY,) + pair + tile, BF16),
-            pltpu.VMEM((n - 1, depth) + pair + tile, BF16),
-            pltpu.VMEM((DELAY,) + tile, BF16),
-            dma((DELAY,)), dma((n,)), regular((n,)),
-            dma((DELAY,)), dma((land_y,)), regular((land_y,)),
-            dma((DELAY,)), dma((n - 1, depth)),
-            dma((DELAY,)), dma((DELAY,)), dma((DELAY,)),
-            dma((items,)), dma((items,)), dma((DELAY,)), dma((items,)),
+            pltpu.VMEM((len(stream["lefts"]), chunks, height * n, span), BF16),
+            pltpu.VMEM((2 * both, chunks * span, at * LANES), BF16),
+            pltpu.VMEM((delay, both) + tile, BF16),
+            pltpu.VMEM((delay, both) + tile, F32),
+            pltpu.VMEM((n, both) + tile, BF16),
+            pltpu.VMEM((1,) + few if paired else (delay,) + tile, F32),
+            pltpu.VMEM((1,) + few if paired else (delay,) + tile, BF16),
+            pltpu.VMEM((1,) + few if paired else (n,) + tile, BF16),
+            pltpu.VMEM((delay,) + tile, BF16),
+            pltpu.VMEM((n - 1, depth) + tile, BF16),
+            pltpu.VMEM((delay,) + tile, BF16),
+            dma((delay,)), dma((n,)), regular((n,)),
+            dma((delay,)), dma((n,)), regular((n,)),
+            dma((delay,)), dma((n - 1, depth)),
+            dma((delay,)), dma((delay,)), dma((delay,)),
+            dma((items,)), dma((items,)), dma((delay,)), dma((items,)),
         ]
         plans.append({
-            "z_first": z_first, "blocks": blocks, "pace": stream["pace"], "which": tuple(stream["which"]), "firsts": tuple(firsts),
-            "lefts": [None] * len(stream["lefts"]), "rights": [[None] * len(segment) for segment in stream["rights"]]})
-    scratch.append(dma((loads,)))
+            "kind": stream["kind"], "blocks": blocks, "delay": delay, "pace": stream["pace"], "which": tuple(stream["which"]),
+            "firsts": tuple(firsts), "lefts": left_plan, "rights": right_plan})
+    chunk = gain.shape[1] // n
+    out_shapes.append(jax.ShapeDtypeStruct((gain.shape[0], chunk), F32))
+    scratch += [dma((loads,))] + [pltpu.VMEM(gain.shape, F32)] * 3
+    scratch += [pltpu.VMEM((n - 1, gain.shape[0], chunk), F32), dma((n + 1,)), dma((n + 1,))]
+    in_vmem = pl.BlockSpec(memory_space=pltpu.VMEM)
     anywhere = pl.BlockSpec(memory_space=pl.ANY)
     return pl.pallas_call(
         functools.partial(reduce_kernel, plans, slots),
-        in_specs=[anywhere] * len(operands),
-        out_specs=[anywhere] * len(out_shapes),
+        in_specs=[in_vmem] + [anywhere] * len(operands),
+        out_specs=[anywhere] * (len(out_shapes) - 1) + [in_vmem],
         out_shape=out_shapes,
         scratch_shapes=scratch,
         compiler_params=pltpu.CompilerParams(
             collective_id=collective_id, has_side_effects=True, vmem_limit_bytes=60 * 1024 * 1024),
         cost_estimate=pl.CostEstimate(flops=flops, bytes_accessed=moved, transcendentals=0),
         name=name,
-    )(*operands)
+    )(gain, *operands)
 
 
 def gather_kernel(splits, *refs):
@@ -488,7 +538,7 @@
     return lax.rsqrt(jnp.mean(rows * rows, axis=-1, keepdims=True) + EPSILON)
 
 
-def ffn_fwd_kernel(mid_ref, gain_ref, w_g, w_u, w_d, out_ref, normed_ref, hidden_ref, gate_fac, up_fac, acc):
+def ffn_fwd_kernel(mid_ref, gain_ref, w_g, w_u, w_d, out_ref, normed_turn, hidden_turn, gate_fac, up_fac, acc, normed_ref):
     step = pl.program_id(0)
 
     @pl.when(step == 0)
@@ -496,13 +546,15 @@
         mid = mid_ref[...]
         normed_ref[...] = (mid * inv_root_of(mid) * gain_ref[...]).astype(BF16)
         acc[...] = mid
+        for at in range(0, mid.shape[1], LANES):
+            normed_turn[at:at + LANES, :] = normed_ref[:, at:at + LANES].T
 
     gate = mm(normed_ref[...], w_g[...])
     up = mm(normed_ref[...], w_u[...])
     sig = jax.nn.sigmoid(gate)
     act = gate * sig
     hidden = (act * up).astype(BF16)
-    hidden_ref[...] = hidden
+    hidden_turn[...] = hidden.T
     up_fac[...] = act.astype(BF16)
     gate_fac[...] = (up * sig * (1.0 + gate * (1.0 - sig))).astype(BF16)
     acc[...] += mm(hidden, w_d[...])
@@ -523,9 +575,10 @@
         ffn_fwd_kernel,
         grid=(ff // FF_TILE,),
         in_specs=[whole, pl.BlockSpec((1, width), lambda i: (0, 0)), tall, tall, pl.BlockSpec((FF_TILE, width), lambda i: (i, 0))],
-        out_specs=[whole, whole, part, part, part],
-        out_shape=[jax.ShapeDtypeStruct((rows, width), BF16)] * 2 + [wide] * 3,
-        scratch_shapes=[pltpu.VMEM((rows, width), F32)],
+        out_specs=[whole, pl.BlockSpec((width, rows), lambda i: (0, 0)), pl.BlockSpec((FF_TILE, rows), lambda i: (i, 0)), part, part],
+        out_shape=[jax.ShapeDtypeStruct((rows, width), BF16), jax.ShapeDtypeStruct((width, rows), BF16),
+                   jax.ShapeDtypeStruct((ff, rows), BF16), wide, wide],
+        scratch_shapes=[pltpu.VMEM((rows, width), F32), pltpu.VMEM((rows, width), BF16)],
         compiler_params=pltpu.CompilerParams(vmem_limit_bytes=58 * 1024 * 1024),
         cost_estimate=pl.CostEstimate(flops=6 * rows * width * ff, bytes_accessed=6 * width * ff, transcendentals=rows * ff),
         name="ffn_fwd",
@@ -593,8 +646,8 @@
 
 
 def attend_block_kernel(x_ref, gain_ref, cos_ref, sin_ref, w_q, w_kv, w_o,
-                        normed_ref, q_ref, kv_ref, attended_ref, lse_ref, mid_ref,
-                        wq_ref, wkv_ref, wo_ref, q_turn, acc, top_ref, total_ref, land,
+                        normed_turn, q_ref, kv_ref, attended_turn, lse_ref, mid_ref,
+                        normed_ref, attended_ref, wq_ref, wkv_ref, wo_ref, q_turn, acc, top_ref, total_ref, land,
                         load_sem, send_sem, recv_sem):
     n = lax.axis_size("shard")
     me = lax.axis_index("shard")
@@ -680,7 +733,10 @@
     for pair in range(HEADS // 2):
         col = pair * LANES
         halves_t = [acc[col + k * HEAD:col + (k + 1) * HEAD, :] * total_ref[2 * pair + k:2 * pair + k + 1, :] for k in range(2)]
-        attended_ref[:, col:col + LANES] = jnp.concatenate(halves_t, axis=0).T.astype(BF16)
+        both_t = jnp.concatenate(halves_t, axis=0).astype(BF16)
+        attended_turn[col:col + LANES, :] = both_t
+        attended_ref[:, col:col + LANES] = both_t.T
+        normed_turn[col:col + LANES, :] = normed_ref[:, col:col + LANES].T
     for d in range(n):
         @pl.when(me >= d)
         def _(d=d):
@@ -707,14 +763,15 @@
         in_specs=[vmem] * 4 + [anywhere] * 3,
         out_specs=[vmem] * 6,
         out_shape=[
-            jax.ShapeDtypeStruct((rows, width), BF16),
+            jax.ShapeDtypeStruct((width, rows), BF16),
             jax.ShapeDtypeStruct((rows, width), BF16),
             jax.ShapeDtypeStruct((n, rows, kv_both), BF16),
-            jax.ShapeDtypeStruct((rows, width), BF16),
+            jax.ShapeDtypeStruct((width, rows), BF16),
             jax.ShapeDtypeStruct((HEADS, rows), F32),
             jax.ShapeDtypeStruct((rows, width), F32),
         ],
         scratch_shapes=[
+            pltpu.VMEM((rows, width), BF16), pltpu.VMEM((rows, width), BF16),
             pltpu.VMEM(w_q.shape, BF16), pltpu.VMEM(w_kv.shape, BF16), pltpu.VMEM(w_o.shape, BF16),
             pltpu.VMEM((width, rows), BF16), pltpu.VMEM((width, rows), F32),
             pltpu.VMEM((HEADS, rows), F32), pltpu.VMEM((HEADS, rows), F32),
@@ -728,7 +785,7 @@
     )(x, gain, cos_table, sin_table, w_q, w_kv, w_o)
 
 
-def attend_back_kernel(da_ref, dmid_ref, x_ref, gain_ref, cos_ref, sin_ref, q_ref, kv_ref, attended_ref, lse_ref, w_q, w_kv, w_o,
+def attend_back_kernel(da_ref, dmid_ref, x_ref, gain_ref, cos_ref, sin_ref, q_ref, kv_ref, attended_turn, lse_ref, w_q, w_kv, w_o,
                        dq_ref, dkv_ref, grad_ref, grad_low_ref, dgain_ref,
                        wq_ref, wkv_ref, wo_ref, do_ref, q_turn, do_turn, delta_ref, dq_acc, dkv_acc, dn_ref, send_kv, land_kv,
                        load_sem, send_sem, recv_sem):
@@ -762,11 +819,10 @@
         do_chunk = mm_t(da_ref[...], wo_ref[at:at + chunk, :]).astype(BF16)
         do_ref[:, at:at + chunk] = do_chunk
         do_turn[at:at + chunk, :] = do_chunk.T
-    for pair in range(HEADS // 2):
-        cols = slice(pair * LANES, (pair + 1) * LANES)
-        both = (attended_ref[:, cols].astype(F32) * do_ref[:, cols].astype(F32)).T
-        for k in range(2):
-            delta_ref[2 * pair + k:2 * pair + k + 1, :] = jnp.sum(both[k * HEAD:(k + 1) * HEAD, :], axis=0, keepdims=True)
+    for j in range(HEADS):
+        span = slice(j * HEAD, (j + 1) * HEAD)
+        both = attended_turn[span, :].astype(F32) * do_turn[span, :].astype(F32)
+        delta_ref[j:j + 1, :] = jnp.sum(both, axis=0, keepdims=True)
     dq_acc[...] = jnp.zeros_like(dq_acc)
     low_lane = lax.broadcasted_iota(jnp.int32, (rows, LANES), 1) < HEAD
     zero_rows = jnp.zeros((rows, LANES), BF16)
@@ -902,27 +958,40 @@
     return lax.all_gather(own, ("shard", "rep"), axis=0, tiled=True)
 
 
-def layer_forward(stream_in, weights, tables):
+Y_PAIRS = [(0, 2), (2, 0), (1, 3), (3, 1)]
+
+
+def halves_of(grad_gate, grad_up):
+    half = grad_gate.shape[1] // 2
+    at = (1 - lax.axis_index("rep") // 2) * half
+    parts = [lax.dynamic_slice_in_dim(term, at, half, 1) for term in (grad_gate, grad_up)]
+    return lax.ppermute(jnp.concatenate(parts, axis=1), "rep", Y_PAIRS)
+
+
+def layer_forward(stream_in, weights, tables, pending):
     w_q, w_kv, w_o, w_g, w_u, w_d, gains_wide = weights
     cos_table, sin_table = tables
     normed, queries, kv, attended, lse, middle = attend_block(
         stream_in, gains_wide[0:1], cos_table, sin_table, w_q, w_kv, w_o, 3)
+    middle, pending = lax.optimization_barrier((middle, pending))
     result, normed_two, hidden, gate_fac, up_fac = ffn_fwd(middle, gains_wide[1:2], w_g, w_u, w_d)
     kept = {"stream": stream_in, "normed": normed, "queries": queries, "kv": kv, "attended": attended, "lse": lse,
             "middle": middle, "normed_two": normed_two, "hidden": hidden, "gate_fac": gate_fac, "up_fac": up_fac}
-    return result, kept
-
-
-def layer_backward(grad_bf, kept, weights, tables):
+    return result, kept, pending
+
+
+def layer_backward(grad_bf, kept, weights, tables, pending):
     w_q, w_kv, w_o, w_g, w_u, w_d, gains_wide = weights
     cos_table, sin_table = tables
     grad_gate, grad_up, grad_middle, grad_branch, gain_two = ffn_bwd(
         grad_bf, kept["middle"], gains_wide[1:2], kept["gate_fac"], kept["up_fac"], w_g, w_u, w_d)
+    grad_branch, pending = lax.optimization_barrier((grad_branch, pending))
+    halves_out = halves_of(grad_gate, grad_up)
     grad_query, grad_kv, grad_stream, grad_low, gain_one = attend_back(
         grad_branch, grad_middle, kept["stream"], gains_wide[0:1], cos_table, -sin_table, kept["queries"], kept["kv"],
         kept["attended"], kept["lse"], w_q, w_kv, w_o, 4)
-    terms = (grad_query, grad_kv, grad_branch, grad_gate, grad_up, grad_bf)
-    return grad_stream, grad_low, terms, jnp.concatenate([gain_one, gain_two], axis=0)
+    terms = (grad_query, grad_kv, grad_branch, grad_gate, grad_up, grad_bf, halves_out)
+    return grad_stream, grad_low, terms, jnp.concatenate([gain_one, gain_two], axis=0), pending
 
 
 def body(tokens, cotangent, live_counts, w_query, w_key, w_value, w_out, w_gate, w_up, w_down, norm_gains):
@@ -940,16 +1009,18 @@
     gain_blocks = gains.reshape(-1, 16, gain_rows.shape[1])[:, :2, :norm_gains.shape[2]]
     gains_wide = gain_blocks.transpose(1, 0, 2).reshape(2, model_width).astype(F32)
     weights = (w_q, w_kv, w_o, w_g, w_u, w_d, gains_wide)
-    masked_in = (tokens.astype(F32) * live_mask[:, None, None]).astype(BF16)
-    masked_cot = (cotangent.astype(F32) * live_mask[:, None, None]).astype(BF16)
+    live_mask = live_mask.astype(BF16)
     zero_slot = jnp.zeros((span_len, model_width), BF16)
     ticks = slot_count + 1
-    results, kept_all = [], []
+    results, kept_all, others = [], [], []
+    pending = []
     received = zero_slot
     for tick in range(ticks):
-        slot_in = masked_in[tick] if tick < slot_count else zero_slot
+        slot_in = tokens[tick] * live_mask[tick] if tick < slot_count else zero_slot
         own_in = jnp.where(section == 0, slot_in, received)
-        result, kept = layer_forward(own_in, weights, tables)
+        result, kept, pending = layer_forward(own_in, weights, tables, pending)
+        others += pending
+        pending = [lax.ppermute(kept["normed_two"], "rep", Y_PAIRS)]
         received = passed_along(result, "section", 1)
         results.append(result)
         kept_all.append(kept)
@@ -958,9 +1029,12 @@
     received = zero_slot
     streams, term_list, gain_total = [], [], 0.0
     for tick in range(ticks):
-        slot_cot = masked_cot[slot_count - 1 - tick] if tick < slot_count else zero_slot
+        slot_cot = cotangent[slot_count - 1 - tick] * live_mask[slot_count - 1 - tick] if tick < slot_count else zero_slot
         grad_bf = jnp.where(first, received, slot_cot)
-        grad_stream, grad_low, terms, gain_grad = layer_backward(grad_bf, kept_all[ticks - 1 - tick], weights, tables)
+        grad_stream, grad_low, terms, gain_grad, pending = layer_backward(
+            grad_bf, kept_all[ticks - 1 - tick], weights, tables, pending)
+        others += pending
+        pending = [terms[6]]
         received = passed_along(grad_low, "section", -1)
         streams.append(grad_stream)
         term_list.append(terms)
@@ -968,23 +1042,29 @@
     grad_in = jnp.stack([
         jnp.where(first, streams[slot_count - j], streams[slot_count - 1 - j]) for j in range(slot_count)])
 
-    def turned(index):
-        picks = [jnp.where(first, kept_all[j][index], kept_all[j + 1][index]) for j in range(slot_count)]
-        return jnp.concatenate(picks, axis=0).T
+    others += pending
+    normed_others, half_others = others[ticks - 1::-1], others[ticks:]
+
+    def kept_by_tick(name):
+        return [kept_all[ticks - 1 - tick][name] for tick in range(ticks)]
 
     def by_tick(index):
         return [terms[index] for terms in term_list]
 
-    gate_sum, up_sum, qkv_sum, out_sum, down_sum = reduce_weights(
+    gate_sum, up_sum, qkv_sum, out_sum, down_sum, gain_sum = reduce_weights(
+        jnp.pad(gain_total, ((0, 6), (0, 0))),
         [
-            {"lefts": [turned("normed_two"), turned("normed"), turned("attended")], "which": [0, 0, 1, 2], "z_first": False, "blocks": 1, "pace": 1,
-             "rights": [[by_tick(3)], [by_tick(4)], [by_tick(0), by_tick(1)], [by_tick(2)]]},
-            {"lefts": [turned("hidden")], "which": [0], "z_first": True, "blocks": 2, "pace": 3, "rights": [[by_tick(5)]]},
+            {"kind": "pair", "blocks": 1, "pace": 1, "delay": 3, "which": [0, 0],
+             "lefts": [[kept_by_tick("normed_two"), normed_others]],
+             "rights": [[by_tick(3), half_others], [by_tick(4), half_others]]},
+            {"kind": "y", "blocks": 1, "pace": 2, "delay": 2, "which": [0, 1],
+             "lefts": [[kept_by_tick("normed")], [kept_by_tick("attended")]],
+             "rights": [[by_tick(0), by_tick(1)], [by_tick(2)]]},
+            {"kind": "y", "blocks": 2, "pace": 2, "delay": 2, "which": [0],
+             "lefts": [[kept_by_tick("hidden")]], "rights": [[by_tick(5)]]},
         ],
         slot_count, 1, "reduce_weights")
     kv_width = w_key.shape[2]
-    gain_part = lax.psum_scatter(gain_total, "shard", scatter_dimension=1, tiled=True)
-    gain_sum = lax.psum(gain_part, "rep")
     outs = (
         qkv_sum[:, :model_width],
         qkv_sum[:, model_width:model_width + kv_width],
@@ -993,7 +1073,7 @@
         gate_sum,
         up_sum,
         down_sum,
-        gain_sum,
+        gain_sum[:2],
     )
     return (acts[None], grad_in[None]) + tuple(out.astype(F32)[None] for out in outs)
 

time: 1630 us -> 1500 us (0.920)
  Pallas kernels: 1360 us -> 1220 us
  waiting for transfers between devices: 137 us -> 160 us
  local copies, waits for them, and re-layouts: 41.6 us -> 24.4 us
    pallas_call x1, Pallas kernels: 557 us -> 424 us  [reduce_weights(): pl.pallas_call(functools.partial(reduce_kernel, plans, slots), in_specs=[...]
    ppermute x4, waiting for transfers between devices: 59.6 us -> 80.2 us  [passed_along(): return lax.ppermute(block, axis, pairs)]
  transfers between devices with their start and end apart: 6 -> 11, of which waited for: 5 -> 5; matrix products, arithmetic and copies ran while one was open for 4% -> 2% of each run, Pallas kernels for 37% -> 19%
where the time goes in v5:
time: 1500 us; the launch traced here: 1490 us
  Pallas kernels  1220 us (81%)
  waiting for transfers between devices  160 us (11%)
  other arithmetic  46.9 us (3%)
  local copies, waits for them, and re-layouts  24.4 us (2%)
  starting transfers between devices  17.1 us (1%)
  between operations  15.4 us (1%)
    pallas_call x1, Pallas kernels, reduce_weights(): pl.pallas_call(functools.partial(reduce_kernel, plans, slots), in_specs=[...  424 us
    pallas_call x1, Pallas kernels, gather_weights(): pl.pallas_call(functools.partial(gather_kernel, splits), in_specs=[anywhe...  292 us
    pallas_call x3, Pallas kernels, attend_back(): pl.pallas_call(attend_back_kernel, in_specs=[vmem] * 10 + [anywhere] * 3,...  168 us
    pallas_call x3, Pallas kernels, attend_block(): pl.pallas_call(attend_block_kernel, in_specs=[vmem] * 4 + [anywhere] * 3,...  121 us
    pallas_call x3, Pallas kernels, ffn_bwd(): pl.pallas_call(ffn_bwd_kernel, grid=(ff // FF_TILE,), in_specs=[whole, wh...  112 us
    pallas_call x3, Pallas kernels, ffn_fwd(): pl.pallas_call(ffn_fwd_kernel, grid=(ff // FF_TILE,), in_specs=[whole, pl...  106 us
    ppermute x4, waiting for transfers between devices, passed_along(): return lax.ppermute(block, axis, pairs)  80.2 us
    all_gather x1, waiting for transfers between devices, gather_rows(): return lax.all_gather(own, ('shard', 'rep'), axis=0, tiled=True)  79.9 us
  transfers between devices with their start and end apart: 11, of which 5 were waited for; matrix products, arithmetic and copies ran while one was open for 2% of the time, Pallas kernels for 19%

profile of v5, /device:TPU:0, one launch (start us, length us, event | category | flops | bytes accessed | tf_op | source)
XLA Modules:
  0.0 1487.0 jit_solution(4193722018696477150)
XLA Ops:
  9.0 2.6 copy-done
  14.8 291.7 %gather_weights.1 = (bf16[2048,2048]{1,0:T(8,128)(2,1)}, bf16[2048,512]{1,0:T(8,128)(2,1)S(1)}, bf16[2048,2048]{1,0:T(8,128)(2,1)}, bf16[64,512]{1,0:T(8,128)(2,...) custom-call(bf16[512,2048]{1,0:T(8,128)(2,1)S(1)} %bitcast.67, ...), custom_call_target="tpu_custom_call" | custom-call | bytes 260308992 | tf_op jit(solution)/shard_map/gather_weights/pallas_call | solution.py:511
  307.9 2.8 constant_dynamic-slice_fusion.6
  314.3 4.1 select_bitcast_fusion.2
  318.4 41.2 %attend_block.3 = (bf16[2048,256]{1,0:T(8,128)(2,1)}, bf16[256,2048]{1,0:T(8,128)(2,1)}, bf16[4,256,512]{2,1,0:T(8,128)(2,1)}, bf16[2048,256]{1,0:T(8,128)(2,1)}...) custom-call(bf16[256,2048]{1,0:T(8,128)(2,1)} %get-tuple-element.196.x_ref, f32[1,2048]{1,0:T(1,128)} %bitcast.88, ...), custom_call_target="tpu_custom_call" | custom-call | flops 6979321856 | bytes 18874368 | tf_op jit(solution)/shard_map/attend_block/pallas_call | solution.py:761
  360.2 79.9 %all-gather.2.cloned.1.call-done.w_d = bf16[5632,2048]{1,0:T(8,128)(2,1)} async-done(((bf16[352,2048]{1,0:T(8,128)(2,1)}), bf16[5632,2048]{1,0:T(8,128)(2,1)}) %all-gather.2.cloned.1.call-update) | async-done | bytes 23068688 | tf_op jit(solution)/shard_map/all_gather | solution.py:958
  440.1 35.4 %ffn_fwd.3 = (bf16[256,2048]{1,0:T(8,128)(2,1)}, bf16[2048,256]{1,0:T(8,128)(2,1)}, bf16[5632,256]{1,0:T(8,128)(2,1)}, bf16[256,5632]{1,0:T(8,128)(2,1)}, bf16[256,5632]{1,0:T(8,128)(2,1)}) custom-call(f32[256,2048]{1,0:T(8,128)} %get-tuple-element.101.mid_ref, f32[1,2048]{1,0:T(1,128)} %bitcast.79, bf16[2048,5632]{1,0:T(8,128)(2,1)} %get-tuple-element.102.w_g, ...), custom_call_target="tpu_custom_call" | custom-call | flops 17716740096 | bytes 69206016 | tf_op jit(solution)/shard_map/ffn_fwd/pallas_call | solution.py:574
  475.5 3.7 collective-permute-start
  480.7 21.1 %collective-permute-done = bf16[256,2048]{1,0:T(8,128)(2,1)S(1)} collective-permute-done((bf16[256,2048]{1,0:T(8,128)(2,1)}, bf16[256,2048]{1,0:T(8,128)(2,1)S(1)}, u32[]{:S(2)}, u32[]{:S(2)}) %collective-permute-start) | collective-permute-done | bytes 1048608 | tf_op jit(solution)/shard_map/ppermute | solution.py:951
  503.5 31.8 %attend_block.4 = (bf16[2048,256]{1,0:T(8,128)(2,1)}, bf16[256,2048]{1,0:T(8,128)(2,1)}, bf16[4,256,512]{2,1,0:T(8,128)(2,1)}, bf16[2048,256]{1,0:T(8,128)(2,1)}...) custom-call(bf16[256,2048]{1,0:T(8,128)(2,1)} %bitcast_select_fusion.1.x_ref, f32[1,2048]{1,0:T(1,128)} %bitcast.89, ...), custom_call_target="tpu_custom_call" | custom-call | flops 6979321856 | bytes 18874368 | tf_op jit(solution)/shard_map/attend_block/pallas_call | solution.py:761
  536.3 35.4 %ffn_fwd.4 = (bf16[256,2048]{1,0:T(8,128)(2,1)}, bf16[2048,256]{1,0:T(8,128)(2,1)}, bf16[5632,256]{1,0:T(8,128)(2,1)}, bf16[256,5632]{1,0:T(8,128)(2,1)}, bf16[256,5632]{1,0:T(8,128)(2,1)}) custom-call(f32[256,2048]{1,0:T(8,128)} %get-tuple-element.108.mid_ref, f32[1,2048]{1,0:T(1,128)} %bitcast.80, bf16[2048,5632]{1,0:T(8,128)(2,1)} %get-tuple-element.102.w_g, ...), custom_call_target="tpu_custom_call" | custom-call | flops 17716740096 | bytes 69206016 | tf_op jit(solution)/shard_map/ffn_fwd/pallas_call | solution.py:574
  571.8 4.3 collective-permute-start.2
  578.5 18.9 %collective-permute-done.2 = bf16[256,2048]{1,0:T(8,128)(2,1)S(1)} collective-permute-done((bf16[256,2048]{1,0:T(8,128)(2,1)}, bf16[256,2048]{1,0:T(8,128)(2,1)S(1)}, u32[]{:S(2)}, u32[]{:S(2)}) %collective-permute-start.2) | collective-permute-done | bytes 1048608 | tf_op jit(solution)/shard_map/ppermute | solution.py:951
  598.5 47.5 %attend_block.5 = (bf16[2048,256]{1,0:T(8,128)(2,1)}, bf16[256,2048]{1,0:T(8,128)(2,1)}, bf16[4,256,512]{2,1,0:T(8,128)(2,1)}, bf16[2048,256]{1,0:T(8,128)(2,1)}...) custom-call(bf16[256,2048]{1,0:T(8,128)(2,1)} %broadcast_select_fusion.1.x_ref, f32[1,2048]{1,0:T(1,128)} %bitcast.90, ...), custom_call_target="tpu_custom_call" | custom-call | flops 6979321856 | bytes 18874368 | tf_op jit(solution)/shard_map/attend_block/pallas_call | solution.py:761
  646.1 35.4 %ffn_fwd.5 = (bf16[256,2048]{1,0:T(8,128)(2,1)}, bf16[2048,256]{1,0:T(8,128)(2,1)}, bf16[5632,256]{1,0:T(8,128)(2,1)}, bf16[256,5632]{1,0:T(8,128)(2,1)}, bf16[256,5632]{1,0:T(8,128)(2,1)}) custom-call(f32[256,2048]{1,0:T(8,128)} %get-tuple-element.112.mid_ref, f32[1,2048]{1,0:T(1,128)} %bitcast.81, bf16[2048,5632]{1,0:T(8,128)(2,1)} %get-tuple-element.102.w_g, ...), custom_call_target="tpu_custom_call" | custom-call | flops 17716740096 | bytes 69206016 | tf_op jit(solution)/shard_map/ffn_fwd/pallas_call | solution.py:574
  683.4 37.4 %ffn_bwd.3 = (bf16[256,5632]{1,0:T(8,128)(2,1)}, bf16[256,5632]{1,0:T(8,128)(2,1)}, f32[256,2048]{1,0:T(8,128)}, bf16[256,2048]{1,0:T(8,128)(2,1)}, f32[1,2048]{1,0:T(1,128)}) custom-call(bf16[256,2048]{1,0:T(8,128)(2,1)} %get-tuple-element.195.grad_ref.refs_37_, f32[256,2048]{1,0:T(8,128)} %get-tuple-element.112.mid_ref, f32[1,2048]{1,0:T(1,128)} %bitcast.82, ...), custom_call_target="tpu_custom_call" | custom-call | flops 17716740096 | bytes 69206016 | tf_op jit(solution)/shard_map/ffn_bwd/pallas_call | solution.py:626
  723.2 58.3 %attend_back.3 = (bf16[256,2048]{1,0:T(8,128)(2,1)}, bf16[256,512]{1,0:T(8,128)(2,1)}, f32[256,2048]{1,0:T(8,128)}, bf16[256,2048]{1,0:T(8,128)(2,1)}, f32[1,2048]{1,0:T(1,128)}) custom-call(bf16[256,2048]{1,0:T(8,128)(2,1)} %get-tuple-element.118.da_ref.refs_34_, f32[256,2048]{1,0:T(8,128)} %get-tuple-element.119.dmid_ref, ...), custom_call_target="tpu_custom_call" | custom-call | flops 10200547328 | bytes 18874368 | tf_op jit(solution)/shard_map/attend_back/pallas_call | solution.py:912
  783.5 19.7 %collective-permute-done.5 = bf16[256,2048]{1,0:T(8,128)(2,1)S(1)} collective-permute-done((bf16[256,2048]{1,0:T(8,128)(2,1)}, bf16[256,2048]{1,0:T(8,128)(2,1)S(1)}, u32[]{:S(2)}, u32[]{:S(2)}) %collective-permute-start.5) | collective-permute-done | bytes 1048608 | tf_op jit(solution)/shard_map/ppermute | solution.py:951
  804.8 37.5 %ffn_bwd.4 = (bf16[256,5632]{1,0:T(8,128)(2,1)}, bf16[256,5632]{1,0:T(8,128)(2,1)}, f32[256,2048]{1,0:T(8,128)}, bf16[256,2048]{1,0:T(8,128)(2,1)}, f32[1,2048]{1,0:T(1,128)}) custom-call(bf16[256,2048]{1,0:T(8,128)(2,1)} %bitcast_select_fusion.grad_ref.refs_38_, f32[256,2048]{1,0:T(8,128)} %get-tuple-element.108.mid_ref, f32[1,2048]{1,0:T(1,128)} %bitcast.83, ...), custom_call_target="tpu_custom_call" | custom-call | flops 17716740096 | bytes 69206016 | tf_op jit(solution)/shard_map/ffn_bwd/pallas_call | solution.py:626
  843.7 54.7 %attend_back.4 = (bf16[256,2048]{1,0:T(8,128)(2,1)}, bf16[256,512]{1,0:T(8,128)(2,1)}, f32[256,2048]{1,0:T(8,128)}, bf16[256,2048]{1,0:T(8,128)(2,1)}, f32[1,2048]{1,0:T(1,128)}) custom-call(bf16[256,2048]{1,0:T(8,128)(2,1)} %get-tuple-element.130.da_ref.refs_35_, f32[256,2048]{1,0:T(8,128)} %get-tuple-element.131.dmid_ref, ...), custom_call_target="tpu_custom_call" | custom-call | flops 10200547328 | bytes 18874368 | tf_op jit(solution)/shard_map/attend_back/pallas_call | solution.py:912
  900.5 20.5 %collective-permute-done.7 = bf16[256,2048]{1,0:T(8,128)(2,1)S(1)} collective-permute-done((bf16[256,2048]{1,0:T(8,128)(2,1)}, bf16[256,2048]{1,0:T(8,128)(2,1)S(1)}, u32[]{:S(2)}, u32[]{:S(2)}) %collective-permute-start.7) | collective-permute-done | bytes 1048608 | tf_op jit(solution)/shard_map/ppermute | solution.py:951
  922.0 37.5 %ffn_bwd.5 = (bf16[256,5632]{1,0:T(8,128)(2,1)}, bf16[256,5632]{1,0:T(8,128)(2,1)}, f32[256,2048]{1,0:T(8,128)}, bf16[256,2048]{1,0:T(8,128)(2,1)}, f32[1,2048]{1,0:T(1,128)}) custom-call(bf16[256,2048]{1,0:T(8,128)(2,1)} %broadcast_select_fusion.grad_ref.refs_39_, f32[256,2048]{1,0:T(8,128)} %get-tuple-element.101.mid_ref, f32[1,2048]{1,0:T(1,128)} %bitcast.84, ...), custom_call_target="tpu_custom_call" | custom-call | flops 17716740096 | bytes 69206016 | tf_op jit(solution)/shard_map/ffn_bwd/pallas_call | solution.py:626
  965.5 54.7 %attend_back.5 = (bf16[256,2048]{1,0:T(8,128)(2,1)}, bf16[256,512]{1,0:T(8,128)(2,1)}, f32[256,2048]{1,0:T(8,128)}, bf16[256,2048]{1,0:T(8,128)(2,1)}, f32[1,2048]{1,0:T(1,128)}) custom-call(bf16[256,2048]{1,0:T(8,128)(2,1)} %get-tuple-element.142.da_ref.refs_36_, f32[256,2048]{1,0:T(8,128)} %get-tuple-element.143.dmid_ref, ...), custom_call_target="tpu_custom_call" | custom-call | flops 10200547328 | bytes 18874368 | tf_op jit(solution)/shard_map/attend_back/pallas_call | solution.py:912
  1021.7 2.8 select_bitcast_fusion.1
  1024.5 2.5 maximum_bitcast_fusion
  1027.0 424.4 %reduce_weights.1 = (bf16[512,5632]{1,0:T(8,128)(2,1)}, bf16[512,5632]{1,0:T(8,128)(2,1)}, bf16[512,2560]{1,0:T(8,128)(2,1)}, bf16[512,2048]{1,0:T(8,128)(2,1)},...) custom-call(f32[8,2048]{1,0:T(8,128)} %pad.9.refs_0_, bf16[2048,256]{1,0:T(8,128)(2,1)} %get-tuple-element.117.refs_1_, ...), custom_call_target="tpu_custom_call" | custom-call | flops 45097156608 | bytes 44040192 | tf_op jit(solution)/shard_map/reduce_weights/pallas_call | solution.py:400
  1451.5 4.3 bitcast_convert_fusion.4
  1455.8 2.2 bitcast_convert_fusion.5
  1458.0 2.7 bitcast_convert_fusion.3
  1460.7 5.9 bitcast_convert_fusion.2
  1466.6 5.9 bitcast_convert_fusion.1
  1472.6 6.0 bitcast_convert_fusion
  (110 shorter events, 38.5 us)
Async XLA Ops:
  7.2 432.9 %all-gather.2.cloned.1.call-start = ((), (), s32[]{:S(2)}) async-start(), calls=%async_computation | async-start | bytes 24510464 | tf_op jit(solution)/shard_map/all_gather | solution.py:958
  9.0 2.6 copy-start
  307.9 6.5 copy-start.5
  475.5 26.3 %collective-permute-start = (bf16[256,2048]{1,0:T(8,128)(2,1)}, bf16[256,2048]{1,0:T(8,128)(2,1)S(1)}, u32[]{:S(2)}, u32[]{:S(2)}) collective-permute-start(bf16[256,2048]{1,0:T(8,128)(2,1)} %get-tuple-element.105), channel_id=1, source_target_pairs={{0,16},{1,17},{2,18},{3,19},{4,20},{5,21},{6,22},{7,23},{8,24},{9,... | collective-permute-start | bytes 3145736 | tf_op jit(solution)/shard_map/ppermute | solution.py:951
  479.2 56.2 %collective-permute-start.1 = (bf16[2048,256]{1,0:T(8,128)(2,1)}, bf16[2048,256]{1,0:T(8,128)(2,1)S(1)}, u32[]{:S(2)}, u32[]{:S(2)}) collective-permute-start(bf16[2048,256]{1,0:T(8,128)(2,1)} %get-tuple-element.107.refs_3_), channel_id=1, source_target_pairs={{0,8},{8,0},{4,12},{12,4},{1,9},{9,1},{5,13},{13,5},{2,10},{10,2},... | collective-permute-start | bytes 3145736 | tf_op jit(solution)/shard_map/ppermute | solution.py:1023
  536.3 39.8 %copy-start.14 = (f32[256,128]{1,0:T(8,128)S(1)}, f32[256,128]{1,0:T(8,128)}, u32[]{:S(2)}) copy-start(f32[256,128]{1,0:T(8,128)} %copy.24.sin_ref) | copy-start | bytes 393220
  571.8 25.7 %collective-permute-start.2 = (bf16[256,2048]{1,0:T(8,128)(2,1)}, bf16[256,2048]{1,0:T(8,128)(2,1)S(1)}, u32[]{:S(2)}, u32[]{:S(2)}) collective-permute-start(bf16[256,2048]{1,0:T(8,128)(2,1)} %get-tuple-element.109), channel_id=1, source_target_pairs={{0,16},{1,17},{2,18},{3,19},{4,20},{5,21},{6,22},{7,23},{8,24},{9,... | collective-permute-start | bytes 3145736 | tf_op jit(solution)/shard_map/ppermute | solution.py:951
  576.8 69.3 %collective-permute-start.3 = (bf16[2048,256]{1,0:T(8,128)(2,1)}, bf16[2048,256]{1,0:T(8,128)(2,1)}, u32[]{:S(2)}, u32[]{:S(2)}) collective-permute-start(bf16[2048,256]{1,0:T(8,128)(2,1)} %get-tuple-element.111.refs_2_), channel_id=1, source_target_pairs={{0,8},{8,0},{4,12},{12,4},{1,9},{9,1},{5,13},{13,5},{2,10},{10,2},... | collective-permute-start | bytes 3145736 | tf_op jit(solution)/shard_map/ppermute | solution.py:1023
  681.5 41.6 %collective-permute-start.4 = (bf16[2048,256]{1,0:T(8,128)(2,1)}, bf16[2048,256]{1,0:T(8,128)(2,1)S(1)}, u32[]{:S(2)}, u32[]{:S(2)}) collective-permute-start(bf16[2048,256]{1,0:T(8,128)(2,1)} %get-tuple-element.117.refs_1_), channel_id=1, source_target_pairs={{0,8},{8,0},{4,12},{12,4},{1,9},{9,1},{5,13},{13,5},{2,10},{10,2},... | collective-permute-start | bytes 3145736 | tf_op jit(solution)/shard_map/ppermute | solution.py:1023
  720.8 2.2 copy-start.11
  723.2 58.3 %copy-start.21 = (bf16[2048,256]{1,0:T(8,128)(2,1)}, bf16[2048,256]{1,0:T(8,128)(2,1)S(1)}, u32[]{:S(2)}) copy-start(bf16[2048,256]{1,0:T(8,128)(2,1)S(1)} %collective-permute-done.4.refs_4_) | copy-start | bytes 3145732
  781.5 21.7 %copy-start.6 = (bf16[2,256,2048]{2,1,0:T(8,128)(2,1)S(1)}, bf16[2,256,2048]{2,1,0:T(8,128)(2,1)}, u32[]{:S(2)}) copy-start(bf16[2,256,2048]{2,1,0:T(8,128)(2,1)} %param.12) | copy-start | bytes 6291460
  781.5 21.7 %collective-permute-start.5 = (bf16[256,2048]{1,0:T(8,128)(2,1)}, bf16[256,2048]{1,0:T(8,128)(2,1)S(1)}, u32[]{:S(2)}, u32[]{:S(2)}) collective-permute-start(bf16[256,2048]{1,0:T(8,128)(2,1)} %get-tuple-element.124), channel_id=1, source_target_pairs={{16,0},{17,1},{18,2},{19,3},{20,4},{21,5},{22,6},{23,7},{24,8},{25... | collective-permute-start | bytes 3145736 | tf_op jit(solution)/shard_map/ppermute | solution.py:951
  783.1 60.6 %collective-permute-start.6 = (bf16[256,5632]{1,0:T(8,128)(2,1)S(1)}, bf16[256,5632]{1,0:T(8,128)(2,1)}, u32[]{:S(2)}, u32[]{:S(2)}) collective-permute-start(bf16[256,5632]{1,0:T(8,128)(2,1)S(1)} %pad_maximum_fusion), channel_id=1, source_target_pairs={{0,8},{8,0},{4,12},{12,4},{1,9},{9,1},{5,13},{13,5},{2,10},{10,2},... | collective-permute-start | bytes 8650760 | tf_op jit(solution)/shard_map/ppermute | solution.py:968
  843.7 56.0 %copy-start.12 = (bf16[256,5632]{1,0:T(8,128)(2,1)S(1)}, bf16[256,5632]{1,0:T(8,128)(2,1)}, u32[]{:S(2)}) copy-start(bf16[256,5632]{1,0:T(8,128)(2,1)} %get-tuple-element.140.refs_17_) | copy-start | bytes 8650756
  898.5 22.5 %collective-permute-start.7 = (bf16[256,2048]{1,0:T(8,128)(2,1)}, bf16[256,2048]{1,0:T(8,128)(2,1)S(1)}, u32[]{:S(2)}, u32[]{:S(2)}) collective-permute-start(bf16[256,2048]{1,0:T(8,128)(2,1)} %get-tuple-element.136), channel_id=1, source_target_pairs={{16,0},{17,1},{18,2},{19,3},{20,4},{21,5},{22,6},{23,7},{24,8},{25... | collective-permute-start | bytes 3145736 | tf_op jit(solution)/shard_map/ppermute | solution.py:951
  900.1 65.4 %collective-permute-start.8 = (bf16[256,5632]{1,0:T(8,128)(2,1)S(1)}, bf16[256,5632]{1,0:T(8,128)(2,1)}, u32[]{:S(2)}, u32[]{:S(2)}) collective-permute-start(bf16[256,5632]{1,0:T(8,128)(2,1)S(1)} %pad_maximum_fusion.1), channel_id=1, source_target_pairs={{0,8},{8,0},{4,12},{12,4},{1,9},{9,1},{5,13},{13,5},{2,10},{10,2},... | collective-permute-start | bytes 8650760 | tf_op jit(solution)/shard_map/ppermute | solution.py:968
  959.6 2.3 copy-start.13
  962.1 64.9 %collective-permute-start.9 = (bf16[256,5632]{1,0:T(8,128)(2,1)S(1)}, bf16[256,5632]{1,0:T(8,128)(2,1)}, u32[]{:S(2)}, u32[]{:S(2)}) collective-permute-start(bf16[256,5632]{1,0:T(8,128)(2,1)S(1)} %pad_maximum_fusion.2), channel_id=1, source_target_pairs={{0,8},{8,0},{4,12},{12,4},{1,9},{9,1},{5,13},{13,5},{2,10},{10,2},... | collective-permute-start | bytes 8650760 | tf_op jit(solution)/shard_map/ppermute | solution.py:968
  965.5 54.8 %copy-start.15 = (f32[1,2048]{1,0:T(1,128)S(1)}, f32[1,2048]{1,0:T(1,128)}, u32[]{:S(2)}) copy-start(f32[1,2048]{1,0:T(1,128)} %get-tuple-element.152) | copy-start | bytes 24580
  965.5 54.8 %copy-start.16 = (f32[1,2048]{1,0:T(1,128)S(1)}, f32[1,2048]{1,0:T(1,128)}, u32[]{:S(2)}) copy-start(f32[1,2048]{1,0:T(1,128)} %get-tuple-element.151) | copy-start | bytes 24580
  965.5 54.8 %copy-start.17 = (f32[1,2048]{1,0:T(1,128)S(1)}, f32[1,2048]{1,0:T(1,128)}, u32[]{:S(2)}) copy-start(f32[1,2048]{1,0:T(1,128)} %get-tuple-element.154) | copy-start | bytes 24580
  965.5 54.8 %copy-start.18 = (f32[1,2048]{1,0:T(1,128)S(1)}, f32[1,2048]{1,0:T(1,128)}, u32[]{:S(2)}) copy-start(f32[1,2048]{1,0:T(1,128)} %get-tuple-element.153) | copy-start | bytes 24580
  965.5 54.8 %copy-start.19 = (f32[1,2048]{1,0:T(1,128)S(1)}, f32[1,2048]{1,0:T(1,128)}, u32[]{:S(2)}) copy-start(f32[1,2048]{1,0:T(1,128)} %get-tuple-element.156) | copy-start | bytes 24580
  965.5 56.2 %copy-start.7 = (f32[256,2048]{1,0:T(8,128)S(1)}, f32[256,2048]{1,0:T(8,128)}, u32[]{:S(2)}) copy-start(f32[256,2048]{1,0:T(8,128)} %get-tuple-element.150) | copy-start | bytes 6291460
  1451.5 6.5 copy-start.4
  1451.5 9.2 slice-start.4
  1455.8 4.9 slice-start.5
  1458.0 8.6 slice-start.2
  1460.7 6.0 slice-start.3
  1460.7 11.9 slice-start
  1466.6 5.9 slice-start.1
  (7 other events, 10.1 us)
Sparse Core Ops, SparseCore 0:
  310.8 129.2 all-gather.1

commit v6 on v5

--- a/solution.py
+++ b/solution.py
@@ -410,22 +410,24 @@
     )(gain, *operands)
 
 
-def gather_kernel(splits, *refs):
+def gather_kernel(splits, x_ref, cos_ref, sin_ref, *refs):
     n = lax.axis_size("shard")
     me = lax.axis_index("shard")
     rep = lax.axis_index("rep")
     right = {"shard": lax.rem(me + 1, n)}
-    left = {"shard": lax.rem(me + n - 1, n)}
     core_peer = {"rep": rep + 1 - 2 * lax.rem(rep, 2)}
     y_rep = rep + 2 - 4 * (rep // 2)
     y_peer = {"rep": y_rep}
     count = len(splits)
-    ins, outs = refs[:count], refs[count:2 * count]
-    holds = refs[2 * count:3 * count]
-    zs, zr, ys, yr, cs, cr, ts, tr, local = refs[3 * count:]
+    early = 4
+    ins, outs, refs = refs[:count], refs[count:2 * count], refs[2 * count:]
+    attend_outs, refs = refs[:6], refs[6:]
+    attend_refs, refs = refs[:13], refs[13:]
+    holds, refs = refs[:count], refs[count:]
+    zs, zr, ys, yr, cs, cr, ts, tr, local, gain_blocks, gain_row, gain_sem = refs
 
     barrier = pltpu.get_barrier_semaphore()
-    for peer in (left, right, core_peer, y_peer):
+    for peer in [{"shard": lax.rem(me + d, n)} for d in range(1, n)] + [core_peer, y_peer]:
         pl.semaphore_signal(barrier, inc=1, device_id=peer, device_id_type=MESH_IDS)
 
     pieces = []
@@ -434,6 +436,8 @@
         for width in split:
             pieces.append((k, at, width))
             at += width
+    first = [piece for piece in range(len(pieces)) if pieces[piece][0] < early]
+    second = [piece for piece in range(len(pieces)) if pieces[piece][0] >= early]
 
     def own_load(k):
         return pltpu.make_async_copy(ins[k], holds[k], local.at[0, k])
@@ -468,56 +472,99 @@
         there = spot(piece, s, y_rep)
         return remote(there, there, ts.at[piece, s - 1], tr.at[piece, s - 1], core_peer)
 
+    def begin(group):
+        for piece in group:
+            z_copy(piece, 0).start()
+
+    def own_rows(which):
+        for k in which:
+            own_load(k).start()
+        for k in which:
+            own_load(k).wait()
+            own_store(k).start()
+
     def turn(piece, s):
         y_copy(piece, s).wait_recv()
         t_copy(piece, s).start()
 
-    pl.semaphore_wait(barrier, 4)
-    for piece in range(len(pieces)):
-        z_copy(piece, 0).start()
-    for k in range(count):
-        own_load(k).start()
-    for k in range(count):
+    def pass_on(group, before_last):
+        before = []
+        for s in range(1, n):
+            if s == n - 1:
+                before_last()
+            for piece in group:
+                z_copy(piece, s - 1).wait_recv()
+                if s < n - 1:
+                    z_copy(piece, s).start()
+                y_copy(piece, s).start()
+                c_copy(piece, s).start()
+                before.append((piece, s))
+                if len(before) > 1:
+                    turn(*before[-2])
+        turn(*before[-1])
+        return before
+
+    def arrived(which, before):
+        for k in which:
+            own_store(k).wait()
+        for piece, s in before:
+            c_copy(piece, s).wait_recv()
+            t_copy(piece, s).wait_recv()
+
+    pl.semaphore_wait(barrier, n + 1)
+    begin(first)
+    own_rows(range(early))
+
+    def start_second():
+        begin(second)
+        for k in range(early, count):
+            own_load(k).start()
+    before = pass_on(first, lambda: None)
+    arrived(range(early), before)
+    load = pltpu.make_async_copy(outs[3], gain_blocks, gain_sem.at[0])
+    load.start()
+    load.wait()
+    rows = ins[3].shape[0]
+    part = x_ref.shape[1] // n
+    for k in range(n):
+        gain_row[:, k * part:(k + 1) * part] = gain_blocks[k * rows:k * rows + 1, :part].astype(F32)
+    attend_steps(lambda: None, start_second, x_ref, gain_row, cos_ref, sin_ref, outs[0], outs[1], outs[2], *attend_outs, *attend_refs)
+    for k in range(early, count):
         own_load(k).wait()
         own_store(k).start()
-    before = []
-    for s in range(1, n):
-        for piece in range(len(pieces)):
-            z_copy(piece, s - 1).wait_recv()
-            if s < n - 1:
-                z_copy(piece, s).start()
-            y_copy(piece, s).start()
-            c_copy(piece, s).start()
-            before.append((piece, s))
-            if len(before) > 1:
-                turn(*before[-2])
-    turn(*before[-1])
-    for k in range(count):
-        own_store(k).wait()
-    for piece, s in before:
+    after = pass_on(second, lambda: None)
+    arrived(range(early, count), after)
+    for piece, s in before + after:
         z_copy(piece, s - 1).wait_send()
         y_copy(piece, s).wait_send()
-        c_copy(piece, s).wait()
-        t_copy(piece, s).wait()
-
-
-def gather_weights(shards, splits, collective_id, name):
+        c_copy(piece, s).wait_send()
+        t_copy(piece, s).wait_send()
+
+
+def gather_weights(x, cos_table, sin_table, shards, splits, collective_id, name):
     n = lax.axis_size("shard")
+    rows, width = x.shape
+    kv_both = shards[1].shape[1]
     dma = pltpu.SemaphoreType.DMA
     pieces = sum(len(split) for split in splits)
     pair = dma((pieces, n - 1))
     anywhere = pl.BlockSpec(memory_space=pl.ANY)
+    vmem = pl.BlockSpec(memory_space=pltpu.VMEM)
     moved = 2 * n * sum(shard.shape[0] * shard.shape[1] for shard in shards)
-    return pl.pallas_call(
+    results = pl.pallas_call(
         functools.partial(gather_kernel, splits),
-        in_specs=[anywhere] * len(shards),
-        out_specs=[anywhere] * len(shards),
-        out_shape=[jax.ShapeDtypeStruct((n * shard.shape[0], shard.shape[1]), BF16) for shard in shards],
-        scratch_shapes=[pltpu.VMEM(shard.shape, BF16) for shard in shards] + [pair] * 8 + [dma((2, len(shards)))],
-        compiler_params=pltpu.CompilerParams(collective_id=collective_id, has_side_effects=True, vmem_limit_bytes=40 * 1024 * 1024),
-        cost_estimate=pl.CostEstimate(flops=0, bytes_accessed=moved * 4, transcendentals=0),
+        in_specs=[vmem] * 3 + [anywhere] * len(shards),
+        out_specs=[anywhere] * len(shards) + [vmem] * 6,
+        out_shape=[jax.ShapeDtypeStruct((n * shard.shape[0], shard.shape[1]), BF16) for shard in shards]
+        + attend_outputs(rows, width, n, kv_both),
+        scratch_shapes=attend_scratch(rows, width, n, kv_both) + [pltpu.VMEM(shard.shape, BF16) for shard in shards]
+        + [pair] * 8 + [dma((2, len(shards))), pltpu.VMEM((n * shards[3].shape[0], shards[3].shape[1]), BF16),
+                        pltpu.VMEM((1, width), F32), dma((1,))],
+        compiler_params=pltpu.CompilerParams(collective_id=collective_id, has_side_effects=True, vmem_limit_bytes=60 * 1024 * 1024),
+        cost_estimate=pl.CostEstimate(flops=4 * rows * width * width, bytes_accessed=moved * 4, transcendentals=0),
         name=name,
-    )(*shards)
+    )(x, cos_table, sin_table, *shards)
+    return results[:len(shards)], results[len(shards):]
 
 
 def halves(width):
@@ -645,21 +692,16 @@
     return rows * jnp.tile(cos_ref[...], (1, reps)) + swapped * jnp.tile(sin_ref[...], (1, reps))
 
 
-def attend_block_kernel(x_ref, gain_ref, cos_ref, sin_ref, w_q, w_kv, w_o,
-                        normed_turn, q_ref, kv_ref, attended_turn, lse_ref, mid_ref,
-                        normed_ref, attended_ref, wq_ref, wkv_ref, wo_ref, q_turn, acc, top_ref, total_ref, land,
-                        load_sem, send_sem, recv_sem):
+def attend_steps(greeted, sent, x_ref, gain_ref, cos_ref, sin_ref, w_q, w_kv, w_o,
+                 normed_turn, q_ref, kv_ref, attended_turn, lse_ref, mid_ref,
+                 normed_ref, attended_ref, wq_ref, wkv_ref, wo_ref, q_turn, acc, top_ref, total_ref, land,
+                 load_sem, send_sem, recv_sem):
     n = lax.axis_size("shard")
     me = lax.axis_index("shard")
     rows, width = x_ref.shape
     kv_width = wkv_ref.shape[1] // 2
     group = HEADS // KV_HEADS
     scale = LOG2E * HEAD ** -0.5
-    barrier = pltpu.get_barrier_semaphore()
-    for d in range(1, n):
-        @pl.when(me >= d)
-        def _(d=d):
-            pl.semaphore_signal(barrier, inc=1, device_id={"shard": me - d}, device_id_type=MESH_IDS)
     loads = [pltpu.make_async_copy(src, dst, load_sem.at[k])
              for k, (src, dst) in enumerate(((w_kv, wkv_ref), (w_q, wq_ref), (w_o, wo_ref)))]
     for load in loads:
@@ -677,14 +719,12 @@
     kv = mm(normed_ref[...], wkv_ref[...])
     land[0, :, :kv_width] = rotated(kv[:, :kv_width], cos_ref, sin_ref).astype(BF16)
     land[0, :, kv_width:] = kv[:, kv_width:].astype(BF16)
-    @pl.when(me < n - 1)
-    def _():
-        pl.semaphore_wait(barrier, n - 1 - me)
-
+    greeted()
     for d in range(1, n):
         @pl.when(me + d < n)
         def _(d=d):
             to_later(d).start()
+    sent()
     loads[1].wait()
     chunk = 4 * LANES
     for at in range(0, width, chunk):
@@ -750,34 +790,58 @@
             to_later(d).wait_send()
 
 
+def attend_block_kernel(*refs):
+    n = lax.axis_size("shard")
+    me = lax.axis_index("shard")
+    barrier = pltpu.get_barrier_semaphore()
+    for d in range(1, n):
+        @pl.when(me >= d)
+        def _(d=d):
+            pl.semaphore_signal(barrier, inc=1, device_id={"shard": me - d}, device_id_type=MESH_IDS)
+
+    def greeted():
+        @pl.when(me < n - 1)
+        def _():
+            pl.semaphore_wait(barrier, n - 1 - me)
+    attend_steps(greeted, lambda: None, *refs)
+
+
+def attend_scratch(rows, width, n, kv_both):
+    dma = pltpu.SemaphoreType.DMA
+    return [
+        pltpu.VMEM((rows, width), BF16), pltpu.VMEM((rows, width), BF16),
+        pltpu.VMEM((width, width), BF16), pltpu.VMEM((width, kv_both), BF16), pltpu.VMEM((width, width), BF16),
+        pltpu.VMEM((width, rows), BF16), pltpu.VMEM((width, rows), F32),
+        pltpu.VMEM((HEADS, rows), F32), pltpu.VMEM((HEADS, rows), F32),
+        pltpu.VMEM((n, rows, kv_both), BF16),
+        dma((3,)), dma((n - 1,)), dma((n - 1,)),
+    ]
+
+
+def attend_outputs(rows, width, n, kv_both):
+    return [
+        jax.ShapeDtypeStruct((width, rows), BF16),
+        jax.ShapeDtypeStruct((rows, width), BF16),
+        jax.ShapeDtypeStruct((n, rows, kv_both), BF16),
+        jax.ShapeDtypeStruct((width, rows), BF16),
+        jax.ShapeDtypeStruct((HEADS, rows), F32),
+        jax.ShapeDtypeStruct((rows, width), F32),
+    ]
+
+
 def attend_block(x, gain, cos_table, sin_table, w_q, w_kv, w_o, collective_id):
     n = lax.axis_size("shard")
     rows, width = x.shape
     kv_both = w_kv.shape[1]
     vmem = pl.BlockSpec(memory_space=pltpu.VMEM)
     anywhere = pl.BlockSpec(memory_space=pl.ANY)
-    dma = pltpu.SemaphoreType.DMA
     flops = 2 * rows * width * (2 * width + kv_both) + 4 * rows * rows * n * width
     return pl.pallas_call(
         attend_block_kernel,
         in_specs=[vmem] * 4 + [anywhere] * 3,
         out_specs=[vmem] * 6,
-        out_shape=[
-            jax.ShapeDtypeStruct((width, rows), BF16),
-            jax.ShapeDtypeStruct((rows, width), BF16),
-            jax.ShapeDtypeStruct((n, rows, kv_both), BF16),
-            jax.ShapeDtypeStruct((width, rows), BF16),
-            jax.ShapeDtypeStruct((HEADS, rows), F32),
-            jax.ShapeDtypeStruct((rows, width), F32),
-        ],
-        scratch_shapes=[
-            pltpu.VMEM((rows, width), BF16), pltpu.VMEM((rows, width), BF16),
-            pltpu.VMEM(w_q.shape, BF16), pltpu.VMEM(w_kv.shape, BF16), pltpu.VMEM(w_o.shape, BF16),
-            pltpu.VMEM((width, rows), BF16), pltpu.VMEM((width, rows), F32),
-            pltpu.VMEM((HEADS, rows), F32), pltpu.VMEM((HEADS, rows), F32),
-            pltpu.VMEM((n, rows, kv_both), BF16),
-            dma((3,)), dma((n - 1,)), dma((n - 1,)),
-        ],
+        out_shape=attend_outputs(rows, width, n, kv_both),
+        scratch_shapes=attend_scratch(rows, width, n, kv_both),
         compiler_params=pltpu.CompilerParams(
             collective_id=collective_id, has_side_effects=True, vmem_limit_bytes=56 * 1024 * 1024),
         cost_estimate=pl.CostEstimate(flops=flops, bytes_accessed=2 * width * (2 * width + kv_both), transcendentals=rows * rows * n * HEADS),
@@ -951,13 +1015,6 @@
     return lax.ppermute(block, axis, pairs)
 
 
-def gather_rows(weight):
-    parts = lax.axis_size("rep")
-    rows = weight.shape[0] // parts
-    own = lax.dynamic_slice_in_dim(weight, lax.axis_index("rep") * rows, rows, 0)
-    return lax.all_gather(own, ("shard", "rep"), axis=0, tiled=True)
-
-
 Y_PAIRS = [(0, 2), (2, 0), (1, 3), (3, 1)]
 
 
@@ -968,10 +1025,10 @@
     return lax.ppermute(jnp.concatenate(parts, axis=1), "rep", Y_PAIRS)
 
 
-def layer_forward(stream_in, weights, tables, pending):
+def layer_forward(stream_in, weights, tables, pending, done):
     w_q, w_kv, w_o, w_g, w_u, w_d, gains_wide = weights
     cos_table, sin_table = tables
-    normed, queries, kv, attended, lse, middle = attend_block(
+    normed, queries, kv, attended, lse, middle = done or attend_block(
         stream_in, gains_wide[0:1], cos_table, sin_table, w_q, w_kv, w_o, 3)
     middle, pending = lax.optimization_barrier((middle, pending))
     result, normed_two, hidden, gate_fac, up_fac = ffn_fwd(middle, gains_wide[1:2], w_g, w_u, w_d)
@@ -1000,16 +1057,16 @@
     query_pos = lax.axis_index("shard") * span_len + jnp.arange(span_len, dtype=jnp.int32)
     cos_half, sin_half = angles_for(query_pos)
     tables = (jnp.tile(cos_half, (1, 4)), jnp.tile(jnp.concatenate([-sin_half, sin_half], axis=1), (1, 2)))
-    live_mask = (jnp.arange(slot_count) < live_counts[0]).astype(F32)
+    live_mask = (jnp.arange(slot_count) < live_counts[0]).astype(BF16)
     gain_rows = jnp.pad(norm_gains[0], ((0, 14), (0, -norm_gains.shape[2] % (4 * LANES))))
-    shards = [w_query[0], jnp.concatenate([w_key[0], w_value[0]], axis=1), w_out[0], gain_rows, w_gate[0], w_up[0]]
-    w_q, w_kv, w_o, gains, w_g, w_u = gather_weights(shards, [halves(shard.shape[1]) for shard in shards], 2, "gather_weights")
-    down_shard, w_q = lax.optimization_barrier((w_down[0], w_q))
-    w_d = gather_rows(down_shard)
+    shards = [w_query[0], jnp.concatenate([w_key[0], w_value[0]], axis=1), w_out[0], gain_rows, w_gate[0], w_up[0], w_down[0]]
+    first_in = jnp.where(section == 0, tokens[0] * live_mask[0], jnp.zeros_like(tokens[0]))
+    gathered, attended_first = gather_weights(
+        first_in, *tables, shards, [halves(shard.shape[1]) for shard in shards], 2, "gather_weights")
+    w_q, w_kv, w_o, gains, w_g, w_u, w_d = gathered
     gain_blocks = gains.reshape(-1, 16, gain_rows.shape[1])[:, :2, :norm_gains.shape[2]]
     gains_wide = gain_blocks.transpose(1, 0, 2).reshape(2, model_width).astype(F32)
     weights = (w_q, w_kv, w_o, w_g, w_u, w_d, gains_wide)
-    live_mask = live_mask.astype(BF16)
     zero_slot = jnp.zeros((span_len, model_width), BF16)
     ticks = slot_count + 1
     results, kept_all, others = [], [], []
@@ -1017,8 +1074,8 @@
     received = zero_slot
     for tick in range(ticks):
         slot_in = tokens[tick] * live_mask[tick] if tick < slot_count else zero_slot
-        own_in = jnp.where(section == 0, slot_in, received)
-        result, kept, pending = layer_forward(own_in, weights, tables, pending)
+        own_in = jnp.where(section == 0, slot_in, received) if tick else first_in
+        result, kept, pending = layer_forward(own_in, weights, tables, pending, None if tick else attended_first)
         others += pending
         pending = [lax.ppermute(kept["normed_two"], "rep", Y_PAIRS)]
         received = passed_along(result, "section", 1)

time: 1500 us -> 1480 us (0.987)
  Pallas kernels: 1220 us -> 1310 us
  waiting for transfers between devices: 160 us -> 79.1 us
    pallas_call x1, Pallas kernels: 292 us -> 402 us  [gather_weights(): pl.pallas_call(functools.partial(gather_kernel, splits), in_specs=[vmem]...]
    all_gather x1 -> x0, waiting for transfers between devices: 79.9 us -> none  [gather_rows(): return lax.all_gather(own, ('shard', 'rep'), axis=0, tiled=True)]
    pallas_call x3 -> x2, Pallas kernels: 121 us -> 95 us  [attend_block(): pl.pallas_call(attend_block_kernel, in_specs=[vmem] * 4 + [anywhere] * 3,...]
  transfers between devices with their start and end apart: 11 -> 10, of which waited for: 5 -> 4; matrix products, arithmetic and copies ran while one was open for 2% -> 1% of each run, Pallas kernels for 19% -> 18%
where the time goes in v6:
time: 1480 us; the launch traced here: 1470 us
  Pallas kernels  1310 us (89%)
  waiting for transfers between devices  79.1 us (5%)
  other arithmetic  47.6 us (3%)
  starting transfers between devices  17 us (1%)
  local copies, waits for them, and re-layouts  15.8 us (1%)
    pallas_call x1, Pallas kernels, reduce_weights(): pl.pallas_call(functools.partial(reduce_kernel, plans, slots), in_specs=[...  425 us
    pallas_call x1, Pallas kernels, gather_weights(): pl.pallas_call(functools.partial(gather_kernel, splits), in_specs=[vmem]...  402 us
    pallas_call x3, Pallas kernels, attend_back(): pl.pallas_call(attend_back_kernel, in_specs=[vmem] * 10 + [anywhere] * 3,...  168 us
    pallas_call x3, Pallas kernels, ffn_bwd(): pl.pallas_call(ffn_bwd_kernel, grid=(ff // FF_TILE,), in_specs=[whole, wh...  112 us
    pallas_call x3, Pallas kernels, ffn_fwd(): pl.pallas_call(ffn_fwd_kernel, grid=(ff // FF_TILE,), in_specs=[whole, pl...  106 us
    pallas_call x2, Pallas kernels, attend_block(): pl.pallas_call(attend_block_kernel, in_specs=[vmem] * 4 + [anywhere] * 3,...  95 us
    ppermute x4, waiting for transfers between devices, passed_along(): return lax.ppermute(block, axis, pairs)  79.1 us
  transfers between devices with their start and end apart: 10, of which 4 were waited for; matrix products, arithmetic and copies ran while one was open for 1% of the time, Pallas kernels for 18%

profile of v6, /device:TPU:0, one launch (start us, length us, event | category | flops | bytes accessed | tf_op | source)
XLA Modules:
  0.0 1470.5 jit_solution(3837138750634269010)
XLA Ops:
  3.8 1.9 pad_maximum_fusion.3.refs_1_
  7.0 4.0 select_bitcast_fusion.2
  10.9 402.4 %gather_weights.1 = (bf16[2048,2048]{1,0:T(8,128)(2,1)}, bf16[2048,512]{1,0:T(8,128)(2,1)}, bf16[2048,2048]{1,0:T(8,128)(2,1)}, bf16[64,512]{1,0:T(8,128)(2,1)},...) custom-call(bf16[256,2048]{1,0:T(8,128)(2,1)} %get-tuple-element.194, ...), custom_call_target="tpu_custom_call" | custom-call | flops 4294967296 | bytes 352583680 | tf_op jit(solution)/shard_map/gather_weights/pallas_call | solution.py:554
  414.7 35.4 %ffn_fwd.3 = (bf16[256,2048]{1,0:T(8,128)(2,1)}, bf16[2048,256]{1,0:T(8,128)(2,1)}, bf16[5632,256]{1,0:T(8,128)(2,1)}, bf16[256,5632]{1,0:T(8,128)(2,1)}, bf16[256,5632]{1,0:T(8,128)(2,1)}) custom-call(f32[256,2048]{1,0:T(8,128)} %get-tuple-element.95.mid_ref, f32[1,2048]{1,0:T(1,128)} %bitcast.79, bf16[2048,5632]{1,0:T(8,128)(2,1)} %get-tuple-element.97.w_g, ...), custom_call_target="tpu_custom_call" | custom-call | flops 17716740096 | bytes 69206016 | tf_op jit(solution)/shard_map/ffn_fwd/pallas_call | solution.py:621
  450.1 3.5 collective-permute-start
  453.6 1.7 collective-permute-start.1
  456.0 20.4 %collective-permute-done = bf16[256,2048]{1,0:T(8,128)(2,1)S(1)} collective-permute-done((bf16[256,2048]{1,0:T(8,128)(2,1)}, bf16[256,2048]{1,0:T(8,128)(2,1)S(1)}, u32[]{:S(2)}, u32[]{:S(2)}) %collective-permute-start) | collective-permute-done | bytes 1048608 | tf_op jit(solution)/shard_map/ppermute | solution.py:1015
  476.3 1.7 bitcast_select_fusion.1.refs_0_.x_ref
  478.1 47.7 %attend_block.2 = (bf16[2048,256]{1,0:T(8,128)(2,1)}, bf16[256,2048]{1,0:T(8,128)(2,1)}, bf16[4,256,512]{2,1,0:T(8,128)(2,1)}, bf16[2048,256]{1,0:T(8,128)(2,1)}...) custom-call(bf16[256,2048]{1,0:T(8,128)(2,1)} %bitcast_select_fusion.1.refs_0_.x_ref, f32[1,2048]{1,0:T(1,128)} %bitcast.87, ...), custom_call_target="tpu_custom_call" | custom-call | flops 6979321856 | bytes 18874368 | tf_op jit(solution)/shard_map/attend_block/pallas_call | solution.py:839
  526.8 35.4 %ffn_fwd.4 = (bf16[256,2048]{1,0:T(8,128)(2,1)}, bf16[2048,256]{1,0:T(8,128)(2,1)}, bf16[5632,256]{1,0:T(8,128)(2,1)}, bf16[256,5632]{1,0:T(8,128)(2,1)}, bf16[256,5632]{1,0:T(8,128)(2,1)}) custom-call(f32[256,2048]{1,0:T(8,128)} %get-tuple-element.106.mid_ref, f32[1,2048]{1,0:T(1,128)} %bitcast.80, bf16[2048,5632]{1,0:T(8,128)(2,1)} %get-tuple-element.97.w_g, ...), custom_call_target="tpu_custom_call" | custom-call | flops 17716740096 | bytes 69206016 | tf_op jit(solution)/shard_map/ffn_fwd/pallas_call | solution.py:621
  562.2 4.3 collective-permute-start.2
  569.0 18.5 %collective-permute-done.2 = bf16[256,2048]{1,0:T(8,128)(2,1)S(1)} collective-permute-done((bf16[256,2048]{1,0:T(8,128)(2,1)}, bf16[256,2048]{1,0:T(8,128)(2,1)S(1)}, u32[]{:S(2)}, u32[]{:S(2)}) %collective-permute-start.2) | collective-permute-done | bytes 1048608 | tf_op jit(solution)/shard_map/ppermute | solution.py:1015
  588.6 47.3 %attend_block.3 = (bf16[2048,256]{1,0:T(8,128)(2,1)}, bf16[256,2048]{1,0:T(8,128)(2,1)}, bf16[4,256,512]{2,1,0:T(8,128)(2,1)}, bf16[2048,256]{1,0:T(8,128)(2,1)}...) custom-call(bf16[256,2048]{1,0:T(8,128)(2,1)} %broadcast_select_fusion.1.refs_0_.x_ref, f32[1,2048]{1,0:T(1,128)} %bitcast.88, ...), custom_call_target="tpu_custom_call" | custom-call | flops 6979321856 | bytes 18874368 | tf_op jit(solution)/shard_map/attend_block/pallas_call | solution.py:839
  635.9 35.4 %ffn_fwd.5 = (bf16[256,2048]{1,0:T(8,128)(2,1)}, bf16[2048,256]{1,0:T(8,128)(2,1)}, bf16[5632,256]{1,0:T(8,128)(2,1)}, bf16[256,5632]{1,0:T(8,128)(2,1)}, bf16[256,5632]{1,0:T(8,128)(2,1)}) custom-call(f32[256,2048]{1,0:T(8,128)} %get-tuple-element.110.mid_ref, f32[1,2048]{1,0:T(1,128)} %bitcast.81, bf16[2048,5632]{1,0:T(8,128)(2,1)} %get-tuple-element.97.w_g, ...), custom_call_target="tpu_custom_call" | custom-call | flops 17716740096 | bytes 69206016 | tf_op jit(solution)/shard_map/ffn_fwd/pallas_call | solution.py:621
  671.4 1.8 collective-permute-start.4
  673.2 37.4 %ffn_bwd.3 = (bf16[256,5632]{1,0:T(8,128)(2,1)}, bf16[256,5632]{1,0:T(8,128)(2,1)}, f32[256,2048]{1,0:T(8,128)}, bf16[256,2048]{1,0:T(8,128)(2,1)}, f32[1,2048]{1,0:T(1,128)}) custom-call(bf16[256,2048]{1,0:T(8,128)(2,1)} %get-tuple-element.193.grad_ref.refs_37_, f32[256,2048]{1,0:T(8,128)} %get-tuple-element.110.mid_ref, f32[1,2048]{1,0:T(1,128)} %bitcast.82, ...), custom_call_target="tpu_custom_call" | custom-call | flops 17716740096 | bytes 69206016 | tf_op jit(solution)/shard_map/ffn_bwd/pallas_call | solution.py:673
  713.0 58.2 %attend_back.3 = (bf16[256,2048]{1,0:T(8,128)(2,1)}, bf16[256,512]{1,0:T(8,128)(2,1)}, f32[256,2048]{1,0:T(8,128)}, bf16[256,2048]{1,0:T(8,128)(2,1)}, f32[1,2048]{1,0:T(1,128)}) custom-call(bf16[256,2048]{1,0:T(8,128)(2,1)} %get-tuple-element.116.da_ref.refs_34_, f32[256,2048]{1,0:T(8,128)} %get-tuple-element.117.dmid_ref, ...), custom_call_target="tpu_custom_call" | custom-call | flops 10200547328 | bytes 18874368 | tf_op jit(solution)/shard_map/attend_back/pallas_call | solution.py:976
  773.3 19.7 %collective-permute-done.5 = bf16[256,2048]{1,0:T(8,128)(2,1)S(1)} collective-permute-done((bf16[256,2048]{1,0:T(8,128)(2,1)}, bf16[256,2048]{1,0:T(8,128)(2,1)S(1)}, u32[]{:S(2)}, u32[]{:S(2)}) %collective-permute-start.5) | collective-permute-done | bytes 1048608 | tf_op jit(solution)/shard_map/ppermute | solution.py:1015
  794.6 37.6 %ffn_bwd.4 = (bf16[256,5632]{1,0:T(8,128)(2,1)}, bf16[256,5632]{1,0:T(8,128)(2,1)}, f32[256,2048]{1,0:T(8,128)}, bf16[256,2048]{1,0:T(8,128)(2,1)}, f32[1,2048]{1,0:T(1,128)}) custom-call(bf16[256,2048]{1,0:T(8,128)(2,1)} %bitcast_select_fusion.grad_ref.refs_38_, f32[256,2048]{1,0:T(8,128)} %get-tuple-element.106.mid_ref, f32[1,2048]{1,0:T(1,128)} %bitcast.83, ...), custom_call_target="tpu_custom_call" | custom-call | flops 17716740096 | bytes 69206016 | tf_op jit(solution)/shard_map/ffn_bwd/pallas_call | solution.py:673
  833.7 54.7 %attend_back.4 = (bf16[256,2048]{1,0:T(8,128)(2,1)}, bf16[256,512]{1,0:T(8,128)(2,1)}, f32[256,2048]{1,0:T(8,128)}, bf16[256,2048]{1,0:T(8,128)(2,1)}, f32[1,2048]{1,0:T(1,128)}) custom-call(bf16[256,2048]{1,0:T(8,128)(2,1)} %get-tuple-element.128.da_ref.refs_35_, f32[256,2048]{1,0:T(8,128)} %get-tuple-element.129.dmid_ref, ...), custom_call_target="tpu_custom_call" | custom-call | flops 10200547328 | bytes 18874368 | tf_op jit(solution)/shard_map/attend_back/pallas_call | solution.py:976
  890.4 20.5 %collective-permute-done.7 = bf16[256,2048]{1,0:T(8,128)(2,1)S(1)} collective-permute-done((bf16[256,2048]{1,0:T(8,128)(2,1)}, bf16[256,2048]{1,0:T(8,128)(2,1)S(1)}, u32[]{:S(2)}, u32[]{:S(2)}) %collective-permute-start.7) | collective-permute-done | bytes 1048608 | tf_op jit(solution)/shard_map/ppermute | solution.py:1015
  912.0 37.4 %ffn_bwd.5 = (bf16[256,5632]{1,0:T(8,128)(2,1)}, bf16[256,5632]{1,0:T(8,128)(2,1)}, f32[256,2048]{1,0:T(8,128)}, bf16[256,2048]{1,0:T(8,128)(2,1)}, f32[1,2048]{1,0:T(1,128)}) custom-call(bf16[256,2048]{1,0:T(8,128)(2,1)} %broadcast_select_fusion.grad_ref.refs_39_, f32[256,2048]{1,0:T(8,128)} %get-tuple-element.95.mid_ref, f32[1,2048]{1,0:T(1,128)} %bitcast.84, ...), custom_call_target="tpu_custom_call" | custom-call | flops 17716740096 | bytes 69206016 | tf_op jit(solution)/shard_map/ffn_bwd/pallas_call | solution.py:673
  955.4 54.7 %attend_back.5 = (bf16[256,2048]{1,0:T(8,128)(2,1)}, bf16[256,512]{1,0:T(8,128)(2,1)}, f32[256,2048]{1,0:T(8,128)}, bf16[256,2048]{1,0:T(8,128)(2,1)}, f32[1,2048]{1,0:T(1,128)}) custom-call(bf16[256,2048]{1,0:T(8,128)(2,1)} %get-tuple-element.140.da_ref.refs_36_, f32[256,2048]{1,0:T(8,128)} %get-tuple-element.141.dmid_ref, ...), custom_call_target="tpu_custom_call" | custom-call | flops 10200547328 | bytes 18874368 | tf_op jit(solution)/shard_map/attend_back/pallas_call | solution.py:976
  1011.6 2.8 select_bitcast_fusion.1
  1014.4 2.5 maximum_bitcast_fusion
  1017.0 424.9 %reduce_weights.1 = (bf16[512,5632]{1,0:T(8,128)(2,1)}, bf16[512,5632]{1,0:T(8,128)(2,1)}, bf16[512,2560]{1,0:T(8,128)(2,1)}, bf16[512,2048]{1,0:T(8,128)(2,1)},...) custom-call(f32[8,2048]{1,0:T(8,128)} %pad.9.refs_0_, bf16[2048,256]{1,0:T(8,128)(2,1)} %get-tuple-element.115.refs_1_, ...), custom_call_target="tpu_custom_call" | custom-call | flops 45097156608 | bytes 44040192 | tf_op jit(solution)/shard_map/reduce_weights/pallas_call | solution.py:400
  1441.9 4.3 bitcast_convert_fusion.4
  1446.2 2.2 bitcast_convert_fusion.5
  1448.4 2.7 bitcast_convert_fusion.3
  1451.0 5.9 bitcast_convert_fusion.2
  1457.0 5.9 bitcast_convert_fusion.1
  1462.9 6.0 bitcast_convert_fusion
  (97 shorter events, 29.2 us)
Async XLA Ops:
  0.6 6.3 copy-start.1
  450.1 26.2 %collective-permute-start = (bf16[256,2048]{1,0:T(8,128)(2,1)}, bf16[256,2048]{1,0:T(8,128)(2,1)S(1)}, u32[]{:S(2)}, u32[]{:S(2)}) collective-permute-start(bf16[256,2048]{1,0:T(8,128)(2,1)} %get-tuple-element.100), channel_id=1, source_target_pairs={{0,16},{1,17},{2,18},{3,19},{4,20},{5,21},{6,22},{7,23},{8,24},{9,... | collective-permute-start | bytes 3145736 | tf_op jit(solution)/shard_map/ppermute | solution.py:1015
  453.6 72.2 %collective-permute-start.1 = (bf16[2048,256]{1,0:T(8,128)(2,1)}, bf16[2048,256]{1,0:T(8,128)(2,1)S(1)}, u32[]{:S(2)}, u32[]{:S(2)}) collective-permute-start(bf16[2048,256]{1,0:T(8,128)(2,1)} %get-tuple-element.105.refs_3_), channel_id=1, source_target_pairs={{0,8},{8,0},{4,12},{12,4},{1,9},{9,1},{5,13},{13,5},{2,10},{10,2},... | collective-permute-start | bytes 3145736 | tf_op jit(solution)/shard_map/ppermute | solution.py:1080
  526.8 39.8 %copy-start.4 = (f32[256,128]{1,0:T(8,128)S(1)}, f32[256,128]{1,0:T(8,128)}, u32[]{:S(2)}) copy-start(f32[256,128]{1,0:T(8,128)} %copy.23.sin_ref.refs_3_) | copy-start | bytes 393220
  562.2 25.3 %collective-permute-start.2 = (bf16[256,2048]{1,0:T(8,128)(2,1)}, bf16[256,2048]{1,0:T(8,128)(2,1)S(1)}, u32[]{:S(2)}, u32[]{:S(2)}) collective-permute-start(bf16[256,2048]{1,0:T(8,128)(2,1)} %get-tuple-element.107), channel_id=1, source_target_pairs={{0,16},{1,17},{2,18},{3,19},{4,20},{5,21},{6,22},{7,23},{8,24},{9,... | collective-permute-start | bytes 3145736 | tf_op jit(solution)/shard_map/ppermute | solution.py:1015
  567.2 68.7 %collective-permute-start.3 = (bf16[2048,256]{1,0:T(8,128)(2,1)}, bf16[2048,256]{1,0:T(8,128)(2,1)}, u32[]{:S(2)}, u32[]{:S(2)}) collective-permute-start(bf16[2048,256]{1,0:T(8,128)(2,1)} %get-tuple-element.109.refs_2_), channel_id=1, source_target_pairs={{0,8},{8,0},{4,12},{12,4},{1,9},{9,1},{5,13},{13,5},{2,10},{10,2},... | collective-permute-start | bytes 3145736 | tf_op jit(solution)/shard_map/ppermute | solution.py:1080
  671.4 41.6 %collective-permute-start.4 = (bf16[2048,256]{1,0:T(8,128)(2,1)}, bf16[2048,256]{1,0:T(8,128)(2,1)S(1)}, u32[]{:S(2)}, u32[]{:S(2)}) collective-permute-start(bf16[2048,256]{1,0:T(8,128)(2,1)} %get-tuple-element.115.refs_1_), channel_id=1, source_target_pairs={{0,8},{8,0},{4,12},{12,4},{1,9},{9,1},{5,13},{13,5},{2,10},{10,2},... | collective-permute-start | bytes 3145736 | tf_op jit(solution)/shard_map/ppermute | solution.py:1080
  710.6 2.2 copy-start.8
  713.0 58.3 %copy-start.17 = (bf16[2048,256]{1,0:T(8,128)(2,1)}, bf16[2048,256]{1,0:T(8,128)(2,1)S(1)}, u32[]{:S(2)}) copy-start(bf16[2048,256]{1,0:T(8,128)(2,1)S(1)} %collective-permute-done.4.refs_4_) | copy-start | bytes 3145732
  771.2 21.7 %copy-start.2 = (bf16[2,256,2048]{2,1,0:T(8,128)(2,1)S(1)}, bf16[2,256,2048]{2,1,0:T(8,128)(2,1)}, u32[]{:S(2)}) copy-start(bf16[2,256,2048]{2,1,0:T(8,128)(2,1)} %param.12) | copy-start | bytes 6291460
  771.3 21.7 %collective-permute-start.5 = (bf16[256,2048]{1,0:T(8,128)(2,1)}, bf16[256,2048]{1,0:T(8,128)(2,1)S(1)}, u32[]{:S(2)}, u32[]{:S(2)}) collective-permute-start(bf16[256,2048]{1,0:T(8,128)(2,1)} %get-tuple-element.122), channel_id=1, source_target_pairs={{16,0},{17,1},{18,2},{19,3},{20,4},{21,5},{22,6},{23,7},{24,8},{25... | collective-permute-start | bytes 3145736 | tf_op jit(solution)/shard_map/ppermute | solution.py:1015
  772.9 60.8 %collective-permute-start.6 = (bf16[256,5632]{1,0:T(8,128)(2,1)S(1)}, bf16[256,5632]{1,0:T(8,128)(2,1)}, u32[]{:S(2)}, u32[]{:S(2)}) collective-permute-start(bf16[256,5632]{1,0:T(8,128)(2,1)S(1)} %pad_maximum_fusion), channel_id=1, source_target_pairs={{0,8},{8,0},{4,12},{12,4},{1,9},{9,1},{5,13},{13,5},{2,10},{10,2},... | collective-permute-start | bytes 8650760 | tf_op jit(solution)/shard_map/ppermute | solution.py:1025
  833.7 56.0 %copy-start.9 = (bf16[256,5632]{1,0:T(8,128)(2,1)S(1)}, bf16[256,5632]{1,0:T(8,128)(2,1)}, u32[]{:S(2)}) copy-start(bf16[256,5632]{1,0:T(8,128)(2,1)} %get-tuple-element.138.refs_17_) | copy-start | bytes 8650756
  888.4 22.5 %collective-permute-start.7 = (bf16[256,2048]{1,0:T(8,128)(2,1)}, bf16[256,2048]{1,0:T(8,128)(2,1)S(1)}, u32[]{:S(2)}, u32[]{:S(2)}) collective-permute-start(bf16[256,2048]{1,0:T(8,128)(2,1)} %get-tuple-element.134), channel_id=1, source_target_pairs={{16,0},{17,1},{18,2},{19,3},{20,4},{21,5},{22,6},{23,7},{24,8},{25... | collective-permute-start | bytes 3145736 | tf_op jit(solution)/shard_map/ppermute | solution.py:1015
  890.0 65.3 %collective-permute-start.8 = (bf16[256,5632]{1,0:T(8,128)(2,1)S(1)}, bf16[256,5632]{1,0:T(8,128)(2,1)}, u32[]{:S(2)}, u32[]{:S(2)}) collective-permute-start(bf16[256,5632]{1,0:T(8,128)(2,1)S(1)} %pad_maximum_fusion.1), channel_id=1, source_target_pairs={{0,8},{8,0},{4,12},{12,4},{1,9},{9,1},{5,13},{13,5},{2,10},{10,2},... | collective-permute-start | bytes 8650760 | tf_op jit(solution)/shard_map/ppermute | solution.py:1025
  949.5 2.3 copy-start.10
  951.8 1.5 copy-start.6
  951.9 1.8 copy-start.7
  952.1 64.9 %collective-permute-start.9 = (bf16[256,5632]{1,0:T(8,128)(2,1)S(1)}, bf16[256,5632]{1,0:T(8,128)(2,1)}, u32[]{:S(2)}, u32[]{:S(2)}) collective-permute-start(bf16[256,5632]{1,0:T(8,128)(2,1)S(1)} %pad_maximum_fusion.2), channel_id=1, source_target_pairs={{0,8},{8,0},{4,12},{12,4},{1,9},{9,1},{5,13},{13,5},{2,10},{10,2},... | collective-permute-start | bytes 8650760 | tf_op jit(solution)/shard_map/ppermute | solution.py:1025
  955.4 54.8 %copy-start.11 = (f32[1,2048]{1,0:T(1,128)S(1)}, f32[1,2048]{1,0:T(1,128)}, u32[]{:S(2)}) copy-start(f32[1,2048]{1,0:T(1,128)} %get-tuple-element.150) | copy-start | bytes 24580
  955.4 54.8 %copy-start.12 = (f32[1,2048]{1,0:T(1,128)S(1)}, f32[1,2048]{1,0:T(1,128)}, u32[]{:S(2)}) copy-start(f32[1,2048]{1,0:T(1,128)} %get-tuple-element.149) | copy-start | bytes 24580
  955.4 54.8 %copy-start.13 = (f32[1,2048]{1,0:T(1,128)S(1)}, f32[1,2048]{1,0:T(1,128)}, u32[]{:S(2)}) copy-start(f32[1,2048]{1,0:T(1,128)} %get-tuple-element.152) | copy-start | bytes 24580
  955.4 54.8 %copy-start.14 = (f32[1,2048]{1,0:T(1,128)S(1)}, f32[1,2048]{1,0:T(1,128)}, u32[]{:S(2)}) copy-start(f32[1,2048]{1,0:T(1,128)} %get-tuple-element.151) | copy-start | bytes 24580
  955.4 54.8 %copy-start.15 = (f32[1,2048]{1,0:T(1,128)S(1)}, f32[1,2048]{1,0:T(1,128)}, u32[]{:S(2)}) copy-start(f32[1,2048]{1,0:T(1,128)} %get-tuple-element.154) | copy-start | bytes 24580
  955.4 56.2 %copy-start.3 = (f32[256,2048]{1,0:T(8,128)S(1)}, f32[256,2048]{1,0:T(8,128)}, u32[]{:S(2)}) copy-start(f32[256,2048]{1,0:T(8,128)} %get-tuple-element.148) | copy-start | bytes 6291460
  1441.8 6.5 copy-start
  1441.9 9.2 slice-start.4
  1446.2 4.9 slice-start.5
  1448.4 8.6 slice-start.2
  1451.0 6.0 slice-start.3
  1451.0 11.9 slice-start
  1457.0 6.0 slice-start.1
  (2 other events, 2.2 us)

commit v7 on v6

--- a/solution.py
+++ b/solution.py
@@ -487,22 +487,24 @@
         y_copy(piece, s).wait_recv()
         t_copy(piece, s).start()
 
-    def pass_on(group, before_last):
-        before = []
-        for s in range(1, n):
-            if s == n - 1:
-                before_last()
-            for piece in group:
-                z_copy(piece, s - 1).wait_recv()
-                if s < n - 1:
-                    z_copy(piece, s).start()
-                y_copy(piece, s).start()
-                c_copy(piece, s).start()
-                before.append((piece, s))
-                if len(before) > 1:
-                    turn(*before[-2])
-        turn(*before[-1])
-        return before
+    def hop(piece, s):
+        z_copy(piece, s - 1).wait_recv()
+        if s < n - 1:
+            z_copy(piece, s).start()
+        y_copy(piece, s).start()
+        c_copy(piece, s).start()
+
+    def pass_on(group, served):
+        order = [(piece, s) for s in range(1, n) for piece in group]
+        turned = 0
+        for at in range(served, len(order)):
+            hop(*order[at])
+            while turned < at:
+                turn(*order[turned])
+                turned += 1
+        for at in range(turned, len(order)):
+            turn(*order[at])
+        return order
 
     def arrived(which, before):
         for k in which:
@@ -519,7 +521,13 @@
         begin(second)
         for k in range(early, count):
             own_load(k).start()
-    before = pass_on(first, lambda: None)
+    served = []
+
+    def serve(pieces):
+        for _ in range(pieces):
+            hop(second[len(served)], 1)
+            served.append(1)
+    before = pass_on(first, 0)
     arrived(range(early), before)
     load = pltpu.make_async_copy(outs[3], gain_blocks, gain_sem.at[0])
     load.start()
@@ -528,11 +536,11 @@
     part = x_ref.shape[1] // n
     for k in range(n):
         gain_row[:, k * part:(k + 1) * part] = gain_blocks[k * rows:k * rows + 1, :part].astype(F32)
-    attend_steps(lambda: None, start_second, x_ref, gain_row, cos_ref, sin_ref, outs[0], outs[1], outs[2], *attend_outs, *attend_refs)
+    attend_steps(lambda: None, start_second, serve, x_ref, gain_row, cos_ref, sin_ref, outs[0], outs[1], outs[2], *attend_outs, *attend_refs)
     for k in range(early, count):
         own_load(k).wait()
         own_store(k).start()
-    after = pass_on(second, lambda: None)
+    after = pass_on(second, len(served))
     arrived(range(early, count), after)
     for piece, s in before + after:
         z_copy(piece, s - 1).wait_send()
@@ -692,7 +700,7 @@
     return rows * jnp.tile(cos_ref[...], (1, reps)) + swapped * jnp.tile(sin_ref[...], (1, reps))
 
 
-def attend_steps(greeted, sent, x_ref, gain_ref, cos_ref, sin_ref, w_q, w_kv, w_o,
+def attend_steps(greeted, sent, serve, x_ref, gain_ref, cos_ref, sin_ref, w_q, w_kv, w_o,
                  normed_turn, q_ref, kv_ref, attended_turn, lse_ref, mid_ref,
                  normed_ref, attended_ref, wq_ref, wkv_ref, wo_ref, q_turn, acc, top_ref, total_ref, land,
                  load_sem, send_sem, recv_sem):
@@ -766,7 +774,9 @@
             acc[span, :] = acc[span, :] * fade + mm(value_t, prob.astype(BF16))
         return carry
 
+    serve(1)
     lax.fori_loop(1, me + 1, earlier, 0)
+    serve(2)
     total = total_ref[...]
     lse_ref[...] = top_ref[...] + jnp.log2(total)
     total_ref[...] = 1.0 / total
@@ -803,7 +813,7 @@
         @pl.when(me < n - 1)
         def _():
             pl.semaphore_wait(barrier, n - 1 - me)
-    attend_steps(greeted, lambda: None, *refs)
+    attend_steps(greeted, lambda: None, lambda pieces: None, *refs)
 
 
 def attend_scratch(rows, width, n, kv_both):

time: 1480 us -> 1480 us (level)
  no operation moved by 1% of the time
where the time goes in v7:
time: 1480 us; the launch traced here: 1470 us
  Pallas kernels  1310 us (89%)
  waiting for transfers between devices  79.1 us (5%)
  other arithmetic  47.6 us (3%)
  starting transfers between devices  16.9 us (1%)
  local copies, waits for them, and re-layouts  15.8 us (1%)
    pallas_call x1, Pallas kernels, reduce_weights(): pl.pallas_call(functools.partial(reduce_kernel, plans, slots), in_specs=[...  425 us
    pallas_call x1, Pallas kernels, gather_weights(): pl.pallas_call(functools.partial(gather_kernel, splits), in_specs=[vmem]...  402 us
    pallas_call x3, Pallas kernels, attend_back(): pl.pallas_call(attend_back_kernel, in_specs=[vmem] * 10 + [anywhere] * 3,...  168 us
    pallas_call x3, Pallas kernels, ffn_bwd(): pl.pallas_call(ffn_bwd_kernel, grid=(ff // FF_TILE,), in_specs=[whole, wh...  112 us
    pallas_call x3, Pallas kernels, ffn_fwd(): pl.pallas_call(ffn_fwd_kernel, grid=(ff // FF_TILE,), in_specs=[whole, pl...  106 us
    pallas_call x2, Pallas kernels, attend_block(): pl.pallas_call(attend_block_kernel, in_specs=[vmem] * 4 + [anywhere] * 3,...  94 us
    ppermute x4, waiting for transfers between devices, passed_along(): return lax.ppermute(block, axis, pairs)  79.1 us
  transfers between devices with their start and end apart: 10, of which 4 were waited for; matrix products, arithmetic and copies ran while one was open for 1% of the time, Pallas kernels for 18%

profile of v7, /device:TPU:0, one launch (start us, length us, event | category | flops | bytes accessed | tf_op | source)
XLA Modules:
  0.0 1469.4 jit_solution(1820108740149238823)
XLA Ops:
  3.8 1.9 pad_maximum_fusion.3.refs_1_
  7.0 4.0 select_bitcast_fusion.2
  10.9 402.4 %gather_weights.1 = (bf16[2048,2048]{1,0:T(8,128)(2,1)}, bf16[2048,512]{1,0:T(8,128)(2,1)}, bf16[2048,2048]{1,0:T(8,128)(2,1)}, bf16[64,512]{1,0:T(8,128)(2,1)},...) custom-call(bf16[256,2048]{1,0:T(8,128)(2,1)} %get-tuple-element.194, ...), custom_call_target="tpu_custom_call" | custom-call | flops 4294967296 | bytes 352583680 | tf_op jit(solution)/shard_map/gather_weights/pallas_call | solution.py:562
  414.7 35.4 %ffn_fwd.3 = (bf16[256,2048]{1,0:T(8,128)(2,1)}, bf16[2048,256]{1,0:T(8,128)(2,1)}, bf16[5632,256]{1,0:T(8,128)(2,1)}, bf16[256,5632]{1,0:T(8,128)(2,1)}, bf16[256,5632]{1,0:T(8,128)(2,1)}) custom-call(f32[256,2048]{1,0:T(8,128)} %get-tuple-element.95.mid_ref, f32[1,2048]{1,0:T(1,128)} %bitcast.79, bf16[2048,5632]{1,0:T(8,128)(2,1)} %get-tuple-element.97.w_g, ...), custom_call_target="tpu_custom_call" | custom-call | flops 17716740096 | bytes 69206016 | tf_op jit(solution)/shard_map/ffn_fwd/pallas_call | solution.py:629
  450.1 3.5 collective-permute-start
  453.6 1.7 collective-permute-start.1
  456.0 20.4 %collective-permute-done = bf16[256,2048]{1,0:T(8,128)(2,1)S(1)} collective-permute-done((bf16[256,2048]{1,0:T(8,128)(2,1)}, bf16[256,2048]{1,0:T(8,128)(2,1)S(1)}, u32[]{:S(2)}, u32[]{:S(2)}) %collective-permute-start) | collective-permute-done | bytes 1048608 | tf_op jit(solution)/shard_map/ppermute | solution.py:1025
  476.3 1.7 bitcast_select_fusion.1.refs_0_.x_ref
  478.1 46.7 %attend_block.2 = (bf16[2048,256]{1,0:T(8,128)(2,1)}, bf16[256,2048]{1,0:T(8,128)(2,1)}, bf16[4,256,512]{2,1,0:T(8,128)(2,1)}, bf16[2048,256]{1,0:T(8,128)(2,1)}...) custom-call(bf16[256,2048]{1,0:T(8,128)(2,1)} %bitcast_select_fusion.1.refs_0_.x_ref, f32[1,2048]{1,0:T(1,128)} %bitcast.87, ...), custom_call_target="tpu_custom_call" | custom-call | flops 6979321856 | bytes 18874368 | tf_op jit(solution)/shard_map/attend_block/pallas_call | solution.py:849
  525.7 35.4 %ffn_fwd.4 = (bf16[256,2048]{1,0:T(8,128)(2,1)}, bf16[2048,256]{1,0:T(8,128)(2,1)}, bf16[5632,256]{1,0:T(8,128)(2,1)}, bf16[256,5632]{1,0:T(8,128)(2,1)}, bf16[256,5632]{1,0:T(8,128)(2,1)}) custom-call(f32[256,2048]{1,0:T(8,128)} %get-tuple-element.106.mid_ref, f32[1,2048]{1,0:T(1,128)} %bitcast.80, bf16[2048,5632]{1,0:T(8,128)(2,1)} %get-tuple-element.97.w_g, ...), custom_call_target="tpu_custom_call" | custom-call | flops 17716740096 | bytes 69206016 | tf_op jit(solution)/shard_map/ffn_fwd/pallas_call | solution.py:629
  561.2 4.3 collective-permute-start.2
  567.9 18.6 %collective-permute-done.2 = bf16[256,2048]{1,0:T(8,128)(2,1)S(1)} collective-permute-done((bf16[256,2048]{1,0:T(8,128)(2,1)}, bf16[256,2048]{1,0:T(8,128)(2,1)S(1)}, u32[]{:S(2)}, u32[]{:S(2)}) %collective-permute-start.2) | collective-permute-done | bytes 1048608 | tf_op jit(solution)/shard_map/ppermute | solution.py:1025
  587.5 47.3 %attend_block.3 = (bf16[2048,256]{1,0:T(8,128)(2,1)}, bf16[256,2048]{1,0:T(8,128)(2,1)}, bf16[4,256,512]{2,1,0:T(8,128)(2,1)}, bf16[2048,256]{1,0:T(8,128)(2,1)}...) custom-call(bf16[256,2048]{1,0:T(8,128)(2,1)} %broadcast_select_fusion.1.refs_0_.x_ref, f32[1,2048]{1,0:T(1,128)} %bitcast.88, ...), custom_call_target="tpu_custom_call" | custom-call | flops 6979321856 | bytes 18874368 | tf_op jit(solution)/shard_map/attend_block/pallas_call | solution.py:849
  634.9 35.4 %ffn_fwd.5 = (bf16[256,2048]{1,0:T(8,128)(2,1)}, bf16[2048,256]{1,0:T(8,128)(2,1)}, bf16[5632,256]{1,0:T(8,128)(2,1)}, bf16[256,5632]{1,0:T(8,128)(2,1)}, bf16[256,5632]{1,0:T(8,128)(2,1)}) custom-call(f32[256,2048]{1,0:T(8,128)} %get-tuple-element.110.mid_ref, f32[1,2048]{1,0:T(1,128)} %bitcast.81, bf16[2048,5632]{1,0:T(8,128)(2,1)} %get-tuple-element.97.w_g, ...), custom_call_target="tpu_custom_call" | custom-call | flops 17716740096 | bytes 69206016 | tf_op jit(solution)/shard_map/ffn_fwd/pallas_call | solution.py:629
  670.3 1.8 collective-permute-start.4
  672.1 37.4 %ffn_bwd.3 = (bf16[256,5632]{1,0:T(8,128)(2,1)}, bf16[256,5632]{1,0:T(8,128)(2,1)}, f32[256,2048]{1,0:T(8,128)}, bf16[256,2048]{1,0:T(8,128)(2,1)}, f32[1,2048]{1,0:T(1,128)}) custom-call(bf16[256,2048]{1,0:T(8,128)(2,1)} %get-tuple-element.193.grad_ref.refs_37_, f32[256,2048]{1,0:T(8,128)} %get-tuple-element.110.mid_ref, f32[1,2048]{1,0:T(1,128)} %bitcast.82, ...), custom_call_target="tpu_custom_call" | custom-call | flops 17716740096 | bytes 69206016 | tf_op jit(solution)/shard_map/ffn_bwd/pallas_call | solution.py:681
  711.9 58.2 %attend_back.3 = (bf16[256,2048]{1,0:T(8,128)(2,1)}, bf16[256,512]{1,0:T(8,128)(2,1)}, f32[256,2048]{1,0:T(8,128)}, bf16[256,2048]{1,0:T(8,128)(2,1)}, f32[1,2048]{1,0:T(1,128)}) custom-call(bf16[256,2048]{1,0:T(8,128)(2,1)} %get-tuple-element.116.da_ref.refs_34_, f32[256,2048]{1,0:T(8,128)} %get-tuple-element.117.dmid_ref, ...), custom_call_target="tpu_custom_call" | custom-call | flops 10200547328 | bytes 18874368 | tf_op jit(solution)/shard_map/attend_back/pallas_call | solution.py:986
  772.2 19.7 %collective-permute-done.5 = bf16[256,2048]{1,0:T(8,128)(2,1)S(1)} collective-permute-done((bf16[256,2048]{1,0:T(8,128)(2,1)}, bf16[256,2048]{1,0:T(8,128)(2,1)S(1)}, u32[]{:S(2)}, u32[]{:S(2)}) %collective-permute-start.5) | collective-permute-done | bytes 1048608 | tf_op jit(solution)/shard_map/ppermute | solution.py:1025
  793.5 37.6 %ffn_bwd.4 = (bf16[256,5632]{1,0:T(8,128)(2,1)}, bf16[256,5632]{1,0:T(8,128)(2,1)}, f32[256,2048]{1,0:T(8,128)}, bf16[256,2048]{1,0:T(8,128)(2,1)}, f32[1,2048]{1,0:T(1,128)}) custom-call(bf16[256,2048]{1,0:T(8,128)(2,1)} %bitcast_select_fusion.grad_ref.refs_38_, f32[256,2048]{1,0:T(8,128)} %get-tuple-element.106.mid_ref, f32[1,2048]{1,0:T(1,128)} %bitcast.83, ...), custom_call_target="tpu_custom_call" | custom-call | flops 17716740096 | bytes 69206016 | tf_op jit(solution)/shard_map/ffn_bwd/pallas_call | solution.py:681
  832.6 54.7 %attend_back.4 = (bf16[256,2048]{1,0:T(8,128)(2,1)}, bf16[256,512]{1,0:T(8,128)(2,1)}, f32[256,2048]{1,0:T(8,128)}, bf16[256,2048]{1,0:T(8,128)(2,1)}, f32[1,2048]{1,0:T(1,128)}) custom-call(bf16[256,2048]{1,0:T(8,128)(2,1)} %get-tuple-element.128.da_ref.refs_35_, f32[256,2048]{1,0:T(8,128)} %get-tuple-element.129.dmid_ref, ...), custom_call_target="tpu_custom_call" | custom-call | flops 10200547328 | bytes 18874368 | tf_op jit(solution)/shard_map/attend_back/pallas_call | solution.py:986
  889.3 20.5 %collective-permute-done.7 = bf16[256,2048]{1,0:T(8,128)(2,1)S(1)} collective-permute-done((bf16[256,2048]{1,0:T(8,128)(2,1)}, bf16[256,2048]{1,0:T(8,128)(2,1)S(1)}, u32[]{:S(2)}, u32[]{:S(2)}) %collective-permute-start.7) | collective-permute-done | bytes 1048608 | tf_op jit(solution)/shard_map/ppermute | solution.py:1025
  910.9 37.4 %ffn_bwd.5 = (bf16[256,5632]{1,0:T(8,128)(2,1)}, bf16[256,5632]{1,0:T(8,128)(2,1)}, f32[256,2048]{1,0:T(8,128)}, bf16[256,2048]{1,0:T(8,128)(2,1)}, f32[1,2048]{1,0:T(1,128)}) custom-call(bf16[256,2048]{1,0:T(8,128)(2,1)} %broadcast_select_fusion.grad_ref.refs_39_, f32[256,2048]{1,0:T(8,128)} %get-tuple-element.95.mid_ref, f32[1,2048]{1,0:T(1,128)} %bitcast.84, ...), custom_call_target="tpu_custom_call" | custom-call | flops 17716740096 | bytes 69206016 | tf_op jit(solution)/shard_map/ffn_bwd/pallas_call | solution.py:681
  954.3 54.7 %attend_back.5 = (bf16[256,2048]{1,0:T(8,128)(2,1)}, bf16[256,512]{1,0:T(8,128)(2,1)}, f32[256,2048]{1,0:T(8,128)}, bf16[256,2048]{1,0:T(8,128)(2,1)}, f32[1,2048]{1,0:T(1,128)}) custom-call(bf16[256,2048]{1,0:T(8,128)(2,1)} %get-tuple-element.140.da_ref.refs_36_, f32[256,2048]{1,0:T(8,128)} %get-tuple-element.141.dmid_ref, ...), custom_call_target="tpu_custom_call" | custom-call | flops 10200547328 | bytes 18874368 | tf_op jit(solution)/shard_map/attend_back/pallas_call | solution.py:986
  1010.5 2.8 select_bitcast_fusion.1
  1013.3 2.5 maximum_bitcast_fusion
  1015.9 424.9 %reduce_weights.1 = (bf16[512,5632]{1,0:T(8,128)(2,1)}, bf16[512,5632]{1,0:T(8,128)(2,1)}, bf16[512,2560]{1,0:T(8,128)(2,1)}, bf16[512,2048]{1,0:T(8,128)(2,1)},...) custom-call(f32[8,2048]{1,0:T(8,128)} %pad.9.refs_0_, bf16[2048,256]{1,0:T(8,128)(2,1)} %get-tuple-element.115.refs_1_, ...), custom_call_target="tpu_custom_call" | custom-call | flops 45097156608 | bytes 44040192 | tf_op jit(solution)/shard_map/reduce_weights/pallas_call | solution.py:400
  1440.8 4.3 bitcast_convert_fusion.4
  1445.0 2.2 bitcast_convert_fusion.5
  1447.2 2.7 bitcast_convert_fusion.3
  1449.9 5.9 bitcast_convert_fusion.2
  1455.9 5.9 bitcast_convert_fusion.1
  1461.8 6.0 bitcast_convert_fusion
  (97 shorter events, 29.2 us)
Async XLA Ops:
  0.6 6.3 copy-start.1
  450.1 26.2 %collective-permute-start = (bf16[256,2048]{1,0:T(8,128)(2,1)}, bf16[256,2048]{1,0:T(8,128)(2,1)S(1)}, u32[]{:S(2)}, u32[]{:S(2)}) collective-permute-start(bf16[256,2048]{1,0:T(8,128)(2,1)} %get-tuple-element.100), channel_id=1, source_target_pairs={{0,16},{1,17},{2,18},{3,19},{4,20},{5,21},{6,22},{7,23},{8,24},{9,... | collective-permute-start | bytes 3145736 | tf_op jit(solution)/shard_map/ppermute | solution.py:1025
  453.6 71.1 %collective-permute-start.1 = (bf16[2048,256]{1,0:T(8,128)(2,1)}, bf16[2048,256]{1,0:T(8,128)(2,1)S(1)}, u32[]{:S(2)}, u32[]{:S(2)}) collective-permute-start(bf16[2048,256]{1,0:T(8,128)(2,1)} %get-tuple-element.105.refs_3_), channel_id=1, source_target_pairs={{0,8},{8,0},{4,12},{12,4},{1,9},{9,1},{5,13},{13,5},{2,10},{10,2},... | collective-permute-start | bytes 3145736 | tf_op jit(solution)/shard_map/ppermute | solution.py:1090
  525.7 39.8 %copy-start.4 = (f32[256,128]{1,0:T(8,128)S(1)}, f32[256,128]{1,0:T(8,128)}, u32[]{:S(2)}) copy-start(f32[256,128]{1,0:T(8,128)} %copy.23.sin_ref.refs_3_) | copy-start | bytes 393220
  561.2 25.3 %collective-permute-start.2 = (bf16[256,2048]{1,0:T(8,128)(2,1)}, bf16[256,2048]{1,0:T(8,128)(2,1)S(1)}, u32[]{:S(2)}, u32[]{:S(2)}) collective-permute-start(bf16[256,2048]{1,0:T(8,128)(2,1)} %get-tuple-element.107), channel_id=1, source_target_pairs={{0,16},{1,17},{2,18},{3,19},{4,20},{5,21},{6,22},{7,23},{8,24},{9,... | collective-permute-start | bytes 3145736 | tf_op jit(solution)/shard_map/ppermute | solution.py:1025
  566.2 68.7 %collective-permute-start.3 = (bf16[2048,256]{1,0:T(8,128)(2,1)}, bf16[2048,256]{1,0:T(8,128)(2,1)}, u32[]{:S(2)}, u32[]{:S(2)}) collective-permute-start(bf16[2048,256]{1,0:T(8,128)(2,1)} %get-tuple-element.109.refs_2_), channel_id=1, source_target_pairs={{0,8},{8,0},{4,12},{12,4},{1,9},{9,1},{5,13},{13,5},{2,10},{10,2},... | collective-permute-start | bytes 3145736 | tf_op jit(solution)/shard_map/ppermute | solution.py:1090
  670.3 41.6 %collective-permute-start.4 = (bf16[2048,256]{1,0:T(8,128)(2,1)}, bf16[2048,256]{1,0:T(8,128)(2,1)S(1)}, u32[]{:S(2)}, u32[]{:S(2)}) collective-permute-start(bf16[2048,256]{1,0:T(8,128)(2,1)} %get-tuple-element.115.refs_1_), channel_id=1, source_target_pairs={{0,8},{8,0},{4,12},{12,4},{1,9},{9,1},{5,13},{13,5},{2,10},{10,2},... | collective-permute-start | bytes 3145736 | tf_op jit(solution)/shard_map/ppermute | solution.py:1090
  709.5 2.2 copy-start.8
  711.9 58.2 %copy-start.17 = (bf16[2048,256]{1,0:T(8,128)(2,1)}, bf16[2048,256]{1,0:T(8,128)(2,1)S(1)}, u32[]{:S(2)}) copy-start(bf16[2048,256]{1,0:T(8,128)(2,1)S(1)} %collective-permute-done.4.refs_4_) | copy-start | bytes 3145732
  770.1 21.7 %copy-start.2 = (bf16[2,256,2048]{2,1,0:T(8,128)(2,1)S(1)}, bf16[2,256,2048]{2,1,0:T(8,128)(2,1)}, u32[]{:S(2)}) copy-start(bf16[2,256,2048]{2,1,0:T(8,128)(2,1)} %param.12) | copy-start | bytes 6291460
  770.1 21.7 %collective-permute-start.5 = (bf16[256,2048]{1,0:T(8,128)(2,1)}, bf16[256,2048]{1,0:T(8,128)(2,1)S(1)}, u32[]{:S(2)}, u32[]{:S(2)}) collective-permute-start(bf16[256,2048]{1,0:T(8,128)(2,1)} %get-tuple-element.122), channel_id=1, source_target_pairs={{16,0},{17,1},{18,2},{19,3},{20,4},{21,5},{22,6},{23,7},{24,8},{25... | collective-permute-start | bytes 3145736 | tf_op jit(solution)/shard_map/ppermute | solution.py:1025
  771.8 60.8 %collective-permute-start.6 = (bf16[256,5632]{1,0:T(8,128)(2,1)S(1)}, bf16[256,5632]{1,0:T(8,128)(2,1)}, u32[]{:S(2)}, u32[]{:S(2)}) collective-permute-start(bf16[256,5632]{1,0:T(8,128)(2,1)S(1)} %pad_maximum_fusion), channel_id=1, source_target_pairs={{0,8},{8,0},{4,12},{12,4},{1,9},{9,1},{5,13},{13,5},{2,10},{10,2},... | collective-permute-start | bytes 8650760 | tf_op jit(solution)/shard_map/ppermute | solution.py:1035
  832.6 56.0 %copy-start.9 = (bf16[256,5632]{1,0:T(8,128)(2,1)S(1)}, bf16[256,5632]{1,0:T(8,128)(2,1)}, u32[]{:S(2)}) copy-start(bf16[256,5632]{1,0:T(8,128)(2,1)} %get-tuple-element.138.refs_17_) | copy-start | bytes 8650756
  887.3 22.5 %collective-permute-start.7 = (bf16[256,2048]{1,0:T(8,128)(2,1)}, bf16[256,2048]{1,0:T(8,128)(2,1)S(1)}, u32[]{:S(2)}, u32[]{:S(2)}) collective-permute-start(bf16[256,2048]{1,0:T(8,128)(2,1)} %get-tuple-element.134), channel_id=1, source_target_pairs={{16,0},{17,1},{18,2},{19,3},{20,4},{21,5},{22,6},{23,7},{24,8},{25... | collective-permute-start | bytes 3145736 | tf_op jit(solution)/shard_map/ppermute | solution.py:1025
  888.9 65.3 %collective-permute-start.8 = (bf16[256,5632]{1,0:T(8,128)(2,1)S(1)}, bf16[256,5632]{1,0:T(8,128)(2,1)}, u32[]{:S(2)}, u32[]{:S(2)}) collective-permute-start(bf16[256,5632]{1,0:T(8,128)(2,1)S(1)} %pad_maximum_fusion.1), channel_id=1, source_target_pairs={{0,8},{8,0},{4,12},{12,4},{1,9},{9,1},{5,13},{13,5},{2,10},{10,2},... | collective-permute-start | bytes 8650760 | tf_op jit(solution)/shard_map/ppermute | solution.py:1035
  948.4 2.3 copy-start.10
  950.7 1.5 copy-start.6
  950.7 1.8 copy-start.7
  951.0 64.9 %collective-permute-start.9 = (bf16[256,5632]{1,0:T(8,128)(2,1)S(1)}, bf16[256,5632]{1,0:T(8,128)(2,1)}, u32[]{:S(2)}, u32[]{:S(2)}) collective-permute-start(bf16[256,5632]{1,0:T(8,128)(2,1)S(1)} %pad_maximum_fusion.2), channel_id=1, source_target_pairs={{0,8},{8,0},{4,12},{12,4},{1,9},{9,1},{5,13},{13,5},{2,10},{10,2},... | collective-permute-start | bytes 8650760 | tf_op jit(solution)/shard_map/ppermute | solution.py:1035
  954.3 54.8 %copy-start.11 = (f32[1,2048]{1,0:T(1,128)S(1)}, f32[1,2048]{1,0:T(1,128)}, u32[]{:S(2)}) copy-start(f32[1,2048]{1,0:T(1,128)} %get-tuple-element.150) | copy-start | bytes 24580
  954.3 54.8 %copy-start.12 = (f32[1,2048]{1,0:T(1,128)S(1)}, f32[1,2048]{1,0:T(1,128)}, u32[]{:S(2)}) copy-start(f32[1,2048]{1,0:T(1,128)} %get-tuple-element.149) | copy-start | bytes 24580
  954.3 54.8 %copy-start.13 = (f32[1,2048]{1,0:T(1,128)S(1)}, f32[1,2048]{1,0:T(1,128)}, u32[]{:S(2)}) copy-start(f32[1,2048]{1,0:T(1,128)} %get-tuple-element.152) | copy-start | bytes 24580
  954.3 54.8 %copy-start.14 = (f32[1,2048]{1,0:T(1,128)S(1)}, f32[1,2048]{1,0:T(1,128)}, u32[]{:S(2)}) copy-start(f32[1,2048]{1,0:T(1,128)} %get-tuple-element.151) | copy-start | bytes 24580
  954.3 54.8 %copy-start.15 = (f32[1,2048]{1,0:T(1,128)S(1)}, f32[1,2048]{1,0:T(1,128)}, u32[]{:S(2)}) copy-start(f32[1,2048]{1,0:T(1,128)} %get-tuple-element.154) | copy-start | bytes 24580
  954.3 56.2 %copy-start.3 = (f32[256,2048]{1,0:T(8,128)S(1)}, f32[256,2048]{1,0:T(8,128)}, u32[]{:S(2)}) copy-start(f32[256,2048]{1,0:T(8,128)} %get-tuple-element.148) | copy-start | bytes 6291460
  1440.7 6.5 copy-start
  1440.7 9.2 slice-start.4
  1445.0 4.9 slice-start.5
  1447.2 8.6 slice-start.2
  1449.9 6.0 slice-start.3
  1449.9 11.9 slice-start
  1455.9 6.0 slice-start.1
  (2 other events, 2.2 us)
